TPU v7x, 256 devices: a whole 4x4x8 slice. The times are simulated.
256 devices in a mesh: replica: 32 (over z, x), fsdp: 8 (over y, core).
Axes of the slice: x: 4, y: 4, z: 8, core: 2. Of those that a mesh axis runs over, the one named last changes fastest.
Arguments:
- features: bfloat16 [65536, 2560], P(('replica', 'fsdp')), may hold values from -0.125 to 0.125
- cotangent: bfloat16 [65536, 2560], P(('replica', 'fsdp')), may hold values from -6 to 6
- weight: bfloat16 [2560, 2560], P('fsdp'), may hold values from -0.125 to 0.125
- feedback: float32 [81920, 2560], P(('replica', 'fsdp')), may hold values from -6 to 6
- start_factors: float32 [2560, 32], replicated, may hold values from -6 to 6
Outputs:
- input_grad: bfloat16 [65536, 2560], P(('replica', 'fsdp'))
- new_feedback: float32 [81920, 2560], P(('replica', 'fsdp'))
- q_factor: float32 [2560, 32], replicated
All inputs are finite; a program needn't handle non-finite values.
Results may differ from a plain program's by a relative error of at most 0.0005.
Values may be sent and summed in bfloat16 or wider, within the bound.
No kernel may reach another device: no remote copies, remote signals or barrier semaphores. Data moves between devices by JAX's collectives and lax.ppermute only.
A program may use at most 128 MiB of HBM per device.

v0:
```python
import jax
import jax.numpy as jnp
from jax import lax
from jax.sharding import PartitionSpec as P


def shards(features, cotangent, weight, feedback, start_factors):
    highest = lax.Precision.HIGHEST
    input_grad = lax.dot_general(
        cotangent,
        lax.all_gather(weight, "fsdp", axis=0, tiled=True),
        (((1,), (1,)), ((), ())),
        preferred_element_type=jnp.float32,
    ).astype(jnp.bfloat16)
    grad_rows = lax.psum_scatter(
        lax.dot_general(
            features, cotangent, (((0,), (0,)), ((), ())), preferred_element_type=jnp.float32
        ),
        "fsdp",
        scatter_dimension=0,
        tiled=True,
    )
    grown = grad_rows + feedback
    local_p = jnp.dot(grown, start_factors, precision=highest)
    psum = lax.psum(local_p, "replica")
    gram = lax.psum(jnp.dot(psum.T, psum, precision=highest), "fsdp")
    lower = jnp.linalg.cholesky(gram)
    ortho = lax.linalg.triangular_solve(lower, psum, left_side=False, lower=True, transpose_a=True)
    q_local = lax.dot_general(grown, ortho, (((0,), (0,)), ((), ())), precision=highest)
    q_factor = lax.psum(q_local, ("replica", "fsdp")) / lax.axis_size("replica")
    new_feedback = grown - jnp.dot(ortho, q_factor.T, precision=highest)
    return (input_grad, new_feedback, q_factor)


def solution(mesh):
    placed = (
        P(("replica", "fsdp"), None),
        P(("replica", "fsdp"), None),
        P("fsdp", None),
        P(("replica", "fsdp"), None),
        P(),
    )
    return jax.shard_map(
        shards,
        mesh=mesh,
        in_specs=placed,
        out_specs=(P(("replica", "fsdp"), None), P(("replica", "fsdp"), None), P()),
        check_vma=False,
    )
```

profile of v0, /device:TPU:1, one launch (start us, length us, event | category | flops | bytes accessed | tf_op | source)
XLA Modules:
  0.0 603.2 jit_solution(5324997080134631771)
XLA Ops:
  7.2 0.0 copy-start
  7.2 0.0 reduce-scatter.2.cloned.1.call-start
  7.2 1.3 copy-done
  8.5 12.0 %fusion.4 = f32[2560,2560]{1,0:T(8,128)} fusion(bf16[256,2560]{1,0:T(8,128)(2,1)} %param.5, bf16[256,2560]{1,0:T(8,128)(2,1)S(1)} %copy-done), kind=kOutput, calls=%fused_computation.13 | convolution fusion | flops 3355443200 | bytes 28835840 | tf_op jit(solution)/shard_map/dot_general | solution.py:16
  20.5 0.0 reduce-scatter.2.cloned.1.call-update
  20.6 0.0 all-gather.2.cloned.1.call-start
  20.6 0.7 all-gather.2.cloned.1.call-update
  21.3 0.0 copy-start.3
  21.3 0.0 all-reduce.2.cloned.1.call-start
  21.4 141.4 %reduce-scatter.2.cloned.1.call-done = f32[320,2560]{1,0:T(8,128)} async-done(((f32[2560,2560]{1,0:T(8,128)}), f32[320,2560]{1,0:T(8,128)}) %reduce-scatter.2.cloned.1.call-update) | async-done | bytes 3276816 | tf_op jit(solution)/shard_map/reduce_scatter | solution.py:15
  162.8 3.4 add.22
  166.2 0.0 copy-start.1
  166.2 1.7 copy-done.1
  167.9 0.0 copy-done.3
  167.9 2.8 fusion.5
  170.7 115.8 %psum.21 = f32[320,32]{0,1:T(8,128)S(1)} all-reduce(f32[320,32]{0,1:T(8,128)S(1)} %fusion.5), channel_id=1, replica_groups=mesh['replica'=32,'fsdp'=8] {'replica'}, use_global_device_ids=true, to_apply=%region_1.0 | all-reduce | flops 10240 | bytes 81920 | tf_op jit(solution)/shard_map/psum | solution.py:25
  286.5 0.2 fusion.6
  286.7 48.7 %psum.22 = f32[32,32]{0,1:T(8,128)S(1)} all-reduce(f32[32,32]{0,1:T(8,128)S(1)} %fusion.6), channel_id=1, replica_groups=mesh['replica'=32,'fsdp'=8] {'fsdp'}, use_global_device_ids=true, to_apply=%region_2.0 | all-reduce | flops 1024 | bytes 8192 | tf_op jit(solution)/shard_map/psum | solution.py:26
  335.4 0.1 copy.9
  335.5 2.9 cholesky.16
  338.4 0.6 compare_reduce_fusion
  339.1 0.7 fusion
  339.7 2.4 custom-call.6
  342.2 0.3 fusion.1
  342.5 4.7 fusion.7
  347.2 0.0 all-reduce.2.cloned.1.call-update
  347.2 0.0 all-gather.2.cloned.1.call-done
  347.3 9.4 %convolution_convert_fusion = bf16[256,2560]{1,0:T(8,128)(2,1)} fusion(bf16[256,2560]{1,0:T(8,128)(2,1)S(1)} %copy-done, bf16[2560,2560]{1,0:T(8,128)(2,1)} %all-gather.2.cloned.1.call-done), kind=kOutput, calls=%fused_computation.1 | convolution fusion | flops 3356098560 | bytes 15728640 | tf_op jit(solution)/shard_map/dot_general | solution.py:9
  356.6 233.3 %all-reduce.2.cloned.1.call-done = f32[2560,32]{0,1:T(8,128)} async-done(((f32[2560,32]{0,1:T(8,128)}), f32[2560,32]{0,1:T(8,128)}) %all-reduce.2.cloned.1.call-update) | async-done | bytes 327696 | tf_op jit(solution)/shard_map/psum | solution.py:30
  589.9 1.0 broadcast_multiply_fusion
  590.9 0.0 copy-start.2
  590.9 5.7 convolution_subtract_fusion
  596.6 0.0 copy-done.2
  (2 shorter events, 0.0 us)
Async XLA Ops:
  7.2 1.3 copy-start
  7.2 155.6 %reduce-scatter.2.cloned.1.call-start = ((), (), s32[]{:S(2)}) async-start(), calls=%async_computation.2 | async-start | bytes 29491200 | tf_op jit(solution)/shard_map/reduce_scatter | solution.py:15
  20.6 326.7 %all-gather.2.cloned.1.call-start = ((), (), s32[]{:S(2)}) async-start(), calls=%async_computation.1 | async-start | bytes 14745600 | tf_op jit(solution)/shard_map/all_gather | solution.py:11
  21.3 146.6 %copy-start.3 = (f32[2560,32]{0,1:T(8,128)S(1)}, f32[2560,32]{0,1:T(8,128)}, u32[]{:S(2)}) copy-start(f32[2560,32]{0,1:T(8,128)} %param.9) | copy-start | bytes 983044
  21.3 568.6 %all-reduce.2.cloned.1.call-start = ((), (), s32[]{:S(2)}) async-start(), calls=%async_computation.3 | async-start | bytes 655360 | tf_op jit(solution)/shard_map/psum | solution.py:30
  166.2 1.7 copy-start.1
  590.9 5.7 copy-start.2
Sparse Core Ops, SparseCore 0:
  20.7 142.0 reduce-scatter.1
  164.6 72.7 all-gather.1
  347.3 242.5 all-reduce.1
where the time goes:
time: 603 us
  waiting for transfers between devices  375 us (62%)
  blocking collectives  165 us (27%)
  matrix products  35.1 us (6%)
  between operations  13.8 us (2%)
  other arithmetic  11.1 us (2%)
    psum x1, waiting for transfers between devices, shards(): q_factor = lax.psum(q_local, ('replica', 'fsdp')) / lax.axis_size('replica')  233 us
    reduce_scatter x1, waiting for transfers between devices, shards(): lax.psum_scatter(lax.dot_general(features, cotangent, (((0,), (0,)), ((),...  141 us
    psum x1, blocking collectives, shards(): psum = lax.psum(local_p, 'replica')  116 us
    psum x1, blocking collectives, shards(): gram = lax.psum(jnp.dot(psum.T, psum, precision=highest), 'fsdp')  48.7 us
  transfers between devices with their start and end apart: 3, of which 2 were waited for; matrix products, arithmetic and copies ran while one was open for 5% of the time, Pallas kernels for 0%

commit v1 on v0

v1 whole, which is shorter than its diff:
```python
import jax
import jax.numpy as jnp
from jax import lax
from jax.sharding import Mesh, PartitionSpec as P

HIGHEST = lax.Precision.HIGHEST
FSDP = ("y", "core")
ALL = ("z", "x", "y", "core")


def dot(a, b, ca, cb, precision=HIGHEST):
    return lax.dot_general(
        a, b, (((ca,), (cb,)), ((), ())), precision=precision, preferred_element_type=jnp.float32
    )


def exchange(u, axes):
    return lax.all_to_all(u, axes, 0, 0, tiled=True)


def swap_cores(v):
    return lax.ppermute(v, "core", [(0, 1), (1, 0)])


def sum_all(v):
    core = lax.axis_index("core")
    tiles = v.reshape(4, 8, 20, 128).transpose(0, 2, 1, 3).reshape(2, 16, 20, 128)
    mine = lax.dynamic_index_in_dim(tiles, core, 0, False)
    other = lax.dynamic_index_in_dim(tiles, 1 - core, 0, False)
    half = mine + swap_cores(other)
    part = exchange(half, ("x", "y")).sum(0)
    part = exchange(jnp.broadcast_to(part[None], (8, 20, 128)), "z").sum(0)
    half = exchange(jnp.broadcast_to(part[None], (16, 20, 128)), ("x", "y"))
    other = swap_cores(half)
    whole = jnp.where(core == 0, jnp.stack([half, other]), jnp.stack([other, half]))
    return whole.reshape(4, 20, 8, 128).transpose(0, 2, 1, 3).reshape(32, 2560)


def shards(features, cotangent, weight, feedback, start_factors):
    f32 = jnp.float32
    place = lax.axis_index(FSDP) * 320
    gathered = lax.all_gather(cotangent, FSDP, axis=0, tiled=True)
    columns = exchange(features.reshape(256, 8, 320).transpose(1, 0, 2), FSDP).reshape(2048, 320)

    x32, c32 = features.astype(f32), cotangent.astype(f32)
    small = dot(c32, start_factors, 1, 0)
    local = dot(small, x32, 0, 0)
    own = dot(start_factors, feedback, 0, 1)
    local = local + lax.dynamic_update_slice(jnp.zeros_like(local), own, (0, place))
    psum = sum_all(local)

    psum_own = lax.dynamic_slice(psum, (0, place), (32, 320))
    small = dot(psum, x32, 1, 1)
    local = dot(small, c32, 1, 0) + dot(psum_own, feedback, 1, 0)
    right = sum_all(local)

    gram = dot(psum, psum, 1, 1)
    lower = jnp.linalg.cholesky(gram)
    inverse = lax.linalg.triangular_solve(lower, jnp.eye(32, dtype=f32), left_side=True, lower=True)
    ortho = dot(inverse, psum_own, 1, 0)
    q_factor = dot(inverse, right, 1, 0) / 32

    grown = dot(columns, gathered, 0, 0, None) + feedback
    new_feedback = grown - dot(ortho, q_factor, 0, 0)

    back = dot(gathered, weight, 1, 1, None).astype(jnp.bfloat16)
    input_grad = exchange(back.reshape(8, 256, 320), FSDP).transpose(1, 0, 2).reshape(256, 2560)
    return (input_grad, new_feedback, q_factor.T)


def solution(mesh):
    split = Mesh(mesh.devices.reshape(8, 4, 4, 2), ALL)
    placed = (P(ALL, None), P(ALL, None), P(FSDP, None), P(ALL, None), P())
    return jax.shard_map(
        shards,
        mesh=split,
        in_specs=placed,
        out_specs=(P(ALL, None), P(ALL, None), P()),
        check_vma=False,
    )
```

time: 603 us -> 180 us (0.30)
  waiting for transfers between devices: 375 us -> 24.1 us
  blocking collectives: 165 us -> 58.4 us
  starting transfers between devices: 0.12 us -> 23.6 us
  local copies, waits for them, and re-layouts: 3.05 us -> 12.4 us
    psum x1 -> x0, waiting for transfers between devices: 233 us -> none  [shards(): q_factor = lax.psum(q_local, ('replica', 'fsdp')) / lax.axis_size('replica')]
    psum x2 -> x0, blocking collectives: 165 us -> none  [the longest x1 116 us: shards(): psum = lax.psum(local_p, 'replica')]
    reduce_scatter x1 -> x0, waiting for transfers between devices: 141 us -> none  [shards(): lax.psum_scatter(lax.dot_general(features, cotangent, (((0,), (0,)), ((),...]
    all_to_all x0 -> x5, blocking collectives: none -> 58.4 us  [exchange(): return lax.all_to_all(u, axes, 0, 0, tiled=True)]
    all_to_all x0 -> x3, waiting for transfers between devices: none -> 20 us  [exchange(): return lax.all_to_all(u, axes, 0, 0, tiled=True)]
    all_to_all x0 -> x3, starting transfers between devices: none -> 15.4 us  [exchange(): return lax.all_to_all(u, axes, 0, 0, tiled=True)]
    ppermute x0 -> x4, starting transfers between devices: none -> 8.19 us  [swap_cores(): return lax.ppermute(v, 'core', [(0, 1), (1, 0)])]
    dot_general x6 -> x12, matrix products: 34.8 us -> 35.3 us  [dot(): lax.dot_general(a, b, (((ca,), (cb,)), ((), ())), precision=precision, pr...]
  transfers between devices with their start and end apart: 3 -> 8, of which waited for: 2 -> 6; matrix products, arithmetic and copies ran while one was open for 5% -> 26% of each run, Pallas kernels for 0% -> 0%
where the time goes in v1:
time: 180 us; the launch traced here: 179 us
  blocking collectives  58.4 us (32%)
  matrix products  35.5 us (20%)
  waiting for transfers between devices  24.1 us (13%)
  starting transfers between devices  23.6 us (13%)
  between operations  14.3 us (8%)
  local copies, waits for them, and re-layouts  12.4 us (7%)
  other arithmetic  10.5 us (6%)
    all_to_all x5, blocking collectives, exchange(): return lax.all_to_all(u, axes, 0, 0, tiled=True)  58.4 us
    dot_general x12, matrix products, dot(): lax.dot_general(a, b, (((ca,), (cb,)), ((), ())), precision=precision, pr...  35.3 us
    all_to_all x3, waiting for transfers between devices, exchange(): return lax.all_to_all(u, axes, 0, 0, tiled=True)  20 us
    all_to_all x3, starting transfers between devices, exchange(): return lax.all_to_all(u, axes, 0, 0, tiled=True)  15.4 us
    ppermute x4, starting transfers between devices, swap_cores(): return lax.ppermute(v, 'core', [(0, 1), (1, 0)])  8.19 us
    unnamed x14, local copies, waits for them, and re-layouts  3.76 us
  transfers between devices with their start and end apart: 8, of which 6 were waited for; matrix products, arithmetic and copies ran while one was open for 26% of the time, Pallas kernels for 0%

profile of v1, /device:TPU:1, one launch (start us, length us, event | category | flops | bytes accessed | tf_op | source)
XLA Modules:
  0.0 178.8 jit_solution(14532307310707512299)
XLA Ops:
  7.2 0.7 all-gather.2.cloned.1.call-update
  7.9 2.7 %fusion.15 = f32[256,32]{0,1:T(8,128)S(1)} fusion(bf16[256,2560]{1,0:T(8,128)(2,1)} %param.6, f32[2560,32]{0,1:T(8,128)} %param.9), kind=kOutput, calls=%fused_computation.34 | convolution fusion | flops 251658240 | bytes 1671168 | tf_op jit(solution)/shard_map/dot_general | solution.py:12
  10.7 0.7 fusion.16
  11.4 3.8 %convolution_add_fusion.2 = f32[32,320]{1,0:T(8,128)S(1)} fusion(f32[2560,32]{0,1:T(8,128)} %param.9, f32[320,2560]{1,0:T(8,128)S(1)} %copy-done.1, f32[32,2560]{1,0:T(8,128)S(1)} %fusion.16, s32[]{:T(128)S(6)} %select_n.38), kind=kOutput, calls=%fused_computation.7 | convolution fusion | flops 314583040 | bytes 3686404 | tf_op jit(solution)/shard_map/dot_general | solution.py:12
  15.2 0.7 add.47
  16.0 0.7 copy-done.4
  16.7 1.0 reshape.64
  17.7 3.2 %collective-permute-start = (f32[16,20,128]{2,1,0:T(8,128)S(1)}, f32[16,20,128]{2,1,0:T(8,128)}, u32[]{:S(2)}, u32[]{:S(2)}) collective-permute-start(f32[16,20,128]{2,1,0:T(8,128)S(1)} %dynamic-slice_bitcast_fusion.1), channel_id=1, source_target_pairs={{0,1},{1,0},{2,3},{3,2},{4,5},{5,4},{6,7},{7,6},{8,9},{9,8},{10,11... | collective-permute-start | bytes 491528 | tf_op jit(solution)/shard_map/ppermute | solution.py:22
  20.9 1.2 collective-permute-done
  22.1 0.9 bitcast_add_fusion.1
  23.0 11.9 %all_to_all.40 = f32[16,20,128]{2,1,0:T(8,128)S(1)} all-to-all(f32[16,20,128]{2,1,0:T(8,128)S(1)} %bitcast_add_fusion.1), channel_id=1, replica_groups=mesh['z'=8,'x'=4,'y'=4,'core'=2] {'x','y'}, dimensions={0} | all-to-all | bytes 327680 | tf_op jit(solution)/shard_map/all_to_all | solution.py:18
  35.0 15.7 %all_to_all.41 = f32[8,20,128]{2,1,0:T(8,128)S(1)} all-to-all(f32[8,20,128]{2,1,0:T(8,128)S(1)} %broadcast_in_dim.9), channel_id=1, replica_groups=mesh['z'=8,'x'=4,'y'=4,'core'=2] {'z'}, dimensions={0} | all-to-all | bytes 163840 | tf_op jit(solution)/shard_map/all_to_all | solution.py:18
  50.7 10.5 %all_to_all.42 = f32[16,20,128]{2,1,0:T(8,128)S(1)} all-to-all(f32[16,20,128]{2,1,0:T(8,128)S(1)} %broadcast_in_dim.10), channel_id=1, replica_groups=mesh['z'=8,'x'=4,'y'=4,'core'=2] {'x','y'}, dimensions={0} | all-to-all | bytes 327680 | tf_op jit(solution)/shard_map/all_to_all | solution.py:18
  61.1 4.3 %collective-permute-start.1 = (f32[16,20,128]{2,1,0:T(8,128)S(1)}, f32[16,20,128]{2,1,0:T(8,128)S(1)}, u32[]{:S(2)}, u32[]{:S(2)}) collective-permute-start(f32[16,20,128]{2,1,0:T(8,128)S(1)} %all_to_all.42), channel_id=1, source_target_pairs={{0,1},{1,0},{2,3},{3,2},{4,5},{5,4},{6,7},{7,6},{8,9},{9,8},{10,11... | collective-permute-start | bytes 491528 | tf_op jit(solution)/shard_map/ppermute | solution.py:22
  65.4 1.1 collective-permute-done.1
  66.5 0.8 maximum_select_fusion
  67.3 1.0 select_n.42
  68.3 1.2 fusion.11
  69.5 2.1 %fusion.17 = f32[32,2560]{1,0:T(8,128)S(1)} fusion(f32[32,256]{1,0:T(8,128)S(1)} %fusion.11, bf16[256,2560]{1,0:T(8,128)(2,1)} %param.6), kind=kOutput, calls=%fused_computation.36 | convolution fusion | flops 251658240 | bytes 1671168 | tf_op jit(solution)/shard_map/dot_general | solution.py:12
  71.6 2.7 %fusion = f32[4,20,8,128]{3,2,1,0:T(8,128)} fusion(f32[32,2560]{1,0:T(8,128)S(1)} %fusion.17, f32[320,2560]{1,0:T(8,128)S(1)} %copy-done.2, f32[32,2560]{1,0:T(8,128)S(1)} %bitcast.79, s32[]{:T(128)S(6)} %select_n.38), kind=kOutput, calls=%fused_computation.6 | convolution fusion | flops 314654720 | bytes 3981316 | tf_op jit(solution)/shard_map/dot_general | solution.py:12
  74.3 1.7 reshape.67
  76.1 0.9 dynamic-slice_bitcast_fusion
  77.0 0.5 collective-permute-start.2
  77.5 1.1 collective-permute-done.2
  78.5 0.9 bitcast_add_fusion
  79.5 10.3 %all_to_all.43 = f32[16,20,128]{2,1,0:T(8,128)S(1)} all-to-all(f32[16,20,128]{2,1,0:T(8,128)S(1)} %bitcast_add_fusion), channel_id=1, replica_groups=mesh['z'=8,'x'=4,'y'=4,'core'=2] {'x','y'}, dimensions={0} | all-to-all | bytes 327680 | tf_op jit(solution)/shard_map/all_to_all | solution.py:18
  89.8 10.1 %all_to_all.44 = f32[8,20,128]{2,1,0:T(8,128)S(1)} all-to-all(f32[8,20,128]{2,1,0:T(8,128)S(1)} %broadcast_in_dim.11), channel_id=1, replica_groups=mesh['z'=8,'x'=4,'y'=4,'core'=2] {'z'}, dimensions={0} | all-to-all | bytes 163840 | tf_op jit(solution)/shard_map/all_to_all | solution.py:18
  99.9 0.7 broadcast_in_dim.12
  100.6 3.6 %all-to-all-start.7 = ((f32[16,20,128]{2,1,0:T(8,128)}), f32[16,20,128]{2,1,0:T(8,128)S(1)}, u32[]{:S(2)}, u32[]{:S(2)}) async-start(f32[16,20,128]{2,1,0:T(8,128)} %broadcast_in_dim.12), calls=%async_computation.7 | async-start | bytes 393216 | tf_op jit(solution)/shard_map/all_to_all | solution.py:18
  104.2 1.4 copy.21
  105.6 5.5 %all-to-all-done.7 = f32[16,20,128]{2,1,0:T(8,128)S(1)} async-done(((f32[16,20,128]{2,1,0:T(8,128)}), f32[16,20,128]{2,1,0:T(8,128)S(1)}, u32[]{:S(2)}, u32[]{:S(2)}) %all-to-all-start.7) | async-done | bytes 163872 | tf_op jit(solution)/shard_map/all_to_all | solution.py:18
  111.1 7.5 %all-to-all-start.1 = ((bf16[8,256,320]{1,2,0:T(8,128)(2,1)}), bf16[8,256,320]{1,2,0:T(8,128)(2,1)S(1)}, u32[]{:S(2)}, u32[]{:S(2)}) async-start(bf16[8,256,320]{1,2,0:T(8,128)(2,1)} %bitcast.75), calls=%async_computation.1 | async-start | bytes 2621440 | tf_op jit(solution)/shard_map/all_to_all | solution.py:18
  118.6 0.4 fusion.13
  119.1 2.9 %cholesky.17 = f32[32,32]{1,0:T(8,128)S(1)} custom-call(f32[32,32]{1,0:T(8,128)S(1)} %fusion.8), custom_call_target="Cholesky" | custom-call | tf_op jit(solution)/shard_map/jit(cholesky)/cholesky | solution.py:58
  122.0 0.6 compare_reduce_fusion
  122.7 0.7 fusion.5
  123.3 2.4 %custom-call.6 = f32[1,32,32]{1,2,0:T(8,128)S(1)} custom-call(f32[1,32,32]{2,1,0:T(8,128)S(1)} %fusion.5), custom_call_target="InvertDiagBlocksLowerTriangular" | custom-call | tf_op jit(solution)/shard_map/triangular_solve | solution.py:59
  126.5 10.0 %all-to-all-done.1 = bf16[8,256,320]{1,2,0:T(8,128)(2,1)S(1)} async-done(((bf16[8,256,320]{1,2,0:T(8,128)(2,1)}), bf16[8,256,320]{1,2,0:T(8,128)(2,1)S(1)}, u32[]{:S(2)}, u32[]{:S(2)}) %all-to-all-start.1) | async-done | bytes 1310752 | tf_op jit(solution)/shard_map/all_to_all | solution.py:18
  136.5 1.2 copy.30
  137.7 1.1 maximum_select_fusion.1
  138.8 0.4 convolution_multiply_fusion
  139.3 7.6 %convolution_convert_fusion = bf16[2048,320]{0,1:T(8,128)(2,1)S(1)} fusion(bf16[2048,2560]{1,0:T(8,128)(2,1)} %all-gather.2.cloned.1.call-done, bf16[320,2560]{1,0:T(8,128)(2,1)S(1)} %copy-done), kind=kOutput, calls=%fused_computation.4 | convolution fusion | flops 3356098560 | bytes 13434880 | tf_op jit(solution)/shard_map/dot_general | solution.py:12
  146.9 1.1 copy.32
  148.1 4.3 %all-to-all-start = ((bf16[8,256,320]{1,2,0:T(8,128)(2,1)}), bf16[8,256,320]{1,2,0:T(8,128)(2,1)S(1)}, u32[]{:S(2)}, u32[]{:S(2)}) async-start(bf16[8,256,320]{1,2,0:T(8,128)(2,1)} %bitcast.78), calls=%async_computation | async-start | bytes 2621440 | tf_op jit(solution)/shard_map/all_to_all | solution.py:18
  152.4 8.8 %convolution_add_fusion = f32[320,2560]{1,0:T(8,128)S(1)} fusion(f32[320,2560]{1,0:T(8,128)} %param.8, bf16[2048,320]{0,1:T(8,128)(2,1)} %bitcast.82, bf16[2048,2560]{1,0:T(8,128)(2,1)} %all-gather.2.cloned.1.call-done), kind=kOutput, calls=%fused_computation.1 | convolution fusion | flops 3356262400 | bytes 18350080 | tf_op jit(solution)/shard_map/dot_general | solution.py:12
  161.3 4.5 %convolution_subtract_fusion = f32[320,2560]{1,0:T(8,128)} fusion(f32[320,2560]{1,0:T(8,128)S(1)} %convolution_add_fusion, f32[32,320]{1,0:T(8,128)S(1)} %fusion.3, f32[32,2560]{1,0:T(8,128)S(1)} %convolution_multiply_fusion), kind=kOutput, calls=%fused_computation | convolution fusion | flops 315392000 | bytes 6922240 | tf_op jit(solution)/shard_map/dot_general | solution.py:12
  165.8 4.5 %all-to-all-done = bf16[8,256,320]{1,2,0:T(8,128)(2,1)S(1)} async-done(((bf16[8,256,320]{1,2,0:T(8,128)(2,1)}), bf16[8,256,320]{1,2,0:T(8,128)(2,1)S(1)}, u32[]{:S(2)}, u32[]{:S(2)}) %all-to-all-start) | async-done | bytes 1310752 | tf_op jit(solution)/shard_map/all_to_all | solution.py:18
  170.4 1.6 copy.26
  (29 shorter events, 1.1 us)
Async XLA Ops:
  7.2 132.1 %copy-start = (bf16[320,2560]{1,0:T(8,128)(2,1)S(1)}, bf16[320,2560]{1,0:T(8,128)(2,1)}, u32[]{:S(2)}) copy-start(bf16[320,2560]{1,0:T(8,128)(2,1)} %param.7) | copy-start | bytes 4915204
  7.2 3.5 %copy-start.3 = (bf16[256,2560]{1,0:T(8,128)(2,1)S(1)}, bf16[256,2560]{1,0:T(8,128)(2,1)}, u32[]{:S(2)}) copy-start(bf16[256,2560]{1,0:T(8,128)(2,1)} %param.5) | copy-start | bytes 3932164
  7.2 132.1 %all-gather.2.cloned.1.call-start = ((), (), s32[]{:S(2)}) async-start(), calls=%async_computation.8 | async-start | bytes 11796480 | tf_op jit(solution)/shard_map/all_gather | solution.py:42
  7.9 3.5 %copy-start.1 = (f32[320,2560]{1,0:T(8,128)S(1)}, f32[320,2560]{1,0:T(8,128)}, u32[]{:S(2)}) copy-start(f32[320,2560]{1,0:T(8,128)} %param.8) | copy-start | bytes 9830404
  15.9 0.7 copy-start.4
  17.7 4.4 %collective-permute-start = (f32[16,20,128]{2,1,0:T(8,128)S(1)}, f32[16,20,128]{2,1,0:T(8,128)}, u32[]{:S(2)}, u32[]{:S(2)}) collective-permute-start(f32[16,20,128]{2,1,0:T(8,128)S(1)} %dynamic-slice_bitcast_fusion.1), channel_id=1, source_target_pairs={{0,1},{1,0},{2,3},{3,2},{4,5},{5,4},{6,7},{7,6},{8,9},{9,8},{10,11... | collective-permute-start | bytes 491528 | tf_op jit(solution)/shard_map/ppermute | solution.py:22
  61.1 5.4 %collective-permute-start.1 = (f32[16,20,128]{2,1,0:T(8,128)S(1)}, f32[16,20,128]{2,1,0:T(8,128)S(1)}, u32[]{:S(2)}, u32[]{:S(2)}) collective-permute-start(f32[16,20,128]{2,1,0:T(8,128)S(1)} %all_to_all.42), channel_id=1, source_target_pairs={{0,1},{1,0},{2,3},{3,2},{4,5},{5,4},{6,7},{7,6},{8,9},{9,8},{10,11... | collective-permute-start | bytes 491528 | tf_op jit(solution)/shard_map/ppermute | solution.py:22
  68.3 3.3 %copy-start.2 = (f32[320,2560]{1,0:T(8,128)S(1)}, f32[320,2560]{1,0:T(8,128)}, u32[]{:S(2)}) copy-start(f32[320,2560]{1,0:T(8,128)} %param.8) | copy-start | bytes 9830404
  77.0 1.5 collective-permute-start.2
  100.6 10.5 %all-to-all-start.7 = ((f32[16,20,128]{2,1,0:T(8,128)}), f32[16,20,128]{2,1,0:T(8,128)S(1)}, u32[]{:S(2)}, u32[]{:S(2)}) async-start(f32[16,20,128]{2,1,0:T(8,128)} %broadcast_in_dim.12), calls=%async_computation.7 | async-start | bytes 393216 | tf_op jit(solution)/shard_map/all_to_all | solution.py:18
  111.1 25.4 %all-to-all-start.1 = ((bf16[8,256,320]{1,2,0:T(8,128)(2,1)}), bf16[8,256,320]{1,2,0:T(8,128)(2,1)S(1)}, u32[]{:S(2)}, u32[]{:S(2)}) async-start(bf16[8,256,320]{1,2,0:T(8,128)(2,1)} %bitcast.75), calls=%async_computation.1 | async-start | bytes 2621440 | tf_op jit(solution)/shard_map/all_to_all | solution.py:18
  126.0 11.8 %collective-permute-start.3 = (f32[16,20,128]{2,1,0:T(8,128)S(1)}, f32[16,20,128]{2,1,0:T(8,128)}, u32[]{:S(2)}, u32[]{:S(2)}) collective-permute-start(f32[16,20,128]{2,1,0:T(8,128)S(1)} %all-to-all-done.7), channel_id=1, source_target_pairs={{0,1},{1,0},{2,3},{3,2},{4,5},{5,4},{6,7},{7,6},{8,9},{9,8},{10,11... | collective-permute-start | bytes 491528 | tf_op jit(solution)/shard_map/ppermute | solution.py:22
  139.3 22.0 %copy-start.5 = (f32[32,2560]{1,0:T(8,128)}, f32[32,2560]{1,0:T(8,128)S(1)}, u32[]{:S(2)}) copy-start(f32[32,2560]{1,0:T(8,128)S(1)} %convolution_multiply_fusion) | copy-start | bytes 983044
  148.1 22.3 %all-to-all-start = ((bf16[8,256,320]{1,2,0:T(8,128)(2,1)}), bf16[8,256,320]{1,2,0:T(8,128)(2,1)S(1)}, u32[]{:S(2)}, u32[]{:S(2)}) async-start(bf16[8,256,320]{1,2,0:T(8,128)(2,1)} %bitcast.78), calls=%async_computation | async-start | bytes 2621440 | tf_op jit(solution)/shard_map/all_to_all | solution.py:18
Sparse Core Ops, SparseCore 0:
  9.9 69.6 all-gather.1

commit v2 on v1

v2 whole, which is shorter than its diff:
```python
import functools

import jax
import jax.numpy as jnp
from jax import lax
from jax.experimental import pallas as pl
from jax.experimental.pallas import tpu as pltpu
from jax.sharding import Mesh, PartitionSpec as P

FSDP = ("y", "core")
ALL = ("z", "x", "y", "core")
BF16 = jnp.bfloat16
F32 = jnp.float32
VMEM = pl.BlockSpec(memory_space=pltpu.VMEM)
ANY = pl.BlockSpec(memory_space=pl.ANY)
SMEM = pl.BlockSpec(memory_space=pltpu.SMEM)
AHEAD = [(2 * y + c, 2 * ((y + 1 - 2 * c) % 4) + c) for y in range(4) for c in range(2)]
BACK = [(b, a) for a, b in AHEAD]
ACROSS = [(2 * y + c, 2 * ((y + 2) % 4) + c) for y in range(4) for c in range(2)]
HALF = (16, 3, 8, 128)


def mm(a, b, ca, cb):
    return lax.dot_general(a, b, (((ca,), (cb,)), ((), ())), preferred_element_type=F32)


def terms(v):
    a = v.astype(BF16)
    rest = v - a.astype(F32)
    b = rest.astype(BF16)
    return a, b, (rest - b.astype(F32)).astype(BF16)


def stacked(v):
    return jnp.concatenate(terms(v), axis=0)


def folded(v):
    return v[0:32] + v[32:64] + v[64:96]


def put_window(place, feedback_ref, window_ref):
    core = place[0]
    zero = jnp.zeros((64, 2560), BF16)
    free = pl.multiple_of(320 * (1 - core), 64)
    first = pl.multiple_of(64 * core, 64)
    for i in range(5):
        rows = pl.ds(64 * i, 64)
        for t, term in enumerate(terms(feedback_ref[rows, :])):
            window_ref[t, pl.ds(pl.multiple_of(first + 64 * i, 64), 64), :] = term
    for t in range(3):
        window_ref[t, pl.ds(free, 64), :] = zero


def emit(core, value, mine_ref, other_ref):
    for tile in range(48):
        if tile < 40:
            r, j = divmod(tile, 20)
            low = value[8 * r : 8 * r + 8, 128 * j : 128 * j + 128]
            high = value[16 + 8 * r : 24 + 8 * r, 128 * j : 128 * j + 128]
            mine, other = jnp.where(core == 0, low, high), jnp.where(core == 0, high, low)
        else:
            mine = other = jnp.zeros((8, 128), F32)
        mine_ref[tile // 3, tile % 3] = mine
        other_ref[tile // 3, tile % 3] = other


def collect(core, mine_ref, other_ref, whole_ref):
    for tile in range(40):
        r, j = divmod(tile, 20)
        mine, other = mine_ref[tile // 3, tile % 3], other_ref[tile // 3, tile % 3]
        lanes = pl.ds(128 * j, 128)
        whole_ref[pl.ds(8 * r, 8), lanes] = jnp.where(core == 0, mine, other)
        whole_ref[pl.ds(16 + 8 * r, 8), lanes] = jnp.where(core == 0, other, mine)


def left_kernel(
    place, x_any, c_ref, s_ref, f_any, mine_ref, other_ref, window_ref, sum_ref, x_ref, f_ref, sems
):
    core, lane = place[0], pl.multiple_of(place[1], 128)
    x_copy = pltpu.make_async_copy(x_any, x_ref, sems.at[0])
    f_copy = pltpu.make_async_copy(f_any, f_ref, sems.at[1])
    x_copy.start()
    f_copy.start()
    s3 = stacked(s_ref[...])
    small = folded(mm(s3, c_ref[...], 1, 1))
    x_copy.wait()
    sum_ref[...] = folded(mm(stacked(small), x_ref[...], 1, 0))
    f_copy.wait()
    put_window(place, f_ref, window_ref)
    own = sum(folded(mm(s3, window_ref[t], 1, 1)) for t in range(3))
    sum_ref[:, pl.ds(lane, 384)] += own
    emit(core, sum_ref[...], mine_ref, other_ref)


def right_kernel(
    place, mine_ref, other_ref, x_ref, c_ref, f_ref, out_ref, away_ref, gram_ref, own_ref,
    window_ref, left_ref,
):
    core, lane = place[0], pl.multiple_of(place[1], 128)
    collect(core, mine_ref, other_ref, left_ref)
    left = left_ref[...]
    p3 = stacked(left)
    small = folded(mm(p3, x_ref[...], 1, 1))
    total = folded(mm(stacked(small), c_ref[...], 1, 0))
    put_window(place, f_ref, window_ref)
    own = left_ref[:, pl.ds(lane, 384)]
    own_ref[...] = own
    own3 = stacked(own)
    total += sum(folded(mm(own3, window_ref[t], 1, 0)) for t in range(3))
    emit(core, total, out_ref, away_ref)
    gram_ref[...] = sum(folded(mm(p3, p3[32 * t : 32 * t + 32], 1, 1)) for t in range(3))


def rows_kernel(
    place, x0, x1, x2, x3, c0, c1, c2, c3, f_ref, mine_ref, other_ref, turned, joined, full
):
    core = place[0]

    @pl.when(pl.program_id(0) == 0)
    def _():
        for k, x in enumerate((x0, x1, x2, x3)):
            turned[:, pl.ds(256 * k, 256)] = x[...].T

    for k, c in enumerate((c0, c1, c2, c3)):
        joined[pl.ds(256 * k, 256), :] = c[...]
    full[...] = mm(turned[...], joined[...], 1, 0)
    mine_ref[...] = full[pl.ds(pl.multiple_of(320 * core, 64), 320), :] + f_ref[...]
    other_ref[...] = full[pl.ds(pl.multiple_of(320 * (1 - core), 64), 320), :]


def back_kernel(n, place, *refs):
    cs, (w_ref, swapped_ref), outs, (both, totals) = refs[:n], refs[n : n + 2], refs[n + 2 : -2], refs[-2:]
    core, k = place[0], pl.program_id(0)
    both[pl.ds(pl.multiple_of(320 * core, 64), 320), :] = w_ref[...]
    both[pl.ds(pl.multiple_of(320 * (1 - core), 64), 320), :] = swapped_ref[...]
    for i in range(n):
        part = mm(cs[i][...], both[...], 1, 1)

        @pl.when(k == 0)
        def _():
            totals[i] = part

        @pl.when((k > 0) & (k < 4))
        def _():
            totals[i] += part

        @pl.when(k == 4)
        def _():
            outs[i][...] = (totals[i] + part).astype(BF16)


def back_columns(place, cs, weight, swapped):
    n = len(cs)
    block = pl.BlockSpec((256, 512), lambda i: (0, i))
    rows = pl.BlockSpec((320, 512), lambda i: (0, i))
    return pl.pallas_call(
        functools.partial(back_kernel, n),
        grid=(5,),
        in_specs=[SMEM] + [block] * n + [rows] * 2,
        out_specs=[pl.BlockSpec((256, 640), lambda i: (0, 0))] * n,
        out_shape=[jax.ShapeDtypeStruct((256, 640), BF16)] * n,
        scratch_shapes=[pltpu.VMEM((640, 512), BF16), pltpu.VMEM((n, 256, 640), F32)],
        compiler_params=pltpu.CompilerParams(vmem_limit_bytes=60 << 20),
        cost_estimate=pl.CostEstimate(flops=n * 84 * 10**7, bytes_accessed=(4 + n) << 20, transcendentals=0),
    )(place, *cs, weight, swapped)


def place_kernel(chips, g0, g1, g2, g3, out_ref):
    for k, g in enumerate((g0, g1, g2, g3)):
        out_ref[:, pl.ds(pl.multiple_of(640 * chips[k], 128), 640)] = g[...]


def placed_columns(chips, blocks):
    return pl.pallas_call(
        place_kernel,
        in_specs=[SMEM] + [VMEM] * 4,
        out_specs=VMEM,
        out_shape=jax.ShapeDtypeStruct((256, 2560), BF16),
        cost_estimate=pl.CostEstimate(flops=0, bytes_accessed=3 << 20, transcendentals=0),
    )(chips, *blocks)


def last_kernel(
    place, mine_ref, other_ref, inverse_ref, ortho_ref, a_ref, b_ref, new_ref, q_ref,
    right_ref, lhs_ref, rhs_ref,
):
    @pl.when(pl.program_id(0) == 0)
    def _():
        collect(place[0], mine_ref, other_ref, right_ref)
        i1, i2, i3 = terms(inverse_ref[...])
        r1, r2, r3 = terms(right_ref[...])
        q = sum(mm(a, b, 1, 0) for a, b in ((i1, r1), (i1, r2), (i2, r1), (i2, r2), (i1, r3), (i3, r1)))
        q = q / 32
        q_ref[...] = q
        q1, q2, q3 = terms(q)
        o1, o2, o3 = terms(ortho_ref[...])
        for k, (o, q) in enumerate(((o1, q1), (o1, q2), (o2, q1), (o2, q2), (o1, q3), (o3, q1))):
            lhs_ref[:, pl.ds(32 * k, 32)] = o
            rhs_ref[pl.ds(32 * k, 32), :] = q

    rows = pl.ds(pl.multiple_of(64 * pl.program_id(0), 64), 64)
    new_ref[...] = a_ref[...] + b_ref[...] - mm(lhs_ref[rows, :], rhs_ref[...], 1, 0)


def call(kernel, ins, outs, scratch, flops, size):
    return pl.pallas_call(
        kernel,
        in_specs=[SMEM] + ins,
        out_specs=[VMEM] * len(outs),
        out_shape=[jax.ShapeDtypeStruct(s, F32) for s in outs],
        scratch_shapes=scratch,
        compiler_params=pltpu.CompilerParams(vmem_limit_bytes=40 << 20),
        cost_estimate=pl.CostEstimate(flops=flops, bytes_accessed=size, transcendentals=0),
    )


def left_product(place, x, c, s, f):
    return call(
        left_kernel, [ANY, VMEM, VMEM, ANY], [HALF, HALF],
        [pltpu.VMEM((3, 384, 2560), BF16), pltpu.VMEM((32, 2560), F32),
         pltpu.VMEM((256, 2560), BF16), pltpu.VMEM((320, 2560), F32), pltpu.SemaphoreType.DMA((2,))],
        2 * 10**9, 7 << 20,
    )(place, x, c, s, f)


def right_product(place, mine, other, x, c, f):
    return call(
        right_kernel, [VMEM] * 5, [HALF, HALF, (32, 32), (32, 384)],
        [pltpu.VMEM((3, 384, 2560), BF16), pltpu.VMEM((32, 2560), F32)], 2 * 10**9, 7 << 20,
    )(place, mine, other, x, c, f)


def gradient_rows(place, xs, cs, feedback):
    whole = pl.BlockSpec((256, 640), lambda i: (0, 0))
    part = pl.BlockSpec((256, 256), lambda i: (0, i))
    rows = pl.BlockSpec((320, 256), lambda i: (0, i))
    return pl.pallas_call(
        rows_kernel,
        grid=(10,),
        in_specs=[SMEM] + [whole] * 4 + [part] * 4 + [rows],
        out_specs=[rows, rows],
        out_shape=[jax.ShapeDtypeStruct((320, 2560), F32)] * 2,
        scratch_shapes=[pltpu.VMEM((640, 1024), BF16), pltpu.VMEM((1024, 256), BF16),
                        pltpu.VMEM((640, 256), F32)],
        compiler_params=pltpu.CompilerParams(vmem_limit_bytes=60 << 20),
        cost_estimate=pl.CostEstimate(flops=34 * 10**8, bytes_accessed=17 << 20, transcendentals=0),
    )(place, *xs, *cs, feedback)


def last_step(place, mine, other, inverse, ortho, a, b):
    part = pl.BlockSpec((64, 2560), lambda i: (i, 0))
    half = pl.BlockSpec(HALF, lambda i: (0, 0, 0, 0))
    return pl.pallas_call(
        last_kernel,
        grid=(5,),
        in_specs=[SMEM, half, half, pl.BlockSpec((32, 32), lambda i: (0, 0)),
                  pl.BlockSpec((320, 32), lambda i: (0, 0)), part, part],
        out_specs=[part, pl.BlockSpec((32, 2560), lambda i: (0, 0))],
        out_shape=[jax.ShapeDtypeStruct((320, 2560), F32), jax.ShapeDtypeStruct((32, 2560), F32)],
        scratch_shapes=[pltpu.VMEM((32, 2560), F32), pltpu.VMEM((320, 192), BF16),
                        pltpu.VMEM((192, 2560), BF16)],
        compiler_params=pltpu.CompilerParams(vmem_limit_bytes=32 << 20),
        cost_estimate=pl.CostEstimate(flops=3 * 10**8, bytes_accessed=10 << 20, transcendentals=0),
    )(place, mine, other, inverse, ortho, a, b)


def exchange(u, axes):
    return lax.all_to_all(u, axes, 0, 0, tiled=True)


def swap(v):
    return lax.ppermute(v, "core", [(0, 1), (1, 0)])


def send(v, pairs):
    return lax.ppermute(v, FSDP, pairs)


def tie(*values):
    return lax.optimization_barrier(values)


def second(v):
    return exchange(jnp.broadcast_to(v.sum(0)[None], (8, 3, 8, 128)), "z")


def third(v):
    return exchange(jnp.broadcast_to(v.sum(0)[None], HALF), ("x", "y"))


def shards(features, cotangent, weight, feedback, start_factors):
    core, y = lax.axis_index("core"), lax.axis_index("y")
    place = jnp.stack([core, 128 * (5 * y + 2 * core)]).astype(jnp.int32)
    ahead, back = lax.rem(y + 5 - 2 * core, 4), lax.rem(y + 3 + 2 * core, 4)
    across = lax.rem(y + 2, 4)

    def columns(chip):
        return lax.dynamic_slice(features, (0, 640 * chip), (256, 640))

    c1, c2 = send(cotangent, AHEAD), send(cotangent, BACK)
    swapped = swap(weight)

    mine, other = left_product(place, features, cotangent, start_factors.T, feedback)
    half = exchange(mine + swap(other), ("x", "y"))
    (g0,) = back_columns(place, (cotangent,), weight, swapped)
    half, g0, features_later = tie(half, g0, features)

    def columns(chip):
        return lax.dynamic_slice(features_later, (0, 640 * chip), (256, 640))

    x0 = columns(y)
    x1, x2 = send(columns(ahead), AHEAD), send(columns(back), BACK)
    x3 = send(columns(across), ACROSS)
    half = second(half)
    half, c1, c2 = tie(half, c1, c2)
    c3 = send(c1, AHEAD)
    half = third(half)
    g1, g2 = back_columns(place, (c1, c2), weight, swapped)
    half, g1, g2 = tie(half, g1, g2)
    u1, u2 = send(g1, BACK), send(g2, AHEAD)

    mine, other, gram, own = right_product(place, half, swap(half), features, cotangent, feedback)
    half = exchange(mine + swap(other), ("x", "y"))
    lower = jnp.linalg.cholesky(gram)
    inverse = lax.linalg.triangular_solve(lower, jnp.eye(32, dtype=F32), left_side=True, lower=True)
    ortho = lax.dot_general(
        own, inverse, (((0,), (1,)), ((), ())), precision=lax.Precision.HIGHEST,
        preferred_element_type=F32,
    )
    ortho = lax.dynamic_slice(ortho, (64 * core, 0), (320, 32))
    half, ortho, inverse, c3, x1, x2, x3 = tie(half, ortho, inverse, c3, x1, x2, x3)
    half = second(half)
    (g3,) = back_columns(place, (c3,), weight, swapped)
    grown, away = gradient_rows(place, (x0, x1, x2, x3), (cotangent, c1, c2, c3), feedback)
    half, grown, away, g3, u1, u2 = tie(half, grown, away, g3, u1, u2)
    away, u3 = swap(away), send(g3, ACROSS)
    half = third(half)
    half, away, u3 = tie(half, away, u3)

    new_feedback, q_factor = last_step(place, half, swap(half), inverse, ortho, grown, away)
    chips = jnp.stack([y, ahead, back, across]).astype(jnp.int32)
    input_grad = placed_columns(chips, (g0, u1, u2, u3))
    return (input_grad, new_feedback, q_factor.T)


def solution(mesh):
    split = Mesh(mesh.devices.reshape(8, 4, 4, 2), ALL)
    placed = (P(ALL, None), P(ALL, None), P(FSDP, None), P(ALL, None), P())
    return jax.shard_map(
        shards,
        mesh=split,
        in_specs=placed,
        out_specs=(P(ALL, None), P(ALL, None), P()),
        check_vma=False,
    )
```

time: 180 us -> 161 us (0.89)
  Pallas kernels: 0 us -> 50.5 us
  blocking collectives: 58.4 us -> 11.9 us
  matrix products: 35.5 us -> 0.68 us
  starting transfers between devices: 23.6 us -> 52.5 us
  between operations: 14.3 us -> 0.88 us
  waiting for transfers between devices: 24.1 us -> 20.7 us
    pallas_call x0 -> x8, Pallas kernels: none -> 50.5 us  [the longest x3 19.5 us: back_columns(): pl.pallas_call(functools.partial(back_kernel, n), grid=(5,), in_specs=[SM...]
    all_to_all x5 -> x1, blocking collectives: 58.4 us -> 11.9 us  [exchange(): return lax.all_to_all(u, axes, 0, 0, tiled=True)]
    dot_general x12 -> x1, matrix products: 35.3 us -> 0.49 us  [shards(): lax.dot_general(own, inverse, (((0,), (1,)), ((), ())), precision=lax.Pre...]
    ppermute x4 -> x15, starting transfers between devices: 8.19 us -> 23.8 us  [the longest x9 15.2 us: send(): return lax.ppermute(v, FSDP, pairs)]
    all_to_all x3 -> x5, starting transfers between devices: 15.4 us -> 28.8 us  [exchange(): return lax.all_to_all(u, axes, 0, 0, tiled=True)]
    unnamed x14 -> x34, local copies, waits for them, and re-layouts: 3.76 us -> 10.1 us
    reshape x4 -> x0, local copies, waits for them, and re-layouts: 5.11 us -> none  [the longest x2 2.74 us: sum_all(): v.reshape(4, 8, 20, 128).transpose(0, 2, 1, 3).reshape(2, 16, 20, 128)]
    select_n x2 -> x0, other arithmetic: 1.83 us -> none  [sum_all(): jnp.where(core == 0, jnp.stack([half, other]), jnp.stack([other, half]))]
  transfers between devices with their start and end apart: 8 -> 20, of which waited for: 6 -> 5; matrix products, arithmetic and copies ran while one was open for 26% -> 8% of each run, Pallas kernels for 0% -> 28%
where the time goes in v2:
time: 161 us; the launch traced here: 160 us
  starting transfers between devices  52.5 us (33%)
  Pallas kernels  50.5 us (31%)
  waiting for transfers between devices  20.7 us (13%)
  local copies, waits for them, and re-layouts  14 us (9%)
  blocking collectives  11.9 us (7%)
  other arithmetic  8.87 us (6%)
    all_to_all x5, starting transfers between devices, exchange(): return lax.all_to_all(u, axes, 0, 0, tiled=True)  28.8 us
    pallas_call x3, Pallas kernels, back_columns(): pl.pallas_call(functools.partial(back_kernel, n), grid=(5,), in_specs=[SM...  19.5 us
    all_to_all x5, waiting for transfers between devices, exchange(): return lax.all_to_all(u, axes, 0, 0, tiled=True)  18.2 us
    ppermute x9, starting transfers between devices, send(): return lax.ppermute(v, FSDP, pairs)  15.2 us
    pallas_call x1, Pallas kernels, gradient_rows(): pl.pallas_call(rows_kernel, grid=(10,), in_specs=[SMEM] + [whole] * 4 + [...  12.3 us
    all_to_all x1, blocking collectives, exchange(): return lax.all_to_all(u, axes, 0, 0, tiled=True)  11.9 us
    unnamed x34, local copies, waits for them, and re-layouts  10.1 us
    ppermute x6, starting transfers between devices, swap(): return lax.ppermute(v, 'core', [(0, 1), (1, 0)])  8.6 us
  transfers between devices with their start and end apart: 20, of which 5 were waited for; matrix products, arithmetic and copies ran while one was open for 8% of the time, Pallas kernels for 28%

profile of v2, /device:TPU:1, one launch (start us, length us, event | category | flops | bytes accessed | tf_op | source)
XLA Modules:
  0.0 160.1 jit_solution(15337779349739560081)
XLA Ops:
  0.6 3.3 %collective-permute-start.1 = (bf16[320,2560]{1,0:T(8,128)(2,1)}, bf16[320,2560]{1,0:T(8,128)(2,1)S(1)}, u32[]{:S(2)}, u32[]{:S(2)}) collective-permute-start(bf16[320,2560]{1,0:T(8,128)(2,1)} %refs_1_.3), channel_id=1, source_target_pairs={{0,1},{1,0},{2,3},{3,2},{4,5},{5,4},{6,7},{7,6},{8,9},{9,8},{10,11... | collective-permute-start | bytes 4915208 | tf_op jit(solution)/shard_map/ppermute | solution.py:273
  4.0 2.7 %collective-permute-start.2 = (bf16[256,2560]{1,0:T(8,128)(2,1)}, bf16[256,2560]{1,0:T(8,128)(2,1)}, u32[]{:S(2)}, u32[]{:S(2)}) collective-permute-start(bf16[256,2560]{1,0:T(8,128)(2,1)} %c0.1), channel_id=1, source_target_pairs={{0,2},{1,7},{2,4},{3,1},{4,6},{5,3},{6,0},{7,5},{8,10},{9,15},{10,... | collective-permute-start | bytes 3932168 | tf_op jit(solution)/shard_map/ppermute | solution.py:277
  6.7 1.3 copy-done.1
  8.0 1.3 copy-done.3
  9.3 1.9 %copy-done.9 = f32[320,2560]{1,0:T(8,128)S(1)} copy-done((f32[320,2560]{1,0:T(8,128)S(1)}, f32[320,2560]{1,0:T(8,128)}, u32[]{:S(2)}) %copy-start.9) | copy-done | bytes 3276824
  11.3 1.0 copy-done.11
  12.2 5.8 %shard_map.76 = (f32[16,3,8,128]{3,2,1,0:T(8,128)S(1)}, f32[16,3,8,128]{3,2,1,0:T(8,128)S(1)}) custom-call(s32[2]{0:T(128)S(1)} %pad_add_fusion.1.place, bf16[256,2560]{1,0:T(8,128)(2,1)S(1)} %copy-done.3, bf16[256,2560]{1,0:T(8,128)(2,1)S(1)} %copy-done.1, f32[32,2560]{1,0:T(8,128)S(1)} %bitcast.19, f32[320,2560]{1,0:T(8,128)S(1)} %copy-done.9), custom_call_target="tpu_custom_call" | custom-call | flops 2000000000 | bytes 7340032 | tf_op jit(solution)/shard_map/pallas_call | solution.py:219
  18.2 1.4 collective-permute-done
  19.6 0.7 add.52
  20.3 5.1 %all-to-all-start = ((f32[16,3,8,128]{3,2,1,0:T(8,128)}), f32[16,3,8,128]{3,2,1,0:T(8,128)S(1)}, u32[]{:S(2)}, u32[]{:S(2)}) async-start(f32[16,3,8,128]{3,2,1,0:T(8,128)} %add.52), calls=%async_computation | async-start | bytes 393216 | tf_op jit(solution)/shard_map/all_to_all | solution.py:269
  25.4 1.2 copy-done.12
  26.6 5.7 %shard_map.77.g0 = bf16[256,640]{1,0:T(8,128)(2,1)} custom-call(s32[2]{0:T(128)} %copy-done.6, bf16[256,2560]{1,0:T(8,128)(2,1)} %c0.1, bf16[320,2560]{1,0:T(8,128)(2,1)} %refs_1_.3, bf16[320,2560]{1,0:T(8,128)(2,1)} %copy-done.12), custom_call_target="tpu_custom_call" | custom-call | flops 840000000 | bytes 5242880 | tf_op jit(solution)/shard_map/pallas_call | solution.py:157
  32.4 4.1 %all-to-all-done = f32[16,3,8,128]{3,2,1,0:T(8,128)S(1)} async-done(((f32[16,3,8,128]{3,2,1,0:T(8,128)}), f32[16,3,8,128]{3,2,1,0:T(8,128)S(1)}, u32[]{:S(2)}, u32[]{:S(2)}) %all-to-all-start) | async-done | bytes 196640 | tf_op jit(solution)/shard_map/all_to_all | solution.py:269
  36.5 0.6 broadcast_in_dim.10
  37.1 7.6 %all-to-all-start.1 = ((f32[8,3,8,128]{3,2,1,0:T(8,128)}), f32[8,3,8,128]{3,2,1,0:T(8,128)S(1)}, u32[]{:S(2)}, u32[]{:S(2)}) async-start(f32[8,3,8,128]{3,2,1,0:T(8,128)} %broadcast_in_dim.10), calls=%async_computation.1 | async-start | bytes 196608 | tf_op jit(solution)/shard_map/all_to_all | solution.py:269
  44.8 7.6 %all-to-all-done.1 = f32[8,3,8,128]{3,2,1,0:T(8,128)S(1)} async-done(((f32[8,3,8,128]{3,2,1,0:T(8,128)}), f32[8,3,8,128]{3,2,1,0:T(8,128)S(1)}, u32[]{:S(2)}, u32[]{:S(2)}) %all-to-all-start.1) | async-done | bytes 98336 | tf_op jit(solution)/shard_map/all_to_all | solution.py:269
  52.3 0.7 broadcast_in_dim.11
  53.0 6.9 %all-to-all-start.2 = ((f32[16,3,8,128]{3,2,1,0:T(8,128)}), f32[16,3,8,128]{3,2,1,0:T(8,128)S(1)}, u32[]{:S(2)}, u32[]{:S(2)}) async-start(f32[16,3,8,128]{3,2,1,0:T(8,128)} %broadcast_in_dim.11), calls=%async_computation.2 | async-start | bytes 393216 | tf_op jit(solution)/shard_map/all_to_all | solution.py:269
  59.9 8.0 %shard_map.78 = (bf16[256,640]{1,0:T(8,128)(2,1)}, bf16[256,640]{1,0:T(8,128)(2,1)}) custom-call(s32[2]{0:T(128)} %copy-done.6, bf16[256,2560]{1,0:T(8,128)(2,1)} %collective-permute-done.2.refs_0_.c1, bf16[256,2560]{1,0:T(8,128)(2,1)} %copy-done.15, bf16[320,2560]{1,0:T(8,128)(2,1)} %refs_1_.3, bf16[320,2560]{1,0:T(8,128)(2,1)} %copy-done.12), custom_call_target="tpu_custom_call" | custom-call | flops 1680000000 | bytes 6291456 | tf_op jit(solution)/shard_map/pallas_call | solution.py:157
  68.0 2.6 %collective-permute-start.4 = (f32[16,3,8,128]{3,2,1,0:T(8,128)S(1)}, f32[16,3,8,128]{3,2,1,0:T(8,128)S(1)}, u32[]{:S(2)}, u32[]{:S(2)}) collective-permute-start(f32[16,3,8,128]{3,2,1,0:T(8,128)S(1)} %all-to-all-done.2.mine_ref), channel_id=1, source_target_pairs={{0,1},{1,0},{2,3},{3,2},{4,5},{5,4},{6,7},{7,6},{8,9},{9,8},{10,11... | collective-permute-start | bytes 589832 | tf_op jit(solution)/shard_map/ppermute | solution.py:273
  70.5 1.1 constant_dynamic-slice_fusion
  71.6 3.2 %collective-permute-start.9 = (bf16[256,640]{1,0:T(8,128)(2,1)}, bf16[256,640]{1,0:T(8,128)(2,1)}, u32[]{:S(2)}, u32[]{:S(2)}) collective-permute-start(bf16[256,640]{1,0:T(8,128)(2,1)} %get-tuple-element.78), channel_id=1, source_target_pairs={{0,4},{1,5},{2,6},{3,7},{4,0},{5,1},{6,2},{7,3},{8,12},{9,13},{10,... | collective-permute-start | bytes 983048 | tf_op jit(solution)/shard_map/ppermute | solution.py:277
  75.1 2.4 %collective-permute-start.7 = (bf16[256,640]{1,0:T(8,128)(2,1)}, bf16[256,640]{1,0:T(8,128)(2,1)}, u32[]{:S(2)}, u32[]{:S(2)}) collective-permute-start(bf16[256,640]{1,0:T(8,128)(2,1)} %get-tuple-element.80), channel_id=1, source_target_pairs={{0,2},{1,7},{2,4},{3,1},{4,6},{5,3},{6,0},{7,5},{8,10},{9,15},{10,... | collective-permute-start | bytes 983048 | tf_op jit(solution)/shard_map/ppermute | solution.py:277
  77.5 1.9 %copy-done.10 = f32[320,2560]{1,0:T(8,128)S(1)} copy-done((f32[320,2560]{1,0:T(8,128)S(1)}, f32[320,2560]{1,0:T(8,128)}, u32[]{:S(2)}) %copy-start.10) | copy-done | bytes 3276824
  79.5 4.1 %shard_map.79 = (f32[16,3,8,128]{3,2,1,0:T(8,128)S(1)}, f32[16,3,8,128]{3,2,1,0:T(8,128)S(1)}, f32[32,32]{1,0:T(8,128)S(1)}, f32[32,384]{1,0:T(8,128)S(1)}) custom-call(s32[2]{0:T(128)S(1)} %copy-done.7, f32[16,3,8,128]{3,2,1,0:T(8,128)S(1)} %all-to-all-done.2.mine_ref, f32[16,3,8,128]{3,2,1,0:T(8,128)S(1)} %collective-permute-done.4.other_ref, ...), custom_call_target="tpu_custom_call" | custom-call | flops 2000000000 | bytes 7340032 | tf_op jit(solution)/shard_map/pallas_call | solution.py:228
  83.6 2.9 %cholesky.17 = f32[32,32]{1,0:T(8,128)S(1)} custom-call(f32[32,32]{1,0:T(8,128)S(1)} %fusion.3), custom_call_target="Cholesky" | custom-call | tf_op jit(solution)/shard_map/jit(cholesky)/cholesky | solution.py:325
  86.6 0.7 compare_reduce_fusion
  87.3 0.6 fusion
  87.9 2.4 %custom-call.6 = f32[1,32,32]{1,2,0:T(8,128)S(1)} custom-call(f32[1,32,32]{2,1,0:T(8,128)S(1)} %fusion), custom_call_target="InvertDiagBlocksLowerTriangular" | custom-call | tf_op jit(solution)/shard_map/triangular_solve | solution.py:326
  90.8 1.0 collective-permute-done.5
  91.9 1.4 collective-permute-start.10
  93.3 0.7 add.53
  94.0 5.8 %all-to-all-start.3 = ((f32[16,3,8,128]{3,2,1,0:T(8,128)}), f32[16,3,8,128]{3,2,1,0:T(8,128)S(1)}, u32[]{:S(2)}, u32[]{:S(2)}) async-start(f32[16,3,8,128]{3,2,1,0:T(8,128)} %add.53), calls=%async_computation.3 | async-start | bytes 393216 | tf_op jit(solution)/shard_map/all_to_all | solution.py:269
  99.8 0.5 fusion.4
  100.3 0.7 constant_dynamic-slice_fusion.4.ortho_ref
  101.0 2.6 %collective-permute-start.11 = (bf16[256,640]{1,0:T(8,128)(2,1)S(1)}, bf16[256,640]{1,0:T(8,128)(2,1)S(1)}, u32[]{:S(2)}, u32[]{:S(2)}) collective-permute-start(bf16[256,640]{1,0:T(8,128)(2,1)S(1)} %copy-done.16), channel_id=1, source_target_pairs={{0,2},{1,7},{2,4},{3,1},{4,6},{5,3},{6,0},{7,5},{8,10},{9,15},{10,... | collective-permute-start | bytes 983048 | tf_op jit(solution)/shard_map/ppermute | solution.py:277
  103.5 6.6 %all-to-all-done.3 = f32[16,3,8,128]{3,2,1,0:T(8,128)S(1)} async-done(((f32[16,3,8,128]{3,2,1,0:T(8,128)}), f32[16,3,8,128]{3,2,1,0:T(8,128)S(1)}, u32[]{:S(2)}, u32[]{:S(2)}) %all-to-all-start.3) | async-done | bytes 196640 | tf_op jit(solution)/shard_map/all_to_all | solution.py:269
  110.2 0.7 broadcast_in_dim.12
  110.8 3.4 %all-to-all-start.4 = ((f32[8,3,8,128]{3,2,1,0:T(8,128)}), f32[8,3,8,128]{3,2,1,0:T(8,128)S(1)}, u32[]{:S(2)}, u32[]{:S(2)}) async-start(f32[8,3,8,128]{3,2,1,0:T(8,128)} %broadcast_in_dim.12), calls=%async_computation.4 | async-start | bytes 196608 | tf_op jit(solution)/shard_map/all_to_all | solution.py:269
  114.2 12.3 %shard_map.80 = (f32[320,2560]{1,0:T(8,128)}, f32[320,2560]{1,0:T(8,128)}) custom-call(s32[2]{0:T(128)} %copy-done.6, bf16[256,640]{1,0:T(8,128)(2,1)} %get-tuple-element.77.x0, bf16[256,640]{1,0:T(8,128)(2,1)} %collective-permute-done.7.x1, bf16[256,640]{1,0:T(8,128)(2,1)} %collective-permute-done.8.x2, bf16[256,640]{1,0:T(8,128)(2,1)} %collective-permute-done.9.x3, ...), custom_call_target="tpu_custom_call" | custom-call | flops 3400000000 | bytes 17825792 | tf_op jit(solution)/shard_map/pallas_call | solution.py:238
  126.5 5.7 %shard_map.81 = bf16[256,640]{1,0:T(8,128)(2,1)} custom-call(s32[2]{0:T(128)} %copy-done.6, bf16[256,2560]{1,0:T(8,128)(2,1)} %collective-permute-done.6.c3.refs_0_, bf16[320,2560]{1,0:T(8,128)(2,1)} %refs_1_.3, bf16[320,2560]{1,0:T(8,128)(2,1)} %copy-done.12), custom_call_target="tpu_custom_call" | custom-call | flops 840000000 | bytes 5242880 | tf_op jit(solution)/shard_map/pallas_call | solution.py:157
  133.1 2.6 %collective-permute-start.13 = (bf16[256,640]{1,0:T(8,128)(2,1)}, bf16[256,640]{1,0:T(8,128)(2,1)}, u32[]{:S(2)}, u32[]{:S(2)}) collective-permute-start(bf16[256,640]{1,0:T(8,128)(2,1)} %shard_map.81), channel_id=1, source_target_pairs={{0,4},{1,5},{2,6},{3,7},{4,0},{5,1},{6,2},{7,3},{8,12},{9,13},{10,... | collective-permute-start | bytes 983048 | tf_op jit(solution)/shard_map/ppermute | solution.py:277
  135.7 11.9 %all_to_all.30.mine_ref = f32[16,3,8,128]{3,2,1,0:T(8,128)S(1)} all-to-all(f32[16,3,8,128]{3,2,1,0:T(8,128)S(1)} %broadcast_in_dim.13), channel_id=1, replica_groups=mesh['z'=8,'x'=4,'y'=4,'core'=2] {'x','y'}, dimensions={0} | all-to-all | bytes 393216 | tf_op jit(solution)/shard_map/all_to_all | solution.py:269
  147.6 2.0 %collective-permute-start.14 = (f32[16,3,8,128]{3,2,1,0:T(8,128)S(1)}, f32[16,3,8,128]{3,2,1,0:T(8,128)}, u32[]{:S(2)}, u32[]{:S(2)}) collective-permute-start(f32[16,3,8,128]{3,2,1,0:T(8,128)S(1)} %all_to_all.30.mine_ref), channel_id=1, source_target_pairs={{0,1},{1,0},{2,3},{3,2},{4,5},{5,4},{6,7},{7,6},{8,9},{9,8},{10,11... | collective-permute-start | bytes 589832 | tf_op jit(solution)/shard_map/ppermute | solution.py:273
  149.7 0.6 pad_add_fusion.chips
  150.3 2.4 %shard_map.82 = bf16[256,2560]{1,0:T(8,128)(2,1)} custom-call(s32[4]{0:T(128)} %pad_add_fusion.chips, bf16[256,640]{1,0:T(8,128)(2,1)} %shard_map.77.g0, bf16[256,640]{1,0:T(8,128)(2,1)} %copy-done.13, bf16[256,640]{1,0:T(8,128)(2,1)} %copy-done.14, bf16[256,640]{1,0:T(8,128)(2,1)} %collective-permute-done.13.g3), custom_call_target="tpu_custom_call" | custom-call | bytes 3145728 | tf_op jit(solution)/shard_map/pallas_call | solution.py:175
  152.8 0.9 copy-done.5
  153.7 6.4 %shard_map.83 = (f32[320,2560]{1,0:T(8,128)}, f32[32,2560]{1,0:T(8,128)}) custom-call(s32[2]{0:T(128)S(1)} %copy-done.8, f32[16,3,8,128]{3,2,1,0:T(8,128)S(1)} %all_to_all.30.mine_ref, f32[16,3,8,128]{3,2,1,0:T(8,128)} %collective-permute-done.14.other_ref, f32[32,32]{1,0:T(8,128)S(1)} %fusion.1.inverse_ref, f32[320,32]{1,0:T(8,128)S(1)} %copy-done.5, ...), custom_call_target="tpu_custom_call" | custom-call | flops 300000000 | bytes 10485760 | tf_op jit(solution)/shard_map/pallas_call | solution.py:254
  (58 shorter events, 2.0 us)
Async XLA Ops:
  0.6 24.8 %collective-permute-start.1 = (bf16[320,2560]{1,0:T(8,128)(2,1)}, bf16[320,2560]{1,0:T(8,128)(2,1)S(1)}, u32[]{:S(2)}, u32[]{:S(2)}) collective-permute-start(bf16[320,2560]{1,0:T(8,128)(2,1)} %refs_1_.3), channel_id=1, source_target_pairs={{0,1},{1,0},{2,3},{3,2},{4,5},{5,4},{6,7},{7,6},{8,9},{9,8},{10,11... | collective-permute-start | bytes 4915208 | tf_op jit(solution)/shard_map/ppermute | solution.py:273
  4.0 40.8 %collective-permute-start.3 = (bf16[256,2560]{1,0:T(8,128)(2,1)}, bf16[256,2560]{1,0:T(8,128)(2,1)S(1)}, u32[]{:S(2)}, u32[]{:S(2)}) collective-permute-start(bf16[256,2560]{1,0:T(8,128)(2,1)} %c0.1), channel_id=1, source_target_pairs={{2,0},{7,1},{4,2},{1,3},{6,4},{3,5},{0,6},{5,7},{10,8},{15,9},{12,... | collective-permute-start | bytes 3932168 | tf_op jit(solution)/shard_map/ppermute | solution.py:277
  4.0 40.8 %collective-permute-start.2 = (bf16[256,2560]{1,0:T(8,128)(2,1)}, bf16[256,2560]{1,0:T(8,128)(2,1)}, u32[]{:S(2)}, u32[]{:S(2)}) collective-permute-start(bf16[256,2560]{1,0:T(8,128)(2,1)} %c0.1), channel_id=1, source_target_pairs={{0,2},{1,7},{2,4},{3,1},{4,6},{5,3},{6,0},{7,5},{8,10},{9,15},{10,... | collective-permute-start | bytes 3932168 | tf_op jit(solution)/shard_map/ppermute | solution.py:277
  6.7 11.3 %copy-start.6 = (s32[2]{0:T(128)}, s32[2]{0:T(128)S(1)}, u32[]{:S(2)}) copy-start(s32[2]{0:T(128)S(1)} %pad_add_fusion.1.place) | copy-start | bytes 28
  6.7 1.3 copy-start.1
  8.0 1.3 copy-start.3
  9.3 1.9 %copy-start.9 = (f32[320,2560]{1,0:T(8,128)S(1)}, f32[320,2560]{1,0:T(8,128)}, u32[]{:S(2)}) copy-start(f32[320,2560]{1,0:T(8,128)} %f_ref.3) | copy-start | bytes 9830404
  11.3 1.0 copy-start.11
  18.1 1.5 collective-permute-start
  20.3 16.2 %all-to-all-start = ((f32[16,3,8,128]{3,2,1,0:T(8,128)}), f32[16,3,8,128]{3,2,1,0:T(8,128)S(1)}, u32[]{:S(2)}, u32[]{:S(2)}) async-start(f32[16,3,8,128]{3,2,1,0:T(8,128)} %add.52), calls=%async_computation | async-start | bytes 393216 | tf_op jit(solution)/shard_map/all_to_all | solution.py:269
  25.4 1.2 copy-start.12
  37.1 15.2 %all-to-all-start.1 = ((f32[8,3,8,128]{3,2,1,0:T(8,128)}), f32[8,3,8,128]{3,2,1,0:T(8,128)S(1)}, u32[]{:S(2)}, u32[]{:S(2)}) async-start(f32[8,3,8,128]{3,2,1,0:T(8,128)} %broadcast_in_dim.10), calls=%async_computation.1 | async-start | bytes 196608 | tf_op jit(solution)/shard_map/all_to_all | solution.py:269
  44.8 15.2 %copy-start.15 = (bf16[256,2560]{1,0:T(8,128)(2,1)}, bf16[256,2560]{1,0:T(8,128)(2,1)S(1)}, u32[]{:S(2)}) copy-start(bf16[256,2560]{1,0:T(8,128)(2,1)S(1)} %collective-permute-done.3.refs_1_.c2) | copy-start | bytes 3932164
  53.0 14.9 %all-to-all-start.2 = ((f32[16,3,8,128]{3,2,1,0:T(8,128)}), f32[16,3,8,128]{3,2,1,0:T(8,128)S(1)}, u32[]{:S(2)}, u32[]{:S(2)}) async-start(f32[16,3,8,128]{3,2,1,0:T(8,128)} %broadcast_in_dim.11), calls=%async_computation.2 | async-start | bytes 393216 | tf_op jit(solution)/shard_map/all_to_all | solution.py:269
  59.9 10.6 %copy-start.4 = (bf16[256,2560]{1,0:T(8,128)(2,1)S(1)}, bf16[256,2560]{1,0:T(8,128)(2,1)}, u32[]{:S(2)}) copy-start(bf16[256,2560]{1,0:T(8,128)(2,1)} %x_ref.1) | copy-start | bytes 3932164
  67.9 9.6 %copy-start.2 = (bf16[256,2560]{1,0:T(8,128)(2,1)S(1)}, bf16[256,2560]{1,0:T(8,128)(2,1)}, u32[]{:S(2)}) copy-start(bf16[256,2560]{1,0:T(8,128)(2,1)} %c0.1) | copy-start | bytes 3932164
  67.9 9.6 %copy-start.7 = (s32[2]{0:T(128)S(1)}, s32[2]{0:T(128)}, u32[]{:S(2)}) copy-start(s32[2]{0:T(128)} %copy-done.6) | copy-start | bytes 28
  68.0 9.6 %collective-permute-start.4 = (f32[16,3,8,128]{3,2,1,0:T(8,128)S(1)}, f32[16,3,8,128]{3,2,1,0:T(8,128)S(1)}, u32[]{:S(2)}, u32[]{:S(2)}) collective-permute-start(f32[16,3,8,128]{3,2,1,0:T(8,128)S(1)} %all-to-all-done.2.mine_ref), channel_id=1, source_target_pairs={{0,1},{1,0},{2,3},{3,2},{4,5},{5,4},{6,7},{7,6},{8,9},{9,8},{10,11... | collective-permute-start | bytes 589832 | tf_op jit(solution)/shard_map/ppermute | solution.py:273
  71.6 29.3 %collective-permute-start.9 = (bf16[256,640]{1,0:T(8,128)(2,1)}, bf16[256,640]{1,0:T(8,128)(2,1)}, u32[]{:S(2)}, u32[]{:S(2)}) collective-permute-start(bf16[256,640]{1,0:T(8,128)(2,1)} %get-tuple-element.78), channel_id=1, source_target_pairs={{0,4},{1,5},{2,6},{3,7},{4,0},{5,1},{6,2},{7,3},{8,12},{9,13},{10,... | collective-permute-start | bytes 983048 | tf_op jit(solution)/shard_map/ppermute | solution.py:277
  74.8 28.7 %collective-permute-start.8 = (bf16[256,640]{1,0:T(8,128)(2,1)}, bf16[256,640]{1,0:T(8,128)(2,1)}, u32[]{:S(2)}, u32[]{:S(2)}) collective-permute-start(bf16[256,640]{1,0:T(8,128)(2,1)} %get-tuple-element.79), channel_id=1, source_target_pairs={{2,0},{7,1},{4,2},{1,3},{6,4},{3,5},{0,6},{5,7},{10,8},{15,9},{12,... | collective-permute-start | bytes 983048 | tf_op jit(solution)/shard_map/ppermute | solution.py:277
  75.1 28.5 %collective-permute-start.7 = (bf16[256,640]{1,0:T(8,128)(2,1)}, bf16[256,640]{1,0:T(8,128)(2,1)}, u32[]{:S(2)}, u32[]{:S(2)}) collective-permute-start(bf16[256,640]{1,0:T(8,128)(2,1)} %get-tuple-element.80), channel_id=1, source_target_pairs={{0,2},{1,7},{2,4},{3,1},{4,6},{5,3},{6,0},{7,5},{8,10},{9,15},{10,... | collective-permute-start | bytes 983048 | tf_op jit(solution)/shard_map/ppermute | solution.py:277
  77.5 32.7 %collective-permute-start.6 = (bf16[256,2560]{1,0:T(8,128)(2,1)}, bf16[256,2560]{1,0:T(8,128)(2,1)}, u32[]{:S(2)}, u32[]{:S(2)}) collective-permute-start(bf16[256,2560]{1,0:T(8,128)(2,1)} %collective-permute-done.2.refs_0_.c1), channel_id=1, source_target_pairs={{0,2},{1,7},{2,4},{3,1},{4,6},{5,3},{6,0},{7,5},{8,10},{9,15},{10,... | collective-permute-start | bytes 3932168 | tf_op jit(solution)/shard_map/ppermute | solution.py:277
  77.5 1.9 %copy-start.10 = (f32[320,2560]{1,0:T(8,128)S(1)}, f32[320,2560]{1,0:T(8,128)}, u32[]{:S(2)}) copy-start(f32[320,2560]{1,0:T(8,128)} %f_ref.3) | copy-start | bytes 9830404
  83.5 17.4 %copy-start.16 = (bf16[256,640]{1,0:T(8,128)(2,1)S(1)}, bf16[256,640]{1,0:T(8,128)(2,1)}, u32[]{:S(2)}) copy-start(bf16[256,640]{1,0:T(8,128)(2,1)} %get-tuple-element.63) | copy-start | bytes 983044
  90.4 1.5 collective-permute-start.5
  91.9 40.4 %collective-permute-start.10 = (bf16[256,640]{1,0:T(8,128)(2,1)}, bf16[256,640]{1,0:T(8,128)(2,1)S(1)}, u32[]{:S(2)}, u32[]{:S(2)}) collective-permute-start(bf16[256,640]{1,0:T(8,128)(2,1)} %get-tuple-element.62), channel_id=1, source_target_pairs={{2,0},{7,1},{4,2},{1,3},{6,4},{3,5},{0,6},{5,7},{10,8},{15,9},{12,... | collective-permute-start | bytes 983048 | tf_op jit(solution)/shard_map/ppermute | solution.py:277
  94.0 16.2 %all-to-all-start.3 = ((f32[16,3,8,128]{3,2,1,0:T(8,128)}), f32[16,3,8,128]{3,2,1,0:T(8,128)S(1)}, u32[]{:S(2)}, u32[]{:S(2)}) async-start(f32[16,3,8,128]{3,2,1,0:T(8,128)} %add.53), calls=%async_computation.3 | async-start | bytes 393216 | tf_op jit(solution)/shard_map/all_to_all | solution.py:269
  101.0 31.3 %collective-permute-start.11 = (bf16[256,640]{1,0:T(8,128)(2,1)S(1)}, bf16[256,640]{1,0:T(8,128)(2,1)S(1)}, u32[]{:S(2)}, u32[]{:S(2)}) collective-permute-start(bf16[256,640]{1,0:T(8,128)(2,1)S(1)} %copy-done.16), channel_id=1, source_target_pairs={{0,2},{1,7},{2,4},{3,1},{4,6},{5,3},{6,0},{7,5},{8,10},{9,15},{10,... | collective-permute-start | bytes 983048 | tf_op jit(solution)/shard_map/ppermute | solution.py:277
  110.8 21.4 %all-to-all-start.4 = ((f32[8,3,8,128]{3,2,1,0:T(8,128)}), f32[8,3,8,128]{3,2,1,0:T(8,128)S(1)}, u32[]{:S(2)}, u32[]{:S(2)}) async-start(f32[8,3,8,128]{3,2,1,0:T(8,128)} %broadcast_in_dim.12), calls=%async_computation.4 | async-start | bytes 196608 | tf_op jit(solution)/shard_map/all_to_all | solution.py:269
  132.2 0.7 copy-start.13
  132.2 0.8 copy-start.14
  132.3 15.4 %collective-permute-start.12 = (f32[320,2560]{1,0:T(8,128)}, f32[320,2560]{1,0:T(8,128)}, u32[]{:S(2)}, u32[]{:S(2)}) collective-permute-start(f32[320,2560]{1,0:T(8,128)} %get-tuple-element.67), channel_id=1, source_target_pairs={{0,1},{1,0},{2,3},{3,2},{4,5},{5,4},{6,7},{7,6},{8,9},{9,8},{10,11... | collective-permute-start | bytes 9830408 | tf_op jit(solution)/shard_map/ppermute | solution.py:273
  133.1 14.6 %collective-permute-start.13 = (bf16[256,640]{1,0:T(8,128)(2,1)}, bf16[256,640]{1,0:T(8,128)(2,1)}, u32[]{:S(2)}, u32[]{:S(2)}) collective-permute-start(bf16[256,640]{1,0:T(8,128)(2,1)} %shard_map.81), channel_id=1, source_target_pairs={{0,4},{1,5},{2,6},{3,7},{4,0},{5,1},{6,2},{7,3},{8,12},{9,13},{10,... | collective-permute-start | bytes 983048 | tf_op jit(solution)/shard_map/ppermute | solution.py:277
  135.7 17.1 %copy-start = (f32[320,2560]{1,0:T(8,128)S(1)}, f32[320,2560]{1,0:T(8,128)}, u32[]{:S(2)}) copy-start(f32[320,2560]{1,0:T(8,128)} %get-tuple-element.73.a_ref) | copy-start | bytes 9830404
  135.7 17.1 %copy-start.8 = (s32[2]{0:T(128)S(1)}, s32[2]{0:T(128)}, u32[]{:S(2)}) copy-start(s32[2]{0:T(128)} %copy-done.6) | copy-start | bytes 28
  147.6 5.1 %collective-permute-start.14 = (f32[16,3,8,128]{3,2,1,0:T(8,128)S(1)}, f32[16,3,8,128]{3,2,1,0:T(8,128)}, u32[]{:S(2)}, u32[]{:S(2)}) collective-permute-start(f32[16,3,8,128]{3,2,1,0:T(8,128)S(1)} %all_to_all.30.mine_ref), channel_id=1, source_target_pairs={{0,1},{1,0},{2,3},{3,2},{4,5},{5,4},{6,7},{7,6},{8,9},{9,8},{10,11... | collective-permute-start | bytes 589832 | tf_op jit(solution)/shard_map/ppermute | solution.py:273
  152.7 0.9 copy-start.5

commit v3 on v1

v3 whole, which is shorter than its diff:
```python
import functools

import jax
import jax.numpy as jnp
from jax import lax
from jax.experimental import pallas as pl
from jax.experimental.pallas import tpu as pltpu
from jax.sharding import Mesh, PartitionSpec as P

FSDP = ("y", "core")
ALL = ("z", "x", "y", "core")
BF16 = jnp.bfloat16
F32 = jnp.float32
VMEM = pl.BlockSpec(memory_space=pltpu.VMEM)
ANY = pl.BlockSpec(memory_space=pl.ANY)
SMEM = pl.BlockSpec(memory_space=pltpu.SMEM)
AHEAD = [(2 * y + c, 2 * ((y + 1 - 2 * c) % 4) + c) for y in range(4) for c in range(2)]
BACK = [(b, a) for a, b in AHEAD]
ACROSS = [(2 * y + c, 2 * ((y + 2) % 4) + c) for y in range(4) for c in range(2)]
HALF = (16, 3, 8, 128)


def mm(a, b, ca, cb):
    return lax.dot_general(a, b, (((ca,), (cb,)), ((), ())), preferred_element_type=F32)


def terms(v):
    a = v.astype(BF16)
    rest = v - a.astype(F32)
    b = rest.astype(BF16)
    return a, b, (rest - b.astype(F32)).astype(BF16)


def stacked(v):
    return jnp.concatenate(terms(v), axis=0)


def folded(v):
    return v[0:32] + v[32:64] + v[64:96]


def two_terms(v):
    return jnp.concatenate(terms(v)[:2], axis=0)


def put_window(place, feedback_ref, window_ref):
    core = place[0]
    zero = jnp.zeros((64, 2560), BF16)
    free = pl.multiple_of(320 * (1 - core), 64)
    first = pl.multiple_of(64 * core, 64)
    for i in range(5):
        rows = pl.ds(64 * i, 64)
        for t, term in enumerate(terms(feedback_ref[rows, :])[:2]):
            window_ref[t, pl.ds(pl.multiple_of(first + 64 * i, 64), 64), :] = term
    for t in range(2):
        window_ref[t, pl.ds(free, 64), :] = zero


class Copies:
    def __init__(self, sems):
        self.sems, self.made = sems, []

    def start(self, source, target):
        copy = pltpu.make_async_copy(source, target, self.sems.at[len(self.made)])
        copy.start()
        self.made.append(copy)
        return copy


def wait(copies):
    for copy in copies:
        copy.wait()


def emit(core, value, mine_ref, other_ref):
    for tile in range(48):
        if tile < 40:
            r, j = divmod(tile, 20)
            low = value[8 * r : 8 * r + 8, 128 * j : 128 * j + 128]
            high = value[16 + 8 * r : 24 + 8 * r, 128 * j : 128 * j + 128]
            mine, other = jnp.where(core == 0, low, high), jnp.where(core == 0, high, low)
        else:
            mine = other = jnp.zeros((8, 128), F32)
        mine_ref[tile // 3, tile % 3] = mine
        other_ref[tile // 3, tile % 3] = other


def collect(core, mine_ref, other_ref, whole_ref):
    for tile in range(40):
        r, j = divmod(tile, 20)
        mine, other = mine_ref[tile // 3, tile % 3], other_ref[tile // 3, tile % 3]
        lanes = pl.ds(128 * j, 128)
        whole_ref[pl.ds(8 * r, 8), lanes] = jnp.where(core == 0, mine, other)
        whole_ref[pl.ds(16 + 8 * r, 8), lanes] = jnp.where(core == 0, other, mine)


def left_kernel(
    place, x_any, c_any, s_ref, f_any, mine_ref, other_ref, sum_ref, x_ref, f_ref, c_ref, sems
):
    core, lane = place[0], pl.multiple_of(place[1], 128)
    copies = Copies(sems)

    def fetch(source, target, parts, rows):
        return [copies.start(source.at[pl.ds(rows * k, rows)], target.at[pl.ds(rows * k, rows)]) for k in parts]

    c_in = fetch(c_any, c_ref, range(4), 64)
    f_in = fetch(f_any, f_ref, range(10), 32)
    x_in = fetch(x_any, x_ref, range(4), 64)
    factors = jnp.concatenate(terms(s_ref[...].T), axis=1)
    wait(c_in)
    small = folded(mm(c_ref[...], factors, 1, 0).T)
    parts = []
    for k in range(2):
        wait(f_in[5 * k : 5 * k + 5])
        part = mm(two_terms(f_ref[pl.ds(160 * k, 160), :]), factors, 1, 0)
        parts.append(part[:160] + part[160:])
    own = folded(jnp.concatenate(parts, axis=0).T)
    zero = jnp.zeros((32, 64), F32)
    own = jnp.where(
        core == 0, jnp.concatenate([own, zero], axis=1), jnp.concatenate([zero, own], axis=1)
    )
    wait(x_in)
    sum_ref[...] = folded(mm(stacked(small), x_ref[...], 1, 0))
    sum_ref[:, pl.ds(lane, 384)] += own
    emit(core, sum_ref[...], mine_ref, other_ref)


def right_kernel(
    place, mine_ref, other_ref, x_ref, c_ref, f_any, out_ref, away_ref, gram_ref, own_ref,
    window_ref, left_ref, f_ref, sem,
):
    core, lane = place[0], pl.multiple_of(place[1], 128)
    f_in = pltpu.make_async_copy(f_any, f_ref, sem)
    f_in.start()
    collect(core, mine_ref, other_ref, left_ref)
    left = left_ref[...]
    p3 = stacked(left)
    small = folded(mm(p3, x_ref[...], 1, 1))
    total = folded(mm(stacked(small), c_ref[...], 1, 0))
    f_in.wait()
    put_window(place, f_ref, window_ref)
    own = left_ref[:, pl.ds(lane, 384)]
    own_ref[...] = own
    own3 = stacked(own)
    total += sum(folded(mm(own3, window_ref[t], 1, 0)) for t in range(2))
    emit(core, total, out_ref, away_ref)
    gram_ref[...] = sum(folded(mm(p3, p3[32 * t : 32 * t + 32], 1, 1)) for t in range(3))


def rows_kernel(place, *refs):
    xs, cs, f_any, mine_any, away_any = refs[:4], refs[4:8], refs[8], refs[9], refs[10]
    x_ref, turned, c_ref, f_ref, out_ref, sems = refs[11:]
    core, copies = place[0], Copies(sems)
    x_in = [copies.start(x, x_ref.at[pl.ds(256 * k, 256)]) for k, x in enumerate(xs)]
    parts = []
    for j in range(4):
        lanes = pl.ds(640 * j, 640)
        parts.append([copies.start(c.at[:, lanes], c_ref.at[pl.ds(256 * k, 256), lanes]) for k, c in enumerate(cs)])
    f_in = copies.start(f_any, f_ref)
    wait(x_in)
    first, second_ = pl.multiple_of(320 * core, 64), pl.multiple_of(320 * (1 - core), 64)
    for k in range(4):
        block = x_ref[pl.ds(256 * k, 256), :].T
        turned[pl.ds(first, 320), pl.ds(256 * k, 256)] = block[:320]
        turned[pl.ds(second_, 320), pl.ds(256 * k, 256)] = block[320:]
    sent = []
    for j in range(4):
        lanes = pl.ds(640 * j, 640)
        wait(parts[j])
        out_ref[1, :, lanes] = mm(turned[pl.ds(320, 320), :], c_ref[:, lanes], 1, 0)
        sent.append(copies.start(out_ref.at[1, :, lanes], away_any.at[:, lanes]))
    f_in.wait()
    for j in range(4):
        lanes = pl.ds(640 * j, 640)
        out_ref[0, :, lanes] = mm(turned[pl.ds(0, 320), :], c_ref[:, lanes], 1, 0) + f_ref[:, lanes]
        sent.append(copies.start(out_ref.at[0, :, lanes], mine_any.at[:, lanes]))
    wait(sent)


def gradient_rows(place, xs, cs, feedback):
    return pl.pallas_call(
        rows_kernel,
        in_specs=[SMEM] + [ANY] * 9,
        out_specs=[ANY] * 2,
        out_shape=[jax.ShapeDtypeStruct((320, 2560), F32)] * 2,
        scratch_shapes=[pltpu.VMEM((1024, 640), BF16), pltpu.VMEM((640, 1024), BF16),
                        pltpu.VMEM((1024, 2560), BF16), pltpu.VMEM((320, 2560), F32),
                        pltpu.VMEM((2, 320, 2560), F32), pltpu.SemaphoreType.DMA((32,))],
        compiler_params=pltpu.CompilerParams(vmem_limit_bytes=119 << 19),
        cost_estimate=pl.CostEstimate(flops=34 * 10**8, bytes_accessed=17 << 20, transcendentals=0),
    )(place, *xs, *cs, feedback)


def place_kernel(place, g0, g1, g2, g3, out_ref):
    for k, g in enumerate((g0, g1, g2, g3)):
        out_ref[:, pl.ds(pl.multiple_of(640 * place[2 + k], 128), 640)] = g[...]


def placed_columns(place, blocks):
    return pl.pallas_call(
        place_kernel,
        in_specs=[SMEM] + [VMEM] * 4,
        out_specs=VMEM,
        out_shape=jax.ShapeDtypeStruct((256, 2560), BF16),
        cost_estimate=pl.CostEstimate(flops=0, bytes_accessed=3 << 20, transcendentals=0),
    )(place, *blocks)


def last_kernel(
    place, mine_ref, other_ref, inverse_ref, ortho_ref, grown_ref, new_any, q_ref,
    right_ref, lhs_ref, rhs_ref, new_ref, sems,
):
    copies = Copies(sems)
    collect(place[0], mine_ref, other_ref, right_ref)
    i1, i2, i3 = terms(inverse_ref[...])
    r1, r2, r3 = terms(right_ref[...])
    q = sum(mm(a, b, 1, 0) for a, b in ((i1, r1), (i1, r2), (i2, r1), (i2, r2), (i1, r3), (i3, r1)))
    q = q / 32
    q_ref[...] = q
    q1, q2, q3 = terms(q)
    o1, o2, o3 = terms(ortho_ref[...].T)
    for k, (o, q) in enumerate(((o1, q1), (o1, q2), (o2, q1), (o2, q2), (o1, q3), (o3, q1))):
        lhs_ref[:, pl.ds(32 * k, 32)] = o
        rhs_ref[pl.ds(32 * k, 32), :] = q
    for k in range(5):
        rows = pl.ds(64 * k, 64)
        lhs = lhs_ref[pl.ds(pl.multiple_of(64 * place[0] + 64 * k, 64), 64), :]
        new_ref[rows, :] = grown_ref[rows, :] - mm(lhs, rhs_ref[...], 1, 0)
        copies.start(new_ref.at[rows], new_any.at[rows])
    wait(copies.made)


def call(kernel, ins, outs, scratch, flops, size, limit=80):
    return pl.pallas_call(
        kernel,
        in_specs=[SMEM] + ins,
        out_specs=[VMEM] * len(outs),
        out_shape=[jax.ShapeDtypeStruct(s, F32) for s in outs],
        scratch_shapes=scratch,
        compiler_params=pltpu.CompilerParams(vmem_limit_bytes=limit << 19),
        cost_estimate=pl.CostEstimate(flops=flops, bytes_accessed=size, transcendentals=0),
    )


def left_product(place, x, c, s, f):
    return call(
        left_kernel, [ANY, ANY, VMEM, ANY], [HALF, HALF],
        [pltpu.VMEM((32, 2560), F32), pltpu.VMEM((256, 2560), BF16),
         pltpu.VMEM((320, 2560), F32), pltpu.VMEM((256, 2560), BF16),
         pltpu.SemaphoreType.DMA((18,))],
        2 * 10**9, 7 << 20, 119,
    )(place, x, c, s, f)


def right_product(place, mine, other, x, c, f):
    return call(
        right_kernel, [VMEM] * 4 + [ANY], [HALF, HALF, (32, 32), (32, 384)],
        [pltpu.VMEM((2, 384, 2560), BF16), pltpu.VMEM((32, 2560), F32),
         pltpu.VMEM((320, 2560), F32), pltpu.SemaphoreType.DMA],
        2 * 10**9, 7 << 20, 115,
    )(place, mine, other, x, c, f)


def factor_kernel(gram_ref, own_ref, inverse_ref, ortho_ref):
    row = lax.broadcasted_iota(jnp.int32, (32, 128), 0)
    lane = lax.broadcasted_iota(jnp.int32, (32, 128), 1)
    a = jnp.concatenate([gram_ref[...], jnp.zeros((32, 96), F32)], axis=1)
    a = jnp.where(lane == row + 32, 1.0, a)
    for j in range(32):
        pivot = a[j : j + 1, :]
        scaled = pivot / jnp.sqrt(a[j : j + 1, j : j + 1])
        column = a[:, j : j + 1] / a[j : j + 1, j : j + 1]
        a = jnp.where(row == j, scaled, jnp.where(row > j, a - column * pivot, a))
    inverse = a[:, 32:64]
    inverse_ref[...] = inverse
    i1, i2, i3 = terms(inverse)
    o1, o2, o3 = terms(own_ref[...])
    pairs = ((i1, o1), (i1, o2), (i2, o1), (i2, o2), (i1, o3), (i3, o1))
    ortho_ref[...] = sum(mm(a, b, 1, 0) for a, b in pairs)


def factor(gram, own):
    return pl.pallas_call(
        factor_kernel,
        in_specs=[VMEM] * 2,
        out_specs=[VMEM] * 2,
        out_shape=[jax.ShapeDtypeStruct((32, 32), F32), jax.ShapeDtypeStruct((32, 384), F32)],
        cost_estimate=pl.CostEstimate(flops=10**7, bytes_accessed=1 << 20, transcendentals=32),
    )(gram, own)


def last_step(place, mine, other, inverse, ortho, grown):
    return pl.pallas_call(
        last_kernel,
        in_specs=[SMEM] + [VMEM] * 5,
        out_specs=[ANY, VMEM],
        out_shape=[jax.ShapeDtypeStruct((320, 2560), F32), jax.ShapeDtypeStruct((32, 2560), F32)],
        scratch_shapes=[pltpu.VMEM((32, 2560), F32), pltpu.VMEM((384, 192), BF16),
                        pltpu.VMEM((192, 2560), BF16), pltpu.VMEM((320, 2560), F32),
                        pltpu.SemaphoreType.DMA((5,))],
        compiler_params=pltpu.CompilerParams(vmem_limit_bytes=24 << 20),
        cost_estimate=pl.CostEstimate(flops=3 * 10**8, bytes_accessed=8 << 20, transcendentals=0),
    )(place, mine, other, inverse, ortho, grown)


def exchange(u, axes):
    return lax.all_to_all(u, axes, 0, 0, tiled=True)


def swap(v):
    return lax.ppermute(v, "core", [(0, 1), (1, 0)])


def send(v, pairs):
    return lax.ppermute(v, FSDP, pairs)


def tie(*values):
    return lax.optimization_barrier(values)


def repeated(v, n):
    return jnp.broadcast_to(v.sum(0)[None], (n, 3, 8, 128))


def shards(features, cotangent, weight, feedback, start_factors):
    core, y = lax.axis_index("core"), lax.axis_index("y")
    ahead, back = lax.rem(y + 5 - 2 * core, 4), lax.rem(y + 3 + 2 * core, 4)
    across = lax.rem(y + 2, 4)
    place = jnp.stack([core, 128 * (5 * y + 2 * core), y, ahead, back, across]).astype(jnp.int32)

    def columns(chip, x):
        return lax.dynamic_slice(x, (0, 640 * chip), (256, 640))

    c1, c2 = send(cotangent, AHEAD), send(cotangent, BACK)
    swapped = swap(weight)
    mine, other = left_product(place, features, cotangent, start_factors.T, feedback)

    half, later = tie(mine + swap(other), features)
    half = exchange(half, ("x", "y"))
    x0, x1, x2, x3 = (columns(chip, later) for chip in (y, ahead, back, across))
    weights = jnp.where(
        core == 0, jnp.concatenate([weight, swapped]), jnp.concatenate([swapped, weight])
    )

    def back_columns(c):
        return mm(c, weights, 1, 1).astype(BF16)

    half, weights, x0, x1, x2, x3 = tie(half, weights, x0, x1, x2, x3)
    half, x1, x2, x3 = tie(repeated(half, 8), x1, x2, x3)
    half = exchange(half, "z")
    x1, x2, x3 = send(x1, AHEAD), send(x2, BACK), send(x3, ACROSS)
    g0 = back_columns(cotangent)
    half, g0, c1, c2 = tie(half, g0, c1, c2)
    half, c1, c2 = tie(repeated(half, 16), c1, c2)
    half = exchange(half, ("x", "y"))
    c3 = send(c1, AHEAD)
    g1, g2 = back_columns(c1), back_columns(c2)
    half, g1, g2, x1, x2, x3 = tie(half, g1, g2, x1, x2, x3)

    mine, other, gram, own = right_product(place, half, swap(half), features, cotangent, feedback)
    half, gram, own, g1, g2 = tie(mine + swap(other), gram, own, g1, g2)
    half = exchange(half, ("x", "y"))
    u1, u2 = send(g1, BACK), send(g2, AHEAD)
    inverse, ortho = factor(gram, own)
    inverse, ortho, c3 = tie(inverse, ortho, c3)
    g3 = back_columns(c3)
    half, ortho, inverse, g3 = tie(half, ortho, inverse, g3)
    half, c3, g3, x1, x2, x3 = tie(repeated(half, 8), c3, g3, x1, x2, x3)
    half = exchange(half, "z")
    u3 = send(g3, ACROSS)
    grown, away = gradient_rows(place, (x0, x1, x2, x3), (cotangent, c1, c2, c3), feedback)
    half, u1, u2, grown, away = tie(half, u1, u2, grown, away)
    half, grown, away = tie(repeated(half, 16), grown, away)
    half = exchange(half, ("x", "y"))
    grown = grown + swap(away)
    input_grad = placed_columns(place, (g0, u1, u2, u3))
    half, grown, input_grad = tie(half, grown, input_grad)

    new_feedback, q_factor = last_step(place, half, swap(half), inverse, ortho, grown)
    return (input_grad, new_feedback, q_factor.T)


def solution(mesh):
    split = Mesh(mesh.devices.reshape(8, 4, 4, 2), ALL)
    placed = (P(ALL, None), P(ALL, None), P(FSDP, None), P(ALL, None), P())
    return jax.shard_map(
        shards,
        mesh=split,
        in_specs=placed,
        out_specs=(P(ALL, None), P(ALL, None), P()),
        check_vma=False,
    )
```

time: 180 us -> 144 us (0.80)
  blocking collectives: 58.4 us -> 0 us
  starting transfers between devices: 23.6 us -> 57.7 us
  Pallas kernels: 0 us -> 33.2 us
  matrix products: 35.5 us -> 13.1 us
  between operations: 14.3 us -> 1 us
  local copies, waits for them, and re-layouts: 12.4 us -> 5.87 us
  waiting for transfers between devices: 24.1 us -> 21.2 us
    all_to_all x5 -> x0, blocking collectives: 58.4 us -> none  [exchange(): return lax.all_to_all(u, axes, 0, 0, tiled=True)]
    pallas_call x0 -> x6, Pallas kernels: none -> 33.2 us  [the longest x1 9.33 us: gradient_rows(): pl.pallas_call(rows_kernel, in_specs=[SMEM] + [ANY] * 9, out_specs=[ANY]...]
    dot_general x12 -> x4, matrix products: 35.3 us -> 13.1 us  [mm(): lax.dot_general(a, b, (((ca,), (cb,)), ((), ())), preferred_element_type=...]
    all_to_all x3 -> x6, starting transfers between devices: 15.4 us -> 37.5 us  [exchange(): return lax.all_to_all(u, axes, 0, 0, tiled=True)]
    ppermute x4 -> x15, starting transfers between devices: 8.19 us -> 20.2 us  [the longest x9 14.3 us: send(): return lax.ppermute(v, FSDP, pairs)]
    all_to_all x3 -> x6, waiting for transfers between devices: 20 us -> 10.2 us  [exchange(): return lax.all_to_all(u, axes, 0, 0, tiled=True)]
    ppermute x4 -> x15, waiting for transfers between devices: 3.35 us -> 11 us  [the longest x6 5.51 us: swap(): return lax.ppermute(v, 'core', [(0, 1), (1, 0)])]
    another operation x5 -> x0, other arithmetic: 6.68 us -> none  [the longest x3 3.6 us: shards(): lower = jnp.linalg.cholesky(gram)]
  transfers between devices with their start and end apart: 8 -> 21, of which waited for: 6 -> 9; matrix products, arithmetic and copies ran while one was open for 26% -> 19% of each run, Pallas kernels for 0% -> 21%
where the time goes in v3:
time: 144 us; the launch traced here: 142 us
  starting transfers between devices  57.7 us (40%)
  Pallas kernels  33.2 us (23%)
  waiting for transfers between devices  21.2 us (15%)
  matrix products  13.1 us (9%)
  other arithmetic  10 us (7%)
  local copies, waits for them, and re-layouts  5.87 us (4%)
    all_to_all x6, starting transfers between devices, exchange(): return lax.all_to_all(u, axes, 0, 0, tiled=True)  37.5 us
    ppermute x9, starting transfers between devices, send(): return lax.ppermute(v, FSDP, pairs)  14.3 us
    dot_general x4, matrix products, mm(): lax.dot_general(a, b, (((ca,), (cb,)), ((), ())), preferred_element_type=...  13.1 us
    all_to_all x6, waiting for transfers between devices, exchange(): return lax.all_to_all(u, axes, 0, 0, tiled=True)  10.2 us
    pallas_call x1, Pallas kernels, gradient_rows(): pl.pallas_call(rows_kernel, in_specs=[SMEM] + [ANY] * 9, out_specs=[ANY]...  9.33 us
    pallas_call x1, Pallas kernels, right_product(): call(right_kernel, [VMEM] * 4 + [ANY], [HALF, HALF, (32, 32), (32, 384)],...  6.69 us
    pallas_call x1, Pallas kernels, left_product(): call(left_kernel, [ANY, ANY, VMEM, ANY], [HALF, HALF], [pltpu.VMEM((32, 2...  6.42 us
    ppermute x6, starting transfers between devices, swap(): return lax.ppermute(v, 'core', [(0, 1), (1, 0)])  5.97 us
  transfers between devices with their start and end apart: 21, of which 9 were waited for; matrix products, arithmetic and copies ran while one was open for 19% of the time, Pallas kernels for 21%

profile of v3, /device:TPU:1, one launch (start us, length us, event | category | flops | bytes accessed | tf_op | source)
XLA Modules:
  0.0 142.1 jit_solution(4355241511425326322)
XLA Ops:
  0.6 3.3 %collective-permute-start.1 = (bf16[320,2560]{1,0:T(8,128)(2,1)}, bf16[320,2560]{1,0:T(8,128)(2,1)}, u32[]{:S(2)}, u32[]{:S(2)}) collective-permute-start(bf16[320,2560]{1,0:T(8,128)(2,1)} %param.7), channel_id=1, source_target_pairs={{0,1},{1,0},{2,3},{3,2},{4,5},{5,4},{6,7},{7,6},{8,9},{9,8},{10,11... | collective-permute-start | bytes 4915208 | tf_op jit(solution)/shard_map/ppermute | solution.py:311
  4.0 2.7 %collective-permute-start.2 = (bf16[256,2560]{1,0:T(8,128)(2,1)}, bf16[256,2560]{1,0:T(8,128)(2,1)}, u32[]{:S(2)}, u32[]{:S(2)}) collective-permute-start(bf16[256,2560]{1,0:T(8,128)(2,1)} %refs_4_.1), channel_id=1, source_target_pairs={{0,2},{1,7},{2,4},{3,1},{4,6},{5,3},{6,0},{7,5},{8,10},{9,15},{10,... | collective-permute-start | bytes 3932168 | tf_op jit(solution)/shard_map/ppermute | solution.py:315
  6.6 0.7 stack.27.place
  7.3 6.4 %shard_map.76 = (f32[16,3,8,128]{3,2,1,0:T(8,128)}, f32[16,3,8,128]{3,2,1,0:T(8,128)}) custom-call(s32[6]{0:T(128)} %stack.27.place, bf16[256,2560]{1,0:T(8,128)(2,1)} %x_ref.1, bf16[256,2560]{1,0:T(8,128)(2,1)} %refs_4_.1, f32[32,2560]{1,0:T(8,128)} %bitcast.18, f32[320,2560]{1,0:T(8,128)} %refs_8_.1), custom_call_target="tpu_custom_call" | custom-call | flops 2000000000 | bytes 7340032 | tf_op jit(solution)/shard_map/pallas_call | solution.py:246
  13.9 1.6 %collective-permute-done = f32[16,3,8,128]{3,2,1,0:T(8,128)S(1)} collective-permute-done((f32[16,3,8,128]{3,2,1,0:T(8,128)}, f32[16,3,8,128]{3,2,1,0:T(8,128)S(1)}, u32[]{:S(2)}, u32[]{:S(2)}) %collective-permute-start) | collective-permute-done | bytes 196640 | tf_op jit(solution)/shard_map/ppermute | solution.py:311
  15.5 1.6 %add.41 = f32[16,3,8,128]{3,2,1,0:T(8,128)} add(f32[16,3,8,128]{3,2,1,0:T(8,128)} %get-tuple-element.69, f32[16,3,8,128]{3,2,1,0:T(8,128)S(1)} %collective-permute-done) | non-fusion elementwise | flops 49152 | bytes 589824 | tf_op jit(solution)/shard_map/add | solution.py:339
  17.1 5.1 %all-to-all-start = ((f32[16,3,8,128]{3,2,1,0:T(8,128)}), f32[16,3,8,128]{3,2,1,0:T(8,128)S(1)}, u32[]{:S(2)}, u32[]{:S(2)}) async-start(f32[16,3,8,128]{3,2,1,0:T(8,128)} %add.41), calls=%async_computation | async-start | bytes 393216 | tf_op jit(solution)/shard_map/all_to_all | solution.py:307
  22.2 1.1 constant_dynamic-slice_fusion
  23.3 3.3 %maximum_select_fusion = bf16[640,2560]{1,0:T(8,128)(2,1)S(1)} fusion(bf16[320,2560]{1,0:T(8,128)(2,1)} %collective-permute-done.1, bf16[320,2560]{1,0:T(8,128)(2,1)} %param.7, pred[]{:T(512)S(6)} %eq.3), kind=kLoop, calls=%fused_computation | loop fusion | flops 14745600 | bytes 6553601 | tf_op jit(solution)/shard_map/jit(_where)/select_n | solution.py:342
  26.7 9.8 %all-to-all-done = f32[16,3,8,128]{3,2,1,0:T(8,128)S(1)} async-done(((f32[16,3,8,128]{3,2,1,0:T(8,128)}), f32[16,3,8,128]{3,2,1,0:T(8,128)S(1)}, u32[]{:S(2)}, u32[]{:S(2)}) %all-to-all-start) | async-done | bytes 196640 | tf_op jit(solution)/shard_map/all_to_all | solution.py:307
  36.5 0.6 broadcast_in_dim.8
  37.1 7.6 %all-to-all-start.1 = ((f32[8,3,8,128]{3,2,1,0:T(8,128)}), f32[8,3,8,128]{3,2,1,0:T(8,128)S(1)}, u32[]{:S(2)}, u32[]{:S(2)}) async-start(f32[8,3,8,128]{3,2,1,0:T(8,128)} %broadcast_in_dim.8), calls=%async_computation.1 | async-start | bytes 196608 | tf_op jit(solution)/shard_map/all_to_all | solution.py:307
  44.8 3.3 %fusion.g0 = bf16[256,640]{1,0:T(8,128)(2,1)} fusion(bf16[640,2560]{1,0:T(8,128)(2,1)S(1)} %maximum_select_fusion, bf16[256,2560]{1,0:T(8,128)(2,1)} %refs_4_.1), kind=kOutput, calls=%fused_computation.5 | convolution fusion | flops 839024640 | bytes 4915200 | tf_op jit(solution)/shard_map/dot_general | solution.py:24
  48.0 3.0 %collective-permute-start.4 = (bf16[256,640]{1,0:T(8,128)(2,1)}, bf16[256,640]{1,0:T(8,128)(2,1)}, u32[]{:S(2)}, u32[]{:S(2)}) collective-permute-start(bf16[256,640]{1,0:T(8,128)(2,1)} %get-tuple-element.85), channel_id=1, source_target_pairs={{0,2},{1,7},{2,4},{3,1},{4,6},{5,3},{6,0},{7,5},{8,10},{9,15},{10,... | collective-permute-start | bytes 983048 | tf_op jit(solution)/shard_map/ppermute | solution.py:315
  51.0 1.2 collective-permute-start.6
  52.3 0.7 broadcast_in_dim.9
  53.0 7.0 %all-to-all-start.2 = ((f32[16,3,8,128]{3,2,1,0:T(8,128)}), f32[16,3,8,128]{3,2,1,0:T(8,128)S(1)}, u32[]{:S(2)}, u32[]{:S(2)}) async-start(f32[16,3,8,128]{3,2,1,0:T(8,128)} %broadcast_in_dim.9), calls=%async_computation.2 | async-start | bytes 393216 | tf_op jit(solution)/shard_map/all_to_all | solution.py:307
  60.0 2.6 %collective-permute-start.9 = (bf16[256,2560]{1,0:T(8,128)(2,1)}, bf16[256,2560]{1,0:T(8,128)(2,1)}, u32[]{:S(2)}, u32[]{:S(2)}) collective-permute-start(bf16[256,2560]{1,0:T(8,128)(2,1)} %collective-permute-done.2.refs_5_), channel_id=1, source_target_pairs={{0,2},{1,7},{2,4},{3,1},{4,6},{5,3},{6,0},{7,5},{8,10},{9,15},{10,... | collective-permute-start | bytes 3932168 | tf_op jit(solution)/shard_map/ppermute | solution.py:315
  62.6 3.3 %convolution_convert_fusion.2 = bf16[256,640]{1,0:T(8,128)(2,1)} fusion(bf16[256,2560]{1,0:T(8,128)(2,1)} %collective-permute-done.2.refs_5_, bf16[640,2560]{1,0:T(8,128)(2,1)S(1)} %maximum_select_fusion), kind=kOutput, calls=%fused_computation.3 | convolution fusion | flops 839024640 | bytes 4915200 | tf_op jit(solution)/shard_map/dot_general | solution.py:24
  65.9 3.3 %convolution_convert_fusion.1 = bf16[256,640]{1,0:T(8,128)(2,1)} fusion(bf16[256,2560]{1,0:T(8,128)(2,1)} %collective-permute-done.3.refs_6_, bf16[640,2560]{1,0:T(8,128)(2,1)S(1)} %maximum_select_fusion), kind=kOutput, calls=%fused_computation.2 | convolution fusion | flops 839024640 | bytes 4915200 | tf_op jit(solution)/shard_map/dot_general | solution.py:24
  69.2 2.0 %collective-permute-done.5.refs_2_ = bf16[256,640]{1,0:T(8,128)(2,1)} collective-permute-done((bf16[256,640]{1,0:T(8,128)(2,1)}, bf16[256,640]{1,0:T(8,128)(2,1)}, u32[]{:S(2)}, u32[]{:S(2)}) %collective-permute-start.5) | collective-permute-done | bytes 327712 | tf_op jit(solution)/shard_map/ppermute | solution.py:315
  71.2 0.3 all-to-all-done.2.mine_ref
  71.4 0.1 collective-permute-start.7
  71.6 1.3 collective-permute-done.7.other_ref
  72.9 0.7 copy-done.7
  73.6 6.7 %shard_map.77 = (f32[16,3,8,128]{3,2,1,0:T(8,128)}, f32[16,3,8,128]{3,2,1,0:T(8,128)}, f32[32,32]{1,0:T(8,128)}, f32[32,384]{1,0:T(8,128)}) custom-call(s32[6]{0:T(128)} %stack.27.place, f32[16,3,8,128]{3,2,1,0:T(8,128)} %copy-done.5, f32[16,3,8,128]{3,2,1,0:T(8,128)} %copy-done.7, bf16[256,2560]{1,0:T(8,128)(2,1)} %x_ref.1, bf16[256,2560]{1,0:T(8,128)(2,1)} %refs_4_.1, ...), custom_call_target="tpu_custom_call" | custom-call | flops 2000000000 | bytes 7340032 | tf_op jit(solution)/shard_map/pallas_call | solution.py:256
  80.3 0.2 collective-permute-start.8
  80.5 1.5 %collective-permute-done.8 = f32[16,3,8,128]{3,2,1,0:T(8,128)S(1)} collective-permute-done((f32[16,3,8,128]{3,2,1,0:T(8,128)}, f32[16,3,8,128]{3,2,1,0:T(8,128)S(1)}, u32[]{:S(2)}, u32[]{:S(2)}) %collective-permute-start.8) | collective-permute-done | bytes 196640 | tf_op jit(solution)/shard_map/ppermute | solution.py:311
  82.0 1.6 %add.46 = f32[16,3,8,128]{3,2,1,0:T(8,128)} add(f32[16,3,8,128]{3,2,1,0:T(8,128)} %get-tuple-element.89, f32[16,3,8,128]{3,2,1,0:T(8,128)S(1)} %collective-permute-done.8) | non-fusion elementwise | flops 49152 | bytes 589824 | tf_op jit(solution)/shard_map/add | solution.py:362
  83.6 5.6 %all-to-all-start.3 = ((f32[16,3,8,128]{3,2,1,0:T(8,128)}), f32[16,3,8,128]{3,2,1,0:T(8,128)S(1)}, u32[]{:S(2)}, u32[]{:S(2)}) async-start(f32[16,3,8,128]{3,2,1,0:T(8,128)} %add.46), calls=%async_computation.3 | async-start | bytes 393216 | tf_op jit(solution)/shard_map/all_to_all | solution.py:307
  89.2 1.4 collective-permute-start.10
  90.6 1.4 collective-permute-start.11
  92.0 4.5 %shard_map.78 = (f32[32,32]{1,0:T(8,128)}, f32[32,384]{1,0:T(8,128)}) custom-call(f32[32,32]{1,0:T(8,128)} %get-tuple-element.96.gram_ref, f32[32,384]{1,0:T(8,128)} %get-tuple-element.97.own_ref), custom_call_target="tpu_custom_call" | custom-call | flops 10000000 | bytes 1048576 | tf_op jit(solution)/shard_map/pallas_call | solution.py:283
  96.5 3.3 %convolution_convert_fusion = bf16[256,640]{1,0:T(8,128)(2,1)} fusion(bf16[256,2560]{1,0:T(8,128)(2,1)} %collective-permute-done.9.refs_7_, bf16[640,2560]{1,0:T(8,128)(2,1)S(1)} %maximum_select_fusion), kind=kOutput, calls=%fused_computation.1 | convolution fusion | flops 839024640 | bytes 4915200 | tf_op jit(solution)/shard_map/dot_general | solution.py:24
  99.8 0.6 broadcast_in_dim.10
  100.4 6.9 %all-to-all-start.4 = ((f32[8,3,8,128]{3,2,1,0:T(8,128)}), f32[8,3,8,128]{3,2,1,0:T(8,128)S(1)}, u32[]{:S(2)}, u32[]{:S(2)}) async-start(f32[8,3,8,128]{3,2,1,0:T(8,128)} %broadcast_in_dim.10), calls=%async_computation.4 | async-start | bytes 196608 | tf_op jit(solution)/shard_map/all_to_all | solution.py:307
  107.3 9.3 %shard_map.79 = (f32[320,2560]{1,0:T(8,128)}, f32[320,2560]{1,0:T(8,128)}) custom-call(s32[6]{0:T(128)} %stack.27.place, bf16[256,640]{1,0:T(8,128)(2,1)} %get-tuple-element.111.refs_0_, bf16[256,640]{1,0:T(8,128)(2,1)} %collective-permute-done.4.refs_1_, bf16[256,640]{1,0:T(8,128)(2,1)} %collective-permute-done.5.refs_2_, ...), custom_call_target="tpu_custom_call" | custom-call | flops 3400000000 | bytes 17825792 | tf_op jit(solution)/shard_map/pallas_call | solution.py:181
  116.7 0.7 broadcast_in_dim.11
  117.4 1.3 collective-permute-start.12
  118.7 2.0 %collective-permute-start.13 = (bf16[256,640]{1,0:T(8,128)(2,1)S(1)}, bf16[256,640]{1,0:T(8,128)(2,1)S(1)}, u32[]{:S(2)}, u32[]{:S(2)}) collective-permute-start(bf16[256,640]{1,0:T(8,128)(2,1)S(1)} %copy-done.6), channel_id=1, source_target_pairs={{0,4},{1,5},{2,6},{3,7},{4,0},{5,1},{6,2},{7,3},{8,12},{9,13},{10,... | collective-permute-start | bytes 983048 | tf_op jit(solution)/shard_map/ppermute | solution.py:315
  120.8 5.3 %all-to-all-start.5 = ((f32[16,3,8,128]{3,2,1,0:T(8,128)}), f32[16,3,8,128]{3,2,1,0:T(8,128)S(1)}, u32[]{:S(2)}, u32[]{:S(2)}) async-start(f32[16,3,8,128]{3,2,1,0:T(8,128)} %broadcast_in_dim.11), calls=%async_computation.5 | async-start | bytes 393216 | tf_op jit(solution)/shard_map/all_to_all | solution.py:307
  126.1 3.5 %collective-permute-done.13.g3 = bf16[256,640]{1,0:T(8,128)(2,1)S(1)} collective-permute-done((bf16[256,640]{1,0:T(8,128)(2,1)S(1)}, bf16[256,640]{1,0:T(8,128)(2,1)S(1)}, u32[]{:S(2)}, u32[]{:S(2)}) %collective-permute-start.13) | collective-permute-done | bytes 327712 | tf_op jit(solution)/shard_map/ppermute | solution.py:315
  129.6 0.7 copy-done.4
  130.3 2.4 %shard_map.80 = bf16[256,2560]{1,0:T(8,128)(2,1)} custom-call(s32[6]{0:T(128)} %stack.27.place, bf16[256,640]{1,0:T(8,128)(2,1)} %fusion.g0, bf16[256,640]{1,0:T(8,128)(2,1)} %collective-permute-done.10.g1, bf16[256,640]{1,0:T(8,128)(2,1)} %collective-permute-done.11.g2, bf16[256,640]{1,0:T(8,128)(2,1)} %copy-done.4), custom_call_target="tpu_custom_call" | custom-call | bytes 3145728 | tf_op jit(solution)/shard_map/pallas_call | solution.py:200
  132.8 3.4 %add.47.grown_ref = f32[320,2560]{1,0:T(8,128)S(1)} add(f32[320,2560]{1,0:T(8,128)} %get-tuple-element.122, f32[320,2560]{1,0:T(8,128)} %collective-permute-done.12) | non-fusion elementwise | flops 819200 | bytes 9830400 | tf_op jit(solution)/shard_map/add | solution.py:376
  136.2 0.9 collective-permute-start.14
  137.1 1.1 collective-permute-done.14.other_ref
  138.1 3.8 %shard_map.81 = (f32[320,2560]{1,0:T(8,128)}, f32[32,2560]{1,0:T(8,128)}) custom-call(s32[6]{0:T(128)S(1)} %copy-done.2, f32[16,3,8,128]{3,2,1,0:T(8,128)S(1)} %all-to-all-done.5.mine_ref, f32[16,3,8,128]{3,2,1,0:T(8,128)S(1)} %collective-permute-done.14.other_ref, f32[32,32]{1,0:T(8,128)S(1)} %copy-done.1, f32[32,384]{1,0:T(8,128)S(1)} %copy-done, ...), custom_call_target="tpu_custom_call" | custom-call | flops 300000000 | bytes 8388608 | tf_op jit(solution)/shard_map/pallas_call | solution.py:293
  (34 shorter events, 0.3 us)
Async XLA Ops:
  0.6 22.7 %collective-permute-start.1 = (bf16[320,2560]{1,0:T(8,128)(2,1)}, bf16[320,2560]{1,0:T(8,128)(2,1)}, u32[]{:S(2)}, u32[]{:S(2)}) collective-permute-start(bf16[320,2560]{1,0:T(8,128)(2,1)} %param.7), channel_id=1, source_target_pairs={{0,1},{1,0},{2,3},{3,2},{4,5},{5,4},{6,7},{7,6},{8,9},{9,8},{10,11... | collective-permute-start | bytes 4915208 | tf_op jit(solution)/shard_map/ppermute | solution.py:311
  4.0 48.3 %collective-permute-start.3 = (bf16[256,2560]{1,0:T(8,128)(2,1)}, bf16[256,2560]{1,0:T(8,128)(2,1)}, u32[]{:S(2)}, u32[]{:S(2)}) collective-permute-start(bf16[256,2560]{1,0:T(8,128)(2,1)} %refs_4_.1), channel_id=1, source_target_pairs={{2,0},{7,1},{4,2},{1,3},{6,4},{3,5},{0,6},{5,7},{10,8},{15,9},{12,... | collective-permute-start | bytes 3932168 | tf_op jit(solution)/shard_map/ppermute | solution.py:315
  4.0 48.3 %collective-permute-start.2 = (bf16[256,2560]{1,0:T(8,128)(2,1)}, bf16[256,2560]{1,0:T(8,128)(2,1)}, u32[]{:S(2)}, u32[]{:S(2)}) collective-permute-start(bf16[256,2560]{1,0:T(8,128)(2,1)} %refs_4_.1), channel_id=1, source_target_pairs={{0,2},{1,7},{2,4},{3,1},{4,6},{5,3},{6,0},{7,5},{8,10},{9,15},{10,... | collective-permute-start | bytes 3932168 | tf_op jit(solution)/shard_map/ppermute | solution.py:315
  7.3 14.9 %copy-start.3 = (bf16[256,2560]{1,0:T(8,128)(2,1)S(1)}, bf16[256,2560]{1,0:T(8,128)(2,1)}, u32[]{:S(2)}) copy-start(bf16[256,2560]{1,0:T(8,128)(2,1)} %x_ref.1) | copy-start | bytes 3932164
  13.7 1.7 %collective-permute-start = (f32[16,3,8,128]{3,2,1,0:T(8,128)}, f32[16,3,8,128]{3,2,1,0:T(8,128)S(1)}, u32[]{:S(2)}, u32[]{:S(2)}) collective-permute-start(f32[16,3,8,128]{3,2,1,0:T(8,128)} %get-tuple-element.70), channel_id=1, source_target_pairs={{0,1},{1,0},{2,3},{3,2},{4,5},{5,4},{6,7},{7,6},{8,9},{9,8},{10,11... | collective-permute-start | bytes 589832 | tf_op jit(solution)/shard_map/ppermute | solution.py:311
  17.1 19.4 %all-to-all-start = ((f32[16,3,8,128]{3,2,1,0:T(8,128)}), f32[16,3,8,128]{3,2,1,0:T(8,128)S(1)}, u32[]{:S(2)}, u32[]{:S(2)}) async-start(f32[16,3,8,128]{3,2,1,0:T(8,128)} %add.41), calls=%async_computation | async-start | bytes 393216 | tf_op jit(solution)/shard_map/all_to_all | solution.py:307
  37.1 15.2 %all-to-all-start.1 = ((f32[8,3,8,128]{3,2,1,0:T(8,128)}), f32[8,3,8,128]{3,2,1,0:T(8,128)S(1)}, u32[]{:S(2)}, u32[]{:S(2)}) async-start(f32[8,3,8,128]{3,2,1,0:T(8,128)} %broadcast_in_dim.8), calls=%async_computation.1 | async-start | bytes 196608 | tf_op jit(solution)/shard_map/all_to_all | solution.py:307
  48.0 21.2 %collective-permute-start.4 = (bf16[256,640]{1,0:T(8,128)(2,1)}, bf16[256,640]{1,0:T(8,128)(2,1)}, u32[]{:S(2)}, u32[]{:S(2)}) collective-permute-start(bf16[256,640]{1,0:T(8,128)(2,1)} %get-tuple-element.85), channel_id=1, source_target_pairs={{0,2},{1,7},{2,4},{3,1},{4,6},{5,3},{6,0},{7,5},{8,10},{9,15},{10,... | collective-permute-start | bytes 983048 | tf_op jit(solution)/shard_map/ppermute | solution.py:315
  51.0 20.1 %collective-permute-start.5 = (bf16[256,640]{1,0:T(8,128)(2,1)}, bf16[256,640]{1,0:T(8,128)(2,1)}, u32[]{:S(2)}, u32[]{:S(2)}) collective-permute-start(bf16[256,640]{1,0:T(8,128)(2,1)} %get-tuple-element.86), channel_id=1, source_target_pairs={{2,0},{7,1},{4,2},{1,3},{6,4},{3,5},{0,6},{5,7},{10,8},{15,9},{12,... | collective-permute-start | bytes 983048 | tf_op jit(solution)/shard_map/ppermute | solution.py:315
  51.0 20.1 %collective-permute-start.6 = (bf16[256,640]{1,0:T(8,128)(2,1)}, bf16[256,640]{1,0:T(8,128)(2,1)}, u32[]{:S(2)}, u32[]{:S(2)}) collective-permute-start(bf16[256,640]{1,0:T(8,128)(2,1)} %get-tuple-element.87), channel_id=1, source_target_pairs={{0,4},{1,5},{2,6},{3,7},{4,0},{5,1},{6,2},{7,3},{8,12},{9,13},{10,... | collective-permute-start | bytes 983048 | tf_op jit(solution)/shard_map/ppermute | solution.py:315
  53.0 18.4 %all-to-all-start.2 = ((f32[16,3,8,128]{3,2,1,0:T(8,128)}), f32[16,3,8,128]{3,2,1,0:T(8,128)S(1)}, u32[]{:S(2)}, u32[]{:S(2)}) async-start(f32[16,3,8,128]{3,2,1,0:T(8,128)} %broadcast_in_dim.9), calls=%async_computation.2 | async-start | bytes 393216 | tf_op jit(solution)/shard_map/all_to_all | solution.py:307
  60.0 36.4 %collective-permute-start.9 = (bf16[256,2560]{1,0:T(8,128)(2,1)}, bf16[256,2560]{1,0:T(8,128)(2,1)}, u32[]{:S(2)}, u32[]{:S(2)}) collective-permute-start(bf16[256,2560]{1,0:T(8,128)(2,1)} %collective-permute-done.2.refs_5_), channel_id=1, source_target_pairs={{0,2},{1,7},{2,4},{3,1},{4,6},{5,3},{6,0},{7,5},{8,10},{9,15},{10,... | collective-permute-start | bytes 3932168 | tf_op jit(solution)/shard_map/ppermute | solution.py:315
  71.4 1.5 %copy-start.5 = (f32[16,3,8,128]{3,2,1,0:T(8,128)}, f32[16,3,8,128]{3,2,1,0:T(8,128)S(1)}, u32[]{:S(2)}) copy-start(f32[16,3,8,128]{3,2,1,0:T(8,128)S(1)} %all-to-all-done.2.mine_ref) | copy-start | bytes 589828
  71.4 1.5 %collective-permute-start.7 = (f32[16,3,8,128]{3,2,1,0:T(8,128)S(1)}, f32[16,3,8,128]{3,2,1,0:T(8,128)S(1)}, u32[]{:S(2)}, u32[]{:S(2)}) collective-permute-start(f32[16,3,8,128]{3,2,1,0:T(8,128)S(1)} %all-to-all-done.2.mine_ref), channel_id=1, source_target_pairs={{0,1},{1,0},{2,3},{3,2},{4,5},{5,4},{6,7},{7,6},{8,9},{9,8},{10,11... | collective-permute-start | bytes 589832 | tf_op jit(solution)/shard_map/ppermute | solution.py:311
  72.9 0.7 copy-start.7
  80.3 1.7 %collective-permute-start.8 = (f32[16,3,8,128]{3,2,1,0:T(8,128)}, f32[16,3,8,128]{3,2,1,0:T(8,128)S(1)}, u32[]{:S(2)}, u32[]{:S(2)}) collective-permute-start(f32[16,3,8,128]{3,2,1,0:T(8,128)} %get-tuple-element.90), channel_id=1, source_target_pairs={{0,1},{1,0},{2,3},{3,2},{4,5},{5,4},{6,7},{7,6},{8,9},{9,8},{10,11... | collective-permute-start | bytes 589832 | tf_op jit(solution)/shard_map/ppermute | solution.py:311
  83.6 16.1 %all-to-all-start.3 = ((f32[16,3,8,128]{3,2,1,0:T(8,128)}), f32[16,3,8,128]{3,2,1,0:T(8,128)S(1)}, u32[]{:S(2)}, u32[]{:S(2)}) async-start(f32[16,3,8,128]{3,2,1,0:T(8,128)} %add.46), calls=%async_computation.3 | async-start | bytes 393216 | tf_op jit(solution)/shard_map/all_to_all | solution.py:307
  89.2 27.5 %collective-permute-start.10 = (bf16[256,640]{1,0:T(8,128)(2,1)}, bf16[256,640]{1,0:T(8,128)(2,1)}, u32[]{:S(2)}, u32[]{:S(2)}) collective-permute-start(bf16[256,640]{1,0:T(8,128)(2,1)} %convolution_convert_fusion.2), channel_id=1, source_target_pairs={{2,0},{7,1},{4,2},{1,3},{6,4},{3,5},{0,6},{5,7},{10,8},{15,9},{12,... | collective-permute-start | bytes 983048 | tf_op jit(solution)/shard_map/ppermute | solution.py:315
  90.6 26.1 %collective-permute-start.11 = (bf16[256,640]{1,0:T(8,128)(2,1)}, bf16[256,640]{1,0:T(8,128)(2,1)}, u32[]{:S(2)}, u32[]{:S(2)}) collective-permute-start(bf16[256,640]{1,0:T(8,128)(2,1)} %convolution_convert_fusion.1), channel_id=1, source_target_pairs={{0,2},{1,7},{2,4},{3,1},{4,6},{5,3},{6,0},{7,5},{8,10},{9,15},{10,... | collective-permute-start | bytes 983048 | tf_op jit(solution)/shard_map/ppermute | solution.py:315
  100.4 16.3 %all-to-all-start.4 = ((f32[8,3,8,128]{3,2,1,0:T(8,128)}), f32[8,3,8,128]{3,2,1,0:T(8,128)S(1)}, u32[]{:S(2)}, u32[]{:S(2)}) async-start(f32[8,3,8,128]{3,2,1,0:T(8,128)} %broadcast_in_dim.10), calls=%async_computation.4 | async-start | bytes 196608 | tf_op jit(solution)/shard_map/all_to_all | solution.py:307
  107.3 11.4 %copy-start.6 = (bf16[256,640]{1,0:T(8,128)(2,1)S(1)}, bf16[256,640]{1,0:T(8,128)(2,1)}, u32[]{:S(2)}) copy-start(bf16[256,640]{1,0:T(8,128)(2,1)} %convolution_convert_fusion) | copy-start | bytes 983044
  117.4 15.4 %collective-permute-start.12 = (f32[320,2560]{1,0:T(8,128)}, f32[320,2560]{1,0:T(8,128)}, u32[]{:S(2)}, u32[]{:S(2)}) collective-permute-start(f32[320,2560]{1,0:T(8,128)} %get-tuple-element.123), channel_id=1, source_target_pairs={{0,1},{1,0},{2,3},{3,2},{4,5},{5,4},{6,7},{7,6},{8,9},{9,8},{10,11... | collective-permute-start | bytes 9830408 | tf_op jit(solution)/shard_map/ppermute | solution.py:311
  118.7 10.8 %collective-permute-start.13 = (bf16[256,640]{1,0:T(8,128)(2,1)S(1)}, bf16[256,640]{1,0:T(8,128)(2,1)S(1)}, u32[]{:S(2)}, u32[]{:S(2)}) collective-permute-start(bf16[256,640]{1,0:T(8,128)(2,1)S(1)} %copy-done.6), channel_id=1, source_target_pairs={{0,4},{1,5},{2,6},{3,7},{4,0},{5,1},{6,2},{7,3},{8,12},{9,13},{10,... | collective-permute-start | bytes 983048 | tf_op jit(solution)/shard_map/ppermute | solution.py:315
  120.8 15.4 %all-to-all-start.5 = ((f32[16,3,8,128]{3,2,1,0:T(8,128)}), f32[16,3,8,128]{3,2,1,0:T(8,128)S(1)}, u32[]{:S(2)}, u32[]{:S(2)}) async-start(f32[16,3,8,128]{3,2,1,0:T(8,128)} %broadcast_in_dim.11), calls=%async_computation.5 | async-start | bytes 393216 | tf_op jit(solution)/shard_map/all_to_all | solution.py:307
  129.6 0.7 copy-start.4
  132.8 5.4 %copy-start = (f32[32,384]{1,0:T(8,128)S(1)}, f32[32,384]{1,0:T(8,128)}, u32[]{:S(2)}) copy-start(f32[32,384]{1,0:T(8,128)} %get-tuple-element.131.ortho_ref) | copy-start | bytes 147460
  132.8 5.4 %copy-start.1 = (f32[32,32]{1,0:T(8,128)S(1)}, f32[32,32]{1,0:T(8,128)}, u32[]{:S(2)}) copy-start(f32[32,32]{1,0:T(8,128)} %get-tuple-element.130.inverse_ref) | copy-start | bytes 12292
  132.8 5.4 %copy-start.2 = (s32[6]{0:T(128)S(1)}, s32[6]{0:T(128)}, u32[]{:S(2)}) copy-start(s32[6]{0:T(128)} %stack.27.place) | copy-start | bytes 76
  136.2 1.9 %collective-permute-start.14 = (f32[16,3,8,128]{3,2,1,0:T(8,128)S(1)}, f32[16,3,8,128]{3,2,1,0:T(8,128)S(1)}, u32[]{:S(2)}, u32[]{:S(2)}) collective-permute-start(f32[16,3,8,128]{3,2,1,0:T(8,128)S(1)} %all-to-all-done.5.mine_ref), channel_id=1, source_target_pairs={{0,1},{1,0},{2,3},{3,2},{4,5},{5,4},{6,7},{7,6},{8,9},{9,8},{10,11... | collective-permute-start | bytes 589832 | tf_op jit(solution)/shard_map/ppermute | solution.py:311

commit v4 on v3

--- a/solution.py
+++ b/solution.py
@@ -17,7 +17,7 @@
 AHEAD = [(2 * y + c, 2 * ((y + 1 - 2 * c) % 4) + c) for y in range(4) for c in range(2)]
 BACK = [(b, a) for a, b in AHEAD]
 ACROSS = [(2 * y + c, 2 * ((y + 2) % 4) + c) for y in range(4) for c in range(2)]
-HALF = (16, 3, 8, 128)
+HALF_Z, HALF_XY = (8, 6, 8, 128), (16, 3, 8, 128)
 
 
 def mm(a, b, ca, cb):
@@ -81,14 +81,16 @@
             mine, other = jnp.where(core == 0, low, high), jnp.where(core == 0, high, low)
         else:
             mine = other = jnp.zeros((8, 128), F32)
-        mine_ref[tile // 3, tile % 3] = mine
-        other_ref[tile // 3, tile % 3] = other
+        at = divmod(tile, mine_ref.shape[1])
+        mine_ref[at] = mine
+        other_ref[at] = other
 
 
 def collect(core, mine_ref, other_ref, whole_ref):
     for tile in range(40):
         r, j = divmod(tile, 20)
-        mine, other = mine_ref[tile // 3, tile % 3], other_ref[tile // 3, tile % 3]
+        at = divmod(tile, mine_ref.shape[1])
+        mine, other = mine_ref[at], other_ref[at]
         lanes = pl.ds(128 * j, 128)
         whole_ref[pl.ds(8 * r, 8), lanes] = jnp.where(core == 0, mine, other)
         whole_ref[pl.ds(16 + 8 * r, 8), lanes] = jnp.where(core == 0, other, mine)
@@ -126,54 +128,70 @@
 
 
 def right_kernel(
-    place, mine_ref, other_ref, x_ref, c_ref, f_any, out_ref, away_ref, gram_ref, own_ref,
-    window_ref, left_ref, f_ref, sem,
+    place, mine_ref, other_ref, x_any, c_any, f_any, out_ref, away_ref, gram_ref, own_ref,
+    window_ref, left_ref, x_ref, c_ref, f_ref, sems,
 ):
     core, lane = place[0], pl.multiple_of(place[1], 128)
-    f_in = pltpu.make_async_copy(f_any, f_ref, sem)
-    f_in.start()
+    copies = Copies(sems)
+    x_in, f_in, c_in = copies.start(x_any, x_ref), copies.start(f_any, f_ref), copies.start(c_any, c_ref)
     collect(core, mine_ref, other_ref, left_ref)
     left = left_ref[...]
-    p3 = stacked(left)
-    small = folded(mm(p3, x_ref[...], 1, 1))
-    total = folded(mm(stacked(small), c_ref[...], 1, 0))
+    own = left_ref[:, pl.ds(lane, 384)]
+    own_ref[...] = own
+    own3, p3 = stacked(own), stacked(left)
+    gram_ref[...] = sum(folded(mm(p3, p3[32 * t : 32 * t + 32], 1, 1)) for t in range(3))
+    x_in.wait()
+    small = stacked(folded(mm(p3, x_ref[...], 1, 1)))
     f_in.wait()
     put_window(place, f_ref, window_ref)
-    own = left_ref[:, pl.ds(lane, 384)]
-    own_ref[...] = own
-    own3 = stacked(own)
-    total += sum(folded(mm(own3, window_ref[t], 1, 0)) for t in range(2))
-    emit(core, total, out_ref, away_ref)
-    gram_ref[...] = sum(folded(mm(p3, p3[32 * t : 32 * t + 32], 1, 1)) for t in range(3))
+    total = sum(mm(own3, window_ref[t], 1, 0) for t in range(2))
+    c_in.wait()
+    emit(core, folded(total + mm(small, c_ref[...], 1, 0)), out_ref, away_ref)
+
+
+def back_kernel(place, c_ref, w_ref, out_ref):
+    del place
+    out_ref[...] = mm(c_ref[...], w_ref[...], 1, 1).astype(BF16)
+
+
+def back_columns(place, c, weights):
+    return pl.pallas_call(
+        back_kernel,
+        in_specs=[SMEM, VMEM, VMEM],
+        out_specs=VMEM,
+        out_shape=jax.ShapeDtypeStruct((256, 640), BF16),
+        compiler_params=pltpu.CompilerParams(vmem_limit_bytes=16 << 20),
+        cost_estimate=pl.CostEstimate(flops=84 * 10**7, bytes_accessed=5 << 20, transcendentals=0),
+    )(place, c, weights)
 
 
 def rows_kernel(place, *refs):
     xs, cs, f_any, mine_any, away_any = refs[:4], refs[4:8], refs[8], refs[9], refs[10]
     x_ref, turned, c_ref, f_ref, out_ref, sems = refs[11:]
-    core, copies = place[0], Copies(sems)
+    core, copies, parts = place[0], Copies(sems), []
     x_in = [copies.start(x, x_ref.at[pl.ds(256 * k, 256)]) for k, x in enumerate(xs)]
-    parts = []
     for j in range(4):
         lanes = pl.ds(640 * j, 640)
         parts.append([copies.start(c.at[:, lanes], c_ref.at[pl.ds(256 * k, 256), lanes]) for k, c in enumerate(cs)])
     f_in = copies.start(f_any, f_ref)
     wait(x_in)
-    first, second_ = pl.multiple_of(320 * core, 64), pl.multiple_of(320 * (1 - core), 64)
+    first, last = pl.multiple_of(320 * core, 64), pl.multiple_of(320 * (1 - core), 64)
     for k in range(4):
         block = x_ref[pl.ds(256 * k, 256), :].T
         turned[pl.ds(first, 320), pl.ds(256 * k, 256)] = block[:320]
-        turned[pl.ds(second_, 320), pl.ds(256 * k, 256)] = block[320:]
+        turned[pl.ds(last, 320), pl.ds(256 * k, 256)] = block[320:]
     sent = []
     for j in range(4):
         lanes = pl.ds(640 * j, 640)
         wait(parts[j])
         out_ref[1, :, lanes] = mm(turned[pl.ds(320, 320), :], c_ref[:, lanes], 1, 0)
         sent.append(copies.start(out_ref.at[1, :, lanes], away_any.at[:, lanes]))
+        out_ref[0, :, lanes] = mm(turned[pl.ds(0, 320), :], c_ref[:, lanes], 1, 0)
     f_in.wait()
     for j in range(4):
-        lanes = pl.ds(640 * j, 640)
-        out_ref[0, :, lanes] = mm(turned[pl.ds(0, 320), :], c_ref[:, lanes], 1, 0) + f_ref[:, lanes]
-        sent.append(copies.start(out_ref.at[0, :, lanes], mine_any.at[:, lanes]))
+        rows = pl.ds(80 * j, 80)
+        out_ref[0, rows, :] += f_ref[rows, :]
+        sent.append(copies.start(out_ref.at[0, rows], mine_any.at[rows]))
     wait(sent)
 
 
@@ -185,7 +203,7 @@
         out_shape=[jax.ShapeDtypeStruct((320, 2560), F32)] * 2,
         scratch_shapes=[pltpu.VMEM((1024, 640), BF16), pltpu.VMEM((640, 1024), BF16),
                         pltpu.VMEM((1024, 2560), BF16), pltpu.VMEM((320, 2560), F32),
-                        pltpu.VMEM((2, 320, 2560), F32), pltpu.SemaphoreType.DMA((32,))],
+                        pltpu.VMEM((2, 320, 2560), F32), pltpu.SemaphoreType.DMA((29,))],
         compiler_params=pltpu.CompilerParams(vmem_limit_bytes=119 << 19),
         cost_estimate=pl.CostEstimate(flops=34 * 10**8, bytes_accessed=17 << 20, transcendentals=0),
     )(place, *xs, *cs, feedback)
@@ -230,7 +248,7 @@
     wait(copies.made)
 
 
-def call(kernel, ins, outs, scratch, flops, size, limit=80):
+def call(kernel, ins, outs, scratch, flops, size, limit=48):
     return pl.pallas_call(
         kernel,
         in_specs=[SMEM] + ins,
@@ -244,7 +262,7 @@
 
 def left_product(place, x, c, s, f):
     return call(
-        left_kernel, [ANY, ANY, VMEM, ANY], [HALF, HALF],
+        left_kernel, [ANY, ANY, VMEM, ANY], [HALF_Z, HALF_Z],
         [pltpu.VMEM((32, 2560), F32), pltpu.VMEM((256, 2560), BF16),
          pltpu.VMEM((320, 2560), F32), pltpu.VMEM((256, 2560), BF16),
          pltpu.SemaphoreType.DMA((18,))],
@@ -254,10 +272,11 @@
 
 def right_product(place, mine, other, x, c, f):
     return call(
-        right_kernel, [VMEM] * 4 + [ANY], [HALF, HALF, (32, 32), (32, 384)],
+        right_kernel, [VMEM] * 2 + [ANY] * 3, [HALF_XY, HALF_XY, (32, 32), (32, 384)],
         [pltpu.VMEM((2, 384, 2560), BF16), pltpu.VMEM((32, 2560), F32),
-         pltpu.VMEM((320, 2560), F32), pltpu.SemaphoreType.DMA],
-        2 * 10**9, 7 << 20, 115,
+         pltpu.VMEM((256, 2560), BF16), pltpu.VMEM((256, 2560), BF16),
+         pltpu.VMEM((320, 2560), F32), pltpu.SemaphoreType.DMA((3,))],
+        2 * 10**9, 7 << 20, 119,
     )(place, mine, other, x, c, f)
 
 
@@ -267,11 +286,10 @@
     a = jnp.concatenate([gram_ref[...], jnp.zeros((32, 96), F32)], axis=1)
     a = jnp.where(lane == row + 32, 1.0, a)
     for j in range(32):
-        pivot = a[j : j + 1, :]
-        scaled = pivot / jnp.sqrt(a[j : j + 1, j : j + 1])
-        column = a[:, j : j + 1] / a[j : j + 1, j : j + 1]
-        a = jnp.where(row == j, scaled, jnp.where(row > j, a - column * pivot, a))
-    inverse = a[:, 32:64]
+        column = a[:, j : j + 1] * (1.0 / a[j : j + 1, j : j + 1])
+        a = jnp.where(row > j, a - column * a[j : j + 1, :], a)
+    pivots = jnp.sum(jnp.where(lane == row, a, 0.0), axis=1, keepdims=True)
+    inverse = a[:, 32:64] / jnp.sqrt(pivots)
     inverse_ref[...] = inverse
     i1, i2, i3 = terms(inverse)
     o1, o2, o3 = terms(own_ref[...])
@@ -320,7 +338,7 @@
 
 
 def repeated(v, n):
-    return jnp.broadcast_to(v.sum(0)[None], (n, 3, 8, 128))
+    return jnp.broadcast_to(v.sum(0)[None], (n, *v.shape[1:]))
 
 
 def shards(features, cotangent, weight, feedback, start_factors):
@@ -337,44 +355,40 @@
     mine, other = left_product(place, features, cotangent, start_factors.T, feedback)
 
     half, later = tie(mine + swap(other), features)
-    half = exchange(half, ("x", "y"))
+    half = exchange(half, "z")
     x0, x1, x2, x3 = (columns(chip, later) for chip in (y, ahead, back, across))
     weights = jnp.where(
         core == 0, jnp.concatenate([weight, swapped]), jnp.concatenate([swapped, weight])
     )
-
-    def back_columns(c):
-        return mm(c, weights, 1, 1).astype(BF16)
-
-    half, weights, x0, x1, x2, x3 = tie(half, weights, x0, x1, x2, x3)
-    half, x1, x2, x3 = tie(repeated(half, 8), x1, x2, x3)
+    g0 = back_columns(place, cotangent, weights)
+    half, g0, x0, x1, x2, x3 = tie(half, g0, x0, x1, x2, x3)
+    half, x1, x2, x3 = tie(repeated(half, 16), x1, x2, x3)
+    half = exchange(half, ("x", "y"))
+    x1, x2, x3 = send(x1, AHEAD), send(x2, BACK), send(x3, ACROSS)
+    half, c1, c2 = tie(half, c1, c2)
+    half, c1, now = tie(repeated(half, 8), c1, place)
     half = exchange(half, "z")
-    x1, x2, x3 = send(x1, AHEAD), send(x2, BACK), send(x3, ACROSS)
-    g0 = back_columns(cotangent)
-    half, g0, c1, c2 = tie(half, g0, c1, c2)
-    half, c1, c2 = tie(repeated(half, 16), c1, c2)
-    half = exchange(half, ("x", "y"))
     c3 = send(c1, AHEAD)
-    g1, g2 = back_columns(c1), back_columns(c2)
-    half, g1, g2, x1, x2, x3 = tie(half, g1, g2, x1, x2, x3)
+    g1, g2 = back_columns(now, c1, weights), back_columns(now, c2, weights)
+    half, g1, g2 = tie(half, g1, g2)
 
     mine, other, gram, own = right_product(place, half, swap(half), features, cotangent, feedback)
     half, gram, own, g1, g2 = tie(mine + swap(other), gram, own, g1, g2)
     half = exchange(half, ("x", "y"))
     u1, u2 = send(g1, BACK), send(g2, AHEAD)
     inverse, ortho = factor(gram, own)
-    inverse, ortho, c3 = tie(inverse, ortho, c3)
-    g3 = back_columns(c3)
+    inverse, ortho, now = tie(inverse, ortho, place)
+    g3 = back_columns(now, c3, weights)
     half, ortho, inverse, g3 = tie(half, ortho, inverse, g3)
-    half, c3, g3, x1, x2, x3 = tie(repeated(half, 8), c3, g3, x1, x2, x3)
+    half, g3, now = tie(repeated(half, 8), g3, place)
     half = exchange(half, "z")
     u3 = send(g3, ACROSS)
-    grown, away = gradient_rows(place, (x0, x1, x2, x3), (cotangent, c1, c2, c3), feedback)
+    grown, away = gradient_rows(now, (x0, x1, x2, x3), (cotangent, c1, c2, c3), feedback)
     half, u1, u2, grown, away = tie(half, u1, u2, grown, away)
     half, grown, away = tie(repeated(half, 16), grown, away)
     half = exchange(half, ("x", "y"))
-    grown = grown + swap(away)
-    input_grad = placed_columns(place, (g0, u1, u2, u3))
+    grown, now = tie(grown + swap(away), place)
+    input_grad = placed_columns(now, (g0, u1, u2, u3))
     half, grown, input_grad = tie(half, grown, input_grad)
 
     new_feedback, q_factor = last_step(place, half, swap(half), inverse, ortho, grown)

time: 144 us -> 134 us (0.931)
  matrix products: 13.1 us -> 0 us
  Pallas kernels: 33.2 us -> 42.2 us
  starting transfers between devices: 57.7 us -> 53 us
  waiting for transfers between devices: 21.2 us -> 18.7 us
  local copies, waits for them, and re-layouts: 5.87 us -> 7.38 us
    dot_general x4 -> x0, matrix products: 13.1 us -> none  [mm(): lax.dot_general(a, b, (((ca,), (cb,)), ((), ())), preferred_element_type=...]
    pallas_call x2 -> x6, Pallas kernels: 13.1 us -> 22.5 us  [the longest x4 10.1 us: back_columns(): pl.pallas_call(back_kernel, in_specs=[SMEM, VMEM, VMEM], out_specs=VMEM,...]
    all_to_all x6, starting transfers between devices: 37.5 us -> 31 us  [exchange(): return lax.all_to_all(u, axes, 0, 0, tiled=True)]
    ppermute x6, starting transfers between devices: 5.97 us -> 10.6 us  [swap(): return lax.ppermute(v, 'core', [(0, 1), (1, 0)])]
    ppermute x9, waiting for transfers between devices: 5.5 us -> 1.01 us  [send(): return lax.ppermute(v, FSDP, pairs)]
    all_to_all x6, waiting for transfers between devices: 10.2 us -> 14 us  [exchange(): return lax.all_to_all(u, axes, 0, 0, tiled=True)]
    ppermute x9, starting transfers between devices: 14.3 us -> 11.3 us  [send(): return lax.ppermute(v, FSDP, pairs)]
    ppermute x6, waiting for transfers between devices: 5.51 us -> 3.76 us  [swap(): return lax.ppermute(v, 'core', [(0, 1), (1, 0)])]
  transfers between devices with their start and end apart: 21 -> 21, of which waited for: 9 -> 9; matrix products, arithmetic and copies ran while one was open for 19% -> 10% of each run, Pallas kernels for 21% -> 29%
where the time goes in v4:
time: 134 us; the launch traced here: 133 us
  starting transfers between devices  53 us (40%)
  Pallas kernels  42.2 us (31%)
  waiting for transfers between devices  18.7 us (14%)
  other arithmetic  11.1 us (8%)
  local copies, waits for them, and re-layouts  7.38 us (6%)
    all_to_all x6, starting transfers between devices, exchange(): return lax.all_to_all(u, axes, 0, 0, tiled=True)  31 us
    all_to_all x6, waiting for transfers between devices, exchange(): return lax.all_to_all(u, axes, 0, 0, tiled=True)  14 us
    ppermute x9, starting transfers between devices, send(): return lax.ppermute(v, FSDP, pairs)  11.3 us
    ppermute x6, starting transfers between devices, swap(): return lax.ppermute(v, 'core', [(0, 1), (1, 0)])  10.6 us
    pallas_call x4, Pallas kernels, back_columns(): pl.pallas_call(back_kernel, in_specs=[SMEM, VMEM, VMEM], out_specs=VMEM,...  10.1 us
    pallas_call x1, Pallas kernels, gradient_rows(): pl.pallas_call(rows_kernel, in_specs=[SMEM] + [ANY] * 9, out_specs=[ANY]...  9.18 us
    pallas_call x1, Pallas kernels, left_product(): call(left_kernel, [ANY, ANY, VMEM, ANY], [HALF_Z, HALF_Z], [pltpu.VMEM((3...  6.42 us
    pallas_call x1, Pallas kernels, right_product(): call(right_kernel, [VMEM] * 2 + [ANY] * 3, [HALF_XY, HALF_XY, (32, 32), (...  6.05 us
  transfers between devices with their start and end apart: 21, of which 9 were waited for; matrix products, arithmetic and copies ran while one was open for 10% of the time, Pallas kernels for 29%

profile of v4, /device:TPU:1, one launch (start us, length us, event | category | flops | bytes accessed | tf_op | source)
XLA Modules:
  0.0 133.5 jit_solution(10101325213425972999)
XLA Ops:
  0.6 3.3 %collective-permute-start.1 = (bf16[320,2560]{1,0:T(8,128)(2,1)}, bf16[320,2560]{1,0:T(8,128)(2,1)}, u32[]{:S(2)}, u32[]{:S(2)}) collective-permute-start(bf16[320,2560]{1,0:T(8,128)(2,1)} %param.7), channel_id=1, source_target_pairs={{0,1},{1,0},{2,3},{3,2},{4,5},{5,4},{6,7},{7,6},{8,9},{9,8},{10,11... | collective-permute-start | bytes 4915208 | tf_op jit(solution)/shard_map/ppermute | solution.py:329
  4.0 2.7 %collective-permute-start.2 = (bf16[256,2560]{1,0:T(8,128)(2,1)}, bf16[256,2560]{1,0:T(8,128)(2,1)}, u32[]{:S(2)}, u32[]{:S(2)}) collective-permute-start(bf16[256,2560]{1,0:T(8,128)(2,1)} %refs_4_.1), channel_id=1, source_target_pairs={{0,2},{1,7},{2,4},{3,1},{4,6},{5,3},{6,0},{7,5},{8,10},{9,15},{10,... | collective-permute-start | bytes 3932168 | tf_op jit(solution)/shard_map/ppermute | solution.py:333
  7.3 6.4 %shard_map.76 = (f32[8,6,8,128]{3,2,1,0:T(8,128)}, f32[8,6,8,128]{3,2,1,0:T(8,128)}) custom-call(s32[6]{0:T(128)} %stack.27.place, bf16[256,2560]{1,0:T(8,128)(2,1)} %x_any.3, bf16[256,2560]{1,0:T(8,128)(2,1)} %refs_4_.1, f32[32,2560]{1,0:T(8,128)} %bitcast.8, f32[320,2560]{1,0:T(8,128)} %refs_8_.1), custom_call_target="tpu_custom_call" | custom-call | flops 2000000000 | bytes 7340032 | tf_op jit(solution)/shard_map/pallas_call | solution.py:264
  13.8 1.6 %collective-permute-done = f32[8,6,8,128]{3,2,1,0:T(8,128)S(1)} collective-permute-done((f32[8,6,8,128]{3,2,1,0:T(8,128)}, f32[8,6,8,128]{3,2,1,0:T(8,128)S(1)}, u32[]{:S(2)}, u32[]{:S(2)}) %collective-permute-start) | collective-permute-done | bytes 196640 | tf_op jit(solution)/shard_map/ppermute | solution.py:329
  15.4 1.6 %add.41 = f32[8,6,8,128]{3,2,1,0:T(8,128)} add(f32[8,6,8,128]{3,2,1,0:T(8,128)} %get-tuple-element.64, f32[8,6,8,128]{3,2,1,0:T(8,128)S(1)} %collective-permute-done) | non-fusion elementwise | flops 49152 | bytes 589824 | tf_op jit(solution)/shard_map/add | solution.py:357
  17.1 6.5 %all-to-all-start = ((f32[8,6,8,128]{3,2,1,0:T(8,128)}), f32[8,6,8,128]{3,2,1,0:T(8,128)S(1)}, u32[]{:S(2)}, u32[]{:S(2)}) async-start(f32[8,6,8,128]{3,2,1,0:T(8,128)} %add.41), calls=%async_computation | async-start | bytes 393216 | tf_op jit(solution)/shard_map/all_to_all | solution.py:325
  23.6 1.1 constant_dynamic-slice_fusion
  24.7 3.4 %maximum_select_fusion.w_ref = bf16[640,2560]{1,0:T(8,128)(2,1)S(1)} fusion(bf16[320,2560]{1,0:T(8,128)(2,1)} %collective-permute-done.1, bf16[320,2560]{1,0:T(8,128)(2,1)} %param.7, pred[]{:T(512)S(6)} %eq.3), kind=kLoop, calls=%fused_computation | loop fusion | flops 14745600 | bytes 6553601 | tf_op jit(solution)/shard_map/jit(_where)/select_n | solution.py:360
  28.1 1.7 %shard_map.77.g0 = bf16[256,640]{1,0:T(8,128)(2,1)S(1)} custom-call(s32[6]{0:T(128)S(1)} %copy-done.5, bf16[256,2560]{1,0:T(8,128)(2,1)S(1)} %copy-done, bf16[640,2560]{1,0:T(8,128)(2,1)S(1)} %maximum_select_fusion.w_ref), custom_call_target="tpu_custom_call" | custom-call | flops 840000000 | bytes 5242880 | tf_op jit(solution)/shard_map/pallas_call | solution.py:158
  29.8 0.7 copy-done.1
  30.5 2.5 %all-to-all-done = f32[8,6,8,128]{3,2,1,0:T(8,128)S(1)} async-done(((f32[8,6,8,128]{3,2,1,0:T(8,128)}), f32[8,6,8,128]{3,2,1,0:T(8,128)S(1)}, u32[]{:S(2)}, u32[]{:S(2)}) %all-to-all-start) | async-done | bytes 196640 | tf_op jit(solution)/shard_map/all_to_all | solution.py:325
  33.0 0.8 broadcast_in_dim.8
  33.8 6.8 %all-to-all-start.1 = ((f32[16,6,8,128]{3,2,1,0:T(8,128)}), f32[16,6,8,128]{3,2,1,0:T(8,128)}, u32[]{:S(2)}, u32[]{:S(2)}) async-start(f32[16,6,8,128]{3,2,1,0:T(8,128)} %broadcast_in_dim.8), calls=%async_computation.1 | async-start | bytes 786432 | tf_op jit(solution)/shard_map/all_to_all | solution.py:325
  40.7 8.1 %all-to-all-done.1 = f32[16,6,8,128]{3,2,1,0:T(8,128)} async-done(((f32[16,6,8,128]{3,2,1,0:T(8,128)}), f32[16,6,8,128]{3,2,1,0:T(8,128)}, u32[]{:S(2)}, u32[]{:S(2)}) %all-to-all-start.1) | async-done | bytes 393248 | tf_op jit(solution)/shard_map/all_to_all | solution.py:325
  48.7 1.0 reduce_sum.37
  49.7 0.7 broadcast_in_dim.9
  50.4 0.7 collective-permute-start.6
  51.2 4.4 %all-to-all-start.2 = ((f32[8,6,8,128]{3,2,1,0:T(8,128)}), f32[8,6,8,128]{3,2,1,0:T(8,128)S(1)}, u32[]{:S(2)}, u32[]{:S(2)}) async-start(f32[8,6,8,128]{3,2,1,0:T(8,128)} %broadcast_in_dim.9), calls=%async_computation.2 | async-start | bytes 393216 | tf_op jit(solution)/shard_map/all_to_all | solution.py:325
  55.6 2.5 %shard_map.78 = bf16[256,640]{1,0:T(8,128)(2,1)S(1)} custom-call(s32[6]{0:T(128)S(1)} %copy-done.5, bf16[256,2560]{1,0:T(8,128)(2,1)} %collective-permute-done.2.c_ref.refs_5_, bf16[640,2560]{1,0:T(8,128)(2,1)S(1)} %maximum_select_fusion.w_ref), custom_call_target="tpu_custom_call" | custom-call | flops 840000000 | bytes 5242880 | tf_op jit(solution)/shard_map/pallas_call | solution.py:158
  58.1 0.7 copy-done.3
  58.9 2.5 %shard_map.79 = bf16[256,640]{1,0:T(8,128)(2,1)S(1)} custom-call(s32[6]{0:T(128)S(1)} %copy-done.5, bf16[256,2560]{1,0:T(8,128)(2,1)} %collective-permute-done.3.c_ref.refs_6_, bf16[640,2560]{1,0:T(8,128)(2,1)S(1)} %maximum_select_fusion.w_ref), custom_call_target="tpu_custom_call" | custom-call | flops 840000000 | bytes 5242880 | tf_op jit(solution)/shard_map/pallas_call | solution.py:158
  61.4 0.7 copy-done.2
  62.1 2.2 %all-to-all-done.2.mine_ref = f32[8,6,8,128]{3,2,1,0:T(8,128)S(1)} async-done(((f32[8,6,8,128]{3,2,1,0:T(8,128)}), f32[8,6,8,128]{3,2,1,0:T(8,128)S(1)}, u32[]{:S(2)}, u32[]{:S(2)}) %all-to-all-start.2) | async-done | bytes 196640 | tf_op jit(solution)/shard_map/all_to_all | solution.py:325
  64.3 3.4 %collective-permute-start.4 = (f32[8,6,8,128]{3,2,1,0:T(8,128)S(1)}, f32[8,6,8,128]{3,2,1,0:T(8,128)S(1)}, u32[]{:S(2)}, u32[]{:S(2)}) collective-permute-start(f32[8,6,8,128]{3,2,1,0:T(8,128)S(1)} %all-to-all-done.2.mine_ref), channel_id=1, source_target_pairs={{0,1},{1,0},{2,3},{3,2},{4,5},{5,4},{6,7},{7,6},{8,9},{9,8},{10,11... | collective-permute-start | bytes 589832 | tf_op jit(solution)/shard_map/ppermute | solution.py:329
  67.8 1.1 collective-permute-done.4.other_ref
  68.8 0.7 copy-done.11
  69.5 6.0 %shard_map.80 = (f32[16,3,8,128]{3,2,1,0:T(8,128)}, f32[16,3,8,128]{3,2,1,0:T(8,128)}, f32[32,32]{1,0:T(8,128)}, f32[32,384]{1,0:T(8,128)}) custom-call(s32[6]{0:T(128)} %stack.27.place, f32[8,6,8,128]{3,2,1,0:T(8,128)} %copy-done.10, f32[8,6,8,128]{3,2,1,0:T(8,128)} %copy-done.11, bf16[256,2560]{1,0:T(8,128)(2,1)} %x_any.3, bf16[256,2560]{1,0:T(8,128)(2,1)} %refs_4_.1, ...), custom_call_target="tpu_custom_call" | custom-call | flops 2000000000 | bytes 7340032 | tf_op jit(solution)/shard_map/pallas_call | solution.py:274
  76.0 2.6 %collective-permute-start.9 = (bf16[256,640]{1,0:T(8,128)(2,1)}, bf16[256,640]{1,0:T(8,128)(2,1)}, u32[]{:S(2)}, u32[]{:S(2)}) collective-permute-start(bf16[256,640]{1,0:T(8,128)(2,1)} %get-tuple-element.101), channel_id=1, source_target_pairs={{0,2},{1,7},{2,4},{3,1},{4,6},{5,3},{6,0},{7,5},{8,10},{9,15},{10,... | collective-permute-start | bytes 983048 | tf_op jit(solution)/shard_map/ppermute | solution.py:333
  78.7 1.2 collective-permute-start.11
  79.8 1.6 %add.46 = f32[16,3,8,128]{3,2,1,0:T(8,128)} add(f32[16,3,8,128]{3,2,1,0:T(8,128)} %get-tuple-element.80, f32[16,3,8,128]{3,2,1,0:T(8,128)S(1)} %collective-permute-done.5) | non-fusion elementwise | flops 49152 | bytes 589824 | tf_op jit(solution)/shard_map/add | solution.py:376
  81.5 4.2 %all-to-all-start.3 = ((f32[16,3,8,128]{3,2,1,0:T(8,128)}), f32[16,3,8,128]{3,2,1,0:T(8,128)S(1)}, u32[]{:S(2)}, u32[]{:S(2)}) async-start(f32[16,3,8,128]{3,2,1,0:T(8,128)} %add.46), calls=%async_computation.3 | async-start | bytes 393216 | tf_op jit(solution)/shard_map/all_to_all | solution.py:325
  85.7 4.3 %shard_map.81 = (f32[32,32]{1,0:T(8,128)}, f32[32,384]{1,0:T(8,128)}) custom-call(f32[32,32]{1,0:T(8,128)} %get-tuple-element.87.gram_ref, f32[32,384]{1,0:T(8,128)} %get-tuple-element.88.own_ref), custom_call_target="tpu_custom_call" | custom-call | flops 10000000 | bytes 1048576 | tf_op jit(solution)/shard_map/pallas_call | solution.py:301
  90.0 1.4 %collective-permute-start.7 = (bf16[256,640]{1,0:T(8,128)(2,1)}, bf16[256,640]{1,0:T(8,128)(2,1)}, u32[]{:S(2)}, u32[]{:S(2)}) collective-permute-start(bf16[256,640]{1,0:T(8,128)(2,1)} %copy-done.3), channel_id=1, source_target_pairs={{2,0},{7,1},{4,2},{1,3},{6,4},{3,5},{0,6},{5,7},{10,8},{15,9},{12,... | collective-permute-start | bytes 983048 | tf_op jit(solution)/shard_map/ppermute | solution.py:333
  91.3 1.3 collective-permute-start.8
  92.6 3.3 %shard_map.82 = bf16[256,640]{1,0:T(8,128)(2,1)} custom-call(s32[6]{0:T(128)S(1)} %copy-done.6, bf16[256,2560]{1,0:T(8,128)(2,1)} %collective-permute-done.6.c_ref.refs_7_, bf16[640,2560]{1,0:T(8,128)(2,1)S(1)} %maximum_select_fusion.w_ref), custom_call_target="tpu_custom_call" | custom-call | flops 840000000 | bytes 5242880 | tf_op jit(solution)/shard_map/pallas_call | solution.py:158
  95.9 1.1 all-to-all-done.3
  97.7 3.8 %all-to-all-start.4 = ((f32[8,3,8,128]{3,2,1,0:T(8,128)}), f32[8,3,8,128]{3,2,1,0:T(8,128)S(1)}, u32[]{:S(2)}, u32[]{:S(2)}) async-start(f32[8,3,8,128]{3,2,1,0:T(8,128)} %broadcast_in_dim.10), calls=%async_computation.4 | async-start | bytes 196608 | tf_op jit(solution)/shard_map/all_to_all | solution.py:325
  101.5 9.2 %shard_map.83 = (f32[320,2560]{1,0:T(8,128)}, f32[320,2560]{1,0:T(8,128)}) custom-call(s32[6]{0:T(128)} %stack.27.place, bf16[256,640]{1,0:T(8,128)(2,1)} %get-tuple-element.100.refs_0_, bf16[256,640]{1,0:T(8,128)(2,1)} %collective-permute-done.9.refs_1_, bf16[256,640]{1,0:T(8,128)(2,1)} %collective-permute-done.10.refs_2_, ...), custom_call_target="tpu_custom_call" | custom-call | flops 3400000000 | bytes 17825792 | tf_op jit(solution)/shard_map/pallas_call | solution.py:199
  110.7 0.7 broadcast_in_dim.11
  111.4 1.4 %collective-permute-start.12 = (f32[320,2560]{1,0:T(8,128)}, f32[320,2560]{1,0:T(8,128)}, u32[]{:S(2)}, u32[]{:S(2)}) collective-permute-start(f32[320,2560]{1,0:T(8,128)} %get-tuple-element.111), channel_id=1, source_target_pairs={{0,1},{1,0},{2,3},{3,2},{4,5},{5,4},{6,7},{7,6},{8,9},{9,8},{10,11... | collective-permute-start | bytes 9830408 | tf_op jit(solution)/shard_map/ppermute | solution.py:329
  112.8 1.5 %collective-permute-start.13 = (bf16[256,640]{1,0:T(8,128)(2,1)}, bf16[256,640]{1,0:T(8,128)(2,1)}, u32[]{:S(2)}, u32[]{:S(2)}) collective-permute-start(bf16[256,640]{1,0:T(8,128)(2,1)} %shard_map.82), channel_id=1, source_target_pairs={{0,4},{1,5},{2,6},{3,7},{4,0},{5,1},{6,2},{7,3},{8,12},{9,13},{10,... | collective-permute-start | bytes 983048 | tf_op jit(solution)/shard_map/ppermute | solution.py:333
  114.3 5.3 %all-to-all-start.5 = ((f32[16,3,8,128]{3,2,1,0:T(8,128)}), f32[16,3,8,128]{3,2,1,0:T(8,128)S(1)}, u32[]{:S(2)}, u32[]{:S(2)}) async-start(f32[16,3,8,128]{3,2,1,0:T(8,128)} %broadcast_in_dim.11), calls=%async_computation.5 | async-start | bytes 393216 | tf_op jit(solution)/shard_map/all_to_all | solution.py:325
  119.6 3.4 %add.47.grown_ref = f32[320,2560]{1,0:T(8,128)S(1)} add(f32[320,2560]{1,0:T(8,128)} %get-tuple-element.110, f32[320,2560]{1,0:T(8,128)} %collective-permute-done.12) | non-fusion elementwise | flops 819200 | bytes 9830400 | tf_op jit(solution)/shard_map/add | solution.py:390
  123.0 1.0 collective-permute-done.13.g3
  124.0 2.4 %shard_map.84 = bf16[256,2560]{1,0:T(8,128)(2,1)} custom-call(s32[6]{0:T(128)} %stack.27.place, bf16[256,640]{1,0:T(8,128)(2,1)} %copy-done.1, bf16[256,640]{1,0:T(8,128)(2,1)} %collective-permute-done.7.g1, bf16[256,640]{1,0:T(8,128)(2,1)} %collective-permute-done.8.g2, bf16[256,640]{1,0:T(8,128)(2,1)} %collective-permute-done.13.g3), custom_call_target="tpu_custom_call" | custom-call | bytes 3145728 | tf_op jit(solution)/shard_map/pallas_call | solution.py:218
  126.6 1.8 %collective-permute-start.14 = (f32[16,3,8,128]{3,2,1,0:T(8,128)S(1)}, f32[16,3,8,128]{3,2,1,0:T(8,128)S(1)}, u32[]{:S(2)}, u32[]{:S(2)}) collective-permute-start(f32[16,3,8,128]{3,2,1,0:T(8,128)S(1)} %all-to-all-done.5.mine_ref), channel_id=1, source_target_pairs={{0,1},{1,0},{2,3},{3,2},{4,5},{5,4},{6,7},{7,6},{8,9},{9,8},{10,11... | collective-permute-start | bytes 589832 | tf_op jit(solution)/shard_map/ppermute | solution.py:329
  128.4 1.1 collective-permute-done.14.other_ref
  129.5 3.8 %shard_map.85 = (f32[320,2560]{1,0:T(8,128)}, f32[32,2560]{1,0:T(8,128)}) custom-call(s32[6]{0:T(128)S(1)} %copy-done.7, f32[16,3,8,128]{3,2,1,0:T(8,128)S(1)} %all-to-all-done.5.mine_ref, f32[16,3,8,128]{3,2,1,0:T(8,128)S(1)} %collective-permute-done.14.other_ref, f32[32,32]{1,0:T(8,128)S(1)} %copy-done.8, f32[32,384]{1,0:T(8,128)S(1)} %copy-done.4, ...), custom_call_target="tpu_custom_call" | custom-call | flops 300000000 | bytes 8388608 | tf_op jit(solution)/shard_map/pallas_call | solution.py:311
  (42 shorter events, 2.1 us)
Async XLA Ops:
  0.6 24.0 %collective-permute-start.1 = (bf16[320,2560]{1,0:T(8,128)(2,1)}, bf16[320,2560]{1,0:T(8,128)(2,1)}, u32[]{:S(2)}, u32[]{:S(2)}) collective-permute-start(bf16[320,2560]{1,0:T(8,128)(2,1)} %param.7), channel_id=1, source_target_pairs={{0,1},{1,0},{2,3},{3,2},{4,5},{5,4},{6,7},{7,6},{8,9},{9,8},{10,11... | collective-permute-start | bytes 4915208 | tf_op jit(solution)/shard_map/ppermute | solution.py:329
  4.0 36.7 %collective-permute-start.3 = (bf16[256,2560]{1,0:T(8,128)(2,1)}, bf16[256,2560]{1,0:T(8,128)(2,1)}, u32[]{:S(2)}, u32[]{:S(2)}) collective-permute-start(bf16[256,2560]{1,0:T(8,128)(2,1)} %refs_4_.1), channel_id=1, source_target_pairs={{2,0},{7,1},{4,2},{1,3},{6,4},{3,5},{0,6},{5,7},{10,8},{15,9},{12,... | collective-permute-start | bytes 3932168 | tf_op jit(solution)/shard_map/ppermute | solution.py:333
  4.0 36.7 %collective-permute-start.2 = (bf16[256,2560]{1,0:T(8,128)(2,1)}, bf16[256,2560]{1,0:T(8,128)(2,1)}, u32[]{:S(2)}, u32[]{:S(2)}) collective-permute-start(bf16[256,2560]{1,0:T(8,128)(2,1)} %refs_4_.1), channel_id=1, source_target_pairs={{0,2},{1,7},{2,4},{3,1},{4,6},{5,3},{6,0},{7,5},{8,10},{9,15},{10,... | collective-permute-start | bytes 3932168 | tf_op jit(solution)/shard_map/ppermute | solution.py:333
  7.3 16.3 %copy-start.9 = (bf16[256,2560]{1,0:T(8,128)(2,1)S(1)}, bf16[256,2560]{1,0:T(8,128)(2,1)}, u32[]{:S(2)}) copy-start(bf16[256,2560]{1,0:T(8,128)(2,1)} %x_any.3) | copy-start | bytes 3932164
  13.7 1.7 %collective-permute-start = (f32[8,6,8,128]{3,2,1,0:T(8,128)}, f32[8,6,8,128]{3,2,1,0:T(8,128)S(1)}, u32[]{:S(2)}, u32[]{:S(2)}) collective-permute-start(f32[8,6,8,128]{3,2,1,0:T(8,128)} %get-tuple-element.65), channel_id=1, source_target_pairs={{0,1},{1,0},{2,3},{3,2},{4,5},{5,4},{6,7},{7,6},{8,9},{9,8},{10,11... | collective-permute-start | bytes 589832 | tf_op jit(solution)/shard_map/ppermute | solution.py:329
  17.1 16.0 %all-to-all-start = ((f32[8,6,8,128]{3,2,1,0:T(8,128)}), f32[8,6,8,128]{3,2,1,0:T(8,128)S(1)}, u32[]{:S(2)}, u32[]{:S(2)}) async-start(f32[8,6,8,128]{3,2,1,0:T(8,128)} %add.41), calls=%async_computation | async-start | bytes 393216 | tf_op jit(solution)/shard_map/all_to_all | solution.py:325
  24.7 3.4 %copy-start = (bf16[256,2560]{1,0:T(8,128)(2,1)S(1)}, bf16[256,2560]{1,0:T(8,128)(2,1)}, u32[]{:S(2)}) copy-start(bf16[256,2560]{1,0:T(8,128)(2,1)} %refs_4_.1) | copy-start | bytes 3932164
  24.7 3.4 %copy-start.5 = (s32[6]{0:T(128)S(1)}, s32[6]{0:T(128)}, u32[]{:S(2)}) copy-start(s32[6]{0:T(128)} %stack.27.place) | copy-start | bytes 76
  29.8 0.7 copy-start.1
  33.8 14.9 %all-to-all-start.1 = ((f32[16,6,8,128]{3,2,1,0:T(8,128)}), f32[16,6,8,128]{3,2,1,0:T(8,128)}, u32[]{:S(2)}, u32[]{:S(2)}) async-start(f32[16,6,8,128]{3,2,1,0:T(8,128)} %broadcast_in_dim.8), calls=%async_computation.1 | async-start | bytes 786432 | tf_op jit(solution)/shard_map/all_to_all | solution.py:325
  50.4 40.9 %collective-permute-start.6 = (bf16[256,2560]{1,0:T(8,128)(2,1)}, bf16[256,2560]{1,0:T(8,128)(2,1)}, u32[]{:S(2)}, u32[]{:S(2)}) collective-permute-start(bf16[256,2560]{1,0:T(8,128)(2,1)} %collective-permute-done.2.c_ref.refs_5_), channel_id=1, source_target_pairs={{0,2},{1,7},{2,4},{3,1},{4,6},{5,3},{6,0},{7,5},{8,10},{9,15},{10,... | collective-permute-start | bytes 3932168 | tf_op jit(solution)/shard_map/ppermute | solution.py:333
  51.2 13.2 %all-to-all-start.2 = ((f32[8,6,8,128]{3,2,1,0:T(8,128)}), f32[8,6,8,128]{3,2,1,0:T(8,128)S(1)}, u32[]{:S(2)}, u32[]{:S(2)}) async-start(f32[8,6,8,128]{3,2,1,0:T(8,128)} %broadcast_in_dim.9), calls=%async_computation.2 | async-start | bytes 393216 | tf_op jit(solution)/shard_map/all_to_all | solution.py:325
  58.1 0.7 copy-start.3
  61.4 0.7 copy-start.2
  62.1 30.5 %copy-start.6 = (s32[6]{0:T(128)S(1)}, s32[6]{0:T(128)}, u32[]{:S(2)}) copy-start(s32[6]{0:T(128)} %stack.27.place) | copy-start | bytes 76
  64.3 4.5 %copy-start.10 = (f32[8,6,8,128]{3,2,1,0:T(8,128)}, f32[8,6,8,128]{3,2,1,0:T(8,128)S(1)}, u32[]{:S(2)}) copy-start(f32[8,6,8,128]{3,2,1,0:T(8,128)S(1)} %all-to-all-done.2.mine_ref) | copy-start | bytes 589828
  64.3 4.5 %collective-permute-start.4 = (f32[8,6,8,128]{3,2,1,0:T(8,128)S(1)}, f32[8,6,8,128]{3,2,1,0:T(8,128)S(1)}, u32[]{:S(2)}, u32[]{:S(2)}) collective-permute-start(f32[8,6,8,128]{3,2,1,0:T(8,128)S(1)} %all-to-all-done.2.mine_ref), channel_id=1, source_target_pairs={{0,1},{1,0},{2,3},{3,2},{4,5},{5,4},{6,7},{7,6},{8,9},{9,8},{10,11... | collective-permute-start | bytes 589832 | tf_op jit(solution)/shard_map/ppermute | solution.py:329
  68.8 0.7 copy-start.11
  75.6 4.3 %collective-permute-start.5 = (f32[16,3,8,128]{3,2,1,0:T(8,128)}, f32[16,3,8,128]{3,2,1,0:T(8,128)S(1)}, u32[]{:S(2)}, u32[]{:S(2)}) collective-permute-start(f32[16,3,8,128]{3,2,1,0:T(8,128)} %get-tuple-element.81), channel_id=1, source_target_pairs={{0,1},{1,0},{2,3},{3,2},{4,5},{5,4},{6,7},{7,6},{8,9},{9,8},{10,11... | collective-permute-start | bytes 589832 | tf_op jit(solution)/shard_map/ppermute | solution.py:329
  76.0 25.4 %collective-permute-start.9 = (bf16[256,640]{1,0:T(8,128)(2,1)}, bf16[256,640]{1,0:T(8,128)(2,1)}, u32[]{:S(2)}, u32[]{:S(2)}) collective-permute-start(bf16[256,640]{1,0:T(8,128)(2,1)} %get-tuple-element.101), channel_id=1, source_target_pairs={{0,2},{1,7},{2,4},{3,1},{4,6},{5,3},{6,0},{7,5},{8,10},{9,15},{10,... | collective-permute-start | bytes 983048 | tf_op jit(solution)/shard_map/ppermute | solution.py:333
  78.7 22.8 %collective-permute-start.10 = (bf16[256,640]{1,0:T(8,128)(2,1)}, bf16[256,640]{1,0:T(8,128)(2,1)}, u32[]{:S(2)}, u32[]{:S(2)}) collective-permute-start(bf16[256,640]{1,0:T(8,128)(2,1)} %get-tuple-element.102), channel_id=1, source_target_pairs={{2,0},{7,1},{4,2},{1,3},{6,4},{3,5},{0,6},{5,7},{10,8},{15,9},{12,... | collective-permute-start | bytes 983048 | tf_op jit(solution)/shard_map/ppermute | solution.py:333
  78.7 22.8 %collective-permute-start.11 = (bf16[256,640]{1,0:T(8,128)(2,1)}, bf16[256,640]{1,0:T(8,128)(2,1)}, u32[]{:S(2)}, u32[]{:S(2)}) collective-permute-start(bf16[256,640]{1,0:T(8,128)(2,1)} %get-tuple-element.103), channel_id=1, source_target_pairs={{0,4},{1,5},{2,6},{3,7},{4,0},{5,1},{6,2},{7,3},{8,12},{9,13},{10,... | collective-permute-start | bytes 983048 | tf_op jit(solution)/shard_map/ppermute | solution.py:333
  81.5 15.5 %all-to-all-start.3 = ((f32[16,3,8,128]{3,2,1,0:T(8,128)}), f32[16,3,8,128]{3,2,1,0:T(8,128)S(1)}, u32[]{:S(2)}, u32[]{:S(2)}) async-start(f32[16,3,8,128]{3,2,1,0:T(8,128)} %add.46), calls=%async_computation.3 | async-start | bytes 393216 | tf_op jit(solution)/shard_map/all_to_all | solution.py:325
  90.0 20.7 %collective-permute-start.7 = (bf16[256,640]{1,0:T(8,128)(2,1)}, bf16[256,640]{1,0:T(8,128)(2,1)}, u32[]{:S(2)}, u32[]{:S(2)}) collective-permute-start(bf16[256,640]{1,0:T(8,128)(2,1)} %copy-done.3), channel_id=1, source_target_pairs={{2,0},{7,1},{4,2},{1,3},{6,4},{3,5},{0,6},{5,7},{10,8},{15,9},{12,... | collective-permute-start | bytes 983048 | tf_op jit(solution)/shard_map/ppermute | solution.py:333
  91.3 19.3 %collective-permute-start.8 = (bf16[256,640]{1,0:T(8,128)(2,1)}, bf16[256,640]{1,0:T(8,128)(2,1)}, u32[]{:S(2)}, u32[]{:S(2)}) collective-permute-start(bf16[256,640]{1,0:T(8,128)(2,1)} %copy-done.2), channel_id=1, source_target_pairs={{0,2},{1,7},{2,4},{3,1},{4,6},{5,3},{6,0},{7,5},{8,10},{9,15},{10,... | collective-permute-start | bytes 983048 | tf_op jit(solution)/shard_map/ppermute | solution.py:333
  97.7 13.0 %all-to-all-start.4 = ((f32[8,3,8,128]{3,2,1,0:T(8,128)}), f32[8,3,8,128]{3,2,1,0:T(8,128)S(1)}, u32[]{:S(2)}, u32[]{:S(2)}) async-start(f32[8,3,8,128]{3,2,1,0:T(8,128)} %broadcast_in_dim.10), calls=%async_computation.4 | async-start | bytes 196608 | tf_op jit(solution)/shard_map/all_to_all | solution.py:325
  111.4 8.2 %collective-permute-start.12 = (f32[320,2560]{1,0:T(8,128)}, f32[320,2560]{1,0:T(8,128)}, u32[]{:S(2)}, u32[]{:S(2)}) collective-permute-start(f32[320,2560]{1,0:T(8,128)} %get-tuple-element.111), channel_id=1, source_target_pairs={{0,1},{1,0},{2,3},{3,2},{4,5},{5,4},{6,7},{7,6},{8,9},{9,8},{10,11... | collective-permute-start | bytes 9830408 | tf_op jit(solution)/shard_map/ppermute | solution.py:329
  112.8 11.2 %collective-permute-start.13 = (bf16[256,640]{1,0:T(8,128)(2,1)}, bf16[256,640]{1,0:T(8,128)(2,1)}, u32[]{:S(2)}, u32[]{:S(2)}) collective-permute-start(bf16[256,640]{1,0:T(8,128)(2,1)} %shard_map.82), channel_id=1, source_target_pairs={{0,4},{1,5},{2,6},{3,7},{4,0},{5,1},{6,2},{7,3},{8,12},{9,13},{10,... | collective-permute-start | bytes 983048 | tf_op jit(solution)/shard_map/ppermute | solution.py:333
  114.3 12.3 %all-to-all-start.5 = ((f32[16,3,8,128]{3,2,1,0:T(8,128)}), f32[16,3,8,128]{3,2,1,0:T(8,128)S(1)}, u32[]{:S(2)}, u32[]{:S(2)}) async-start(f32[16,3,8,128]{3,2,1,0:T(8,128)} %broadcast_in_dim.11), calls=%async_computation.5 | async-start | bytes 393216 | tf_op jit(solution)/shard_map/all_to_all | solution.py:325
  119.6 9.9 %copy-start.4 = (f32[32,384]{1,0:T(8,128)S(1)}, f32[32,384]{1,0:T(8,128)}, u32[]{:S(2)}) copy-start(f32[32,384]{1,0:T(8,128)} %get-tuple-element.121.ortho_ref) | copy-start | bytes 147460
  119.6 9.9 %copy-start.7 = (s32[6]{0:T(128)S(1)}, s32[6]{0:T(128)}, u32[]{:S(2)}) copy-start(s32[6]{0:T(128)} %stack.27.place) | copy-start | bytes 76
  119.6 9.9 %copy-start.8 = (f32[32,32]{1,0:T(8,128)S(1)}, f32[32,32]{1,0:T(8,128)}, u32[]{:S(2)}) copy-start(f32[32,32]{1,0:T(8,128)} %get-tuple-element.120.inverse_ref) | copy-start | bytes 12292
  126.6 2.9 %collective-permute-start.14 = (f32[16,3,8,128]{3,2,1,0:T(8,128)S(1)}, f32[16,3,8,128]{3,2,1,0:T(8,128)S(1)}, u32[]{:S(2)}, u32[]{:S(2)}) collective-permute-start(f32[16,3,8,128]{3,2,1,0:T(8,128)S(1)} %all-to-all-done.5.mine_ref), channel_id=1, source_target_pairs={{0,1},{1,0},{2,3},{3,2},{4,5},{5,4},{6,7},{7,6},{8,9},{9,8},{10,11... | collective-permute-start | bytes 589832 | tf_op jit(solution)/shard_map/ppermute | solution.py:329

commit v5 on v4

--- a/solution.py
+++ b/solution.py
@@ -97,9 +97,10 @@
 
 
 def left_kernel(
-    place, x_any, c_any, s_ref, f_any, mine_ref, other_ref, sum_ref, x_ref, f_ref, c_ref, sems
+    x_any, c_any, s_ref, f_any, mine_ref, other_ref, sum_ref, x_ref, f_ref, c_ref, sems
 ):
-    core, lane = place[0], pl.multiple_of(place[1], 128)
+    core = lax.axis_index("core")
+    lane = pl.multiple_of(128 * (5 * lax.axis_index("y") + 2 * core), 128)
     copies = Copies(sems)
 
     def fetch(source, target, parts, rows):
@@ -251,7 +252,7 @@
 def call(kernel, ins, outs, scratch, flops, size, limit=48):
     return pl.pallas_call(
         kernel,
-        in_specs=[SMEM] + ins,
+        in_specs=ins,
         out_specs=[VMEM] * len(outs),
         out_shape=[jax.ShapeDtypeStruct(s, F32) for s in outs],
         scratch_shapes=scratch,
@@ -260,19 +261,19 @@
     )
 
 
-def left_product(place, x, c, s, f):
+def left_product(x, c, s, f):
     return call(
         left_kernel, [ANY, ANY, VMEM, ANY], [HALF_Z, HALF_Z],
         [pltpu.VMEM((32, 2560), F32), pltpu.VMEM((256, 2560), BF16),
          pltpu.VMEM((320, 2560), F32), pltpu.VMEM((256, 2560), BF16),
          pltpu.SemaphoreType.DMA((18,))],
         2 * 10**9, 7 << 20, 119,
-    )(place, x, c, s, f)
+    )(x, c, s, f)
 
 
 def right_product(place, mine, other, x, c, f):
     return call(
-        right_kernel, [VMEM] * 2 + [ANY] * 3, [HALF_XY, HALF_XY, (32, 32), (32, 384)],
+        right_kernel, [SMEM] + [VMEM] * 2 + [ANY] * 3, [HALF_XY, HALF_XY, (32, 32), (32, 384)],
         [pltpu.VMEM((2, 384, 2560), BF16), pltpu.VMEM((32, 2560), F32),
          pltpu.VMEM((256, 2560), BF16), pltpu.VMEM((256, 2560), BF16),
          pltpu.VMEM((320, 2560), F32), pltpu.SemaphoreType.DMA((3,))],
@@ -352,7 +353,7 @@
 
     c1, c2 = send(cotangent, AHEAD), send(cotangent, BACK)
     swapped = swap(weight)
-    mine, other = left_product(place, features, cotangent, start_factors.T, feedback)
+    mine, other = left_product(features, cotangent, start_factors.T, feedback)
 
     half, later = tie(mine + swap(other), features)
     half = exchange(half, "z")

time: 134 us -> 134 us (level)
  transfers between devices with their start and end apart: 21 -> 21, of which waited for: 9 -> 9; matrix products, arithmetic and copies ran while one was open for 10% -> 9% of each run, Pallas kernels for 29% -> 29%
where the time goes in v5:
time: 134 us; the launch traced here: 133 us
  starting transfers between devices  53 us (40%)
  Pallas kernels  42.1 us (31%)
  waiting for transfers between devices  18.7 us (14%)
  other arithmetic  11.1 us (8%)
  local copies, waits for them, and re-layouts  6.85 us (5%)
    all_to_all x6, starting transfers between devices, exchange(): return lax.all_to_all(u, axes, 0, 0, tiled=True)  31.1 us
    all_to_all x6, waiting for transfers between devices, exchange(): return lax.all_to_all(u, axes, 0, 0, tiled=True)  14 us
    ppermute x9, starting transfers between devices, send(): return lax.ppermute(v, FSDP, pairs)  11.3 us
    ppermute x6, starting transfers between devices, swap(): return lax.ppermute(v, 'core', [(0, 1), (1, 0)])  10.6 us
    pallas_call x4, Pallas kernels, back_columns(): pl.pallas_call(back_kernel, in_specs=[SMEM, VMEM, VMEM], out_specs=VMEM,...  10.1 us
    pallas_call x1, Pallas kernels, gradient_rows(): pl.pallas_call(rows_kernel, in_specs=[SMEM] + [ANY] * 9, out_specs=[ANY]...  9.18 us
    pallas_call x1, Pallas kernels, left_product(): call(left_kernel, [ANY, ANY, VMEM, ANY], [HALF_Z, HALF_Z], [pltpu.VMEM((3...  6.33 us
    pallas_call x1, Pallas kernels, right_product(): call(right_kernel, [SMEM] + [VMEM] * 2 + [ANY] * 3, [HALF_XY, HALF_XY, (3...  6.05 us
  transfers between devices with their start and end apart: 21, of which 9 were waited for; matrix products, arithmetic and copies ran while one was open for 9% of the time, Pallas kernels for 29%

profile of v5, /device:TPU:1, one launch (start us, length us, event | category | flops | bytes accessed | tf_op | source)
XLA Modules:
  0.0 132.8 jit_solution(1782540237868472330)
XLA Ops:
  0.6 3.3 %collective-permute-start.1 = (bf16[320,2560]{1,0:T(8,128)(2,1)}, bf16[320,2560]{1,0:T(8,128)(2,1)}, u32[]{:S(2)}, u32[]{:S(2)}) collective-permute-start(bf16[320,2560]{1,0:T(8,128)(2,1)} %param.7), channel_id=1, source_target_pairs={{0,1},{1,0},{2,3},{3,2},{4,5},{5,4},{6,7},{7,6},{8,9},{9,8},{10,11... | collective-permute-start | bytes 4915208 | tf_op jit(solution)/shard_map/ppermute | solution.py:330
  4.0 2.7 %collective-permute-start.2 = (bf16[256,2560]{1,0:T(8,128)(2,1)}, bf16[256,2560]{1,0:T(8,128)(2,1)}, u32[]{:S(2)}, u32[]{:S(2)}) collective-permute-start(bf16[256,2560]{1,0:T(8,128)(2,1)} %refs_4_.1), channel_id=1, source_target_pairs={{0,2},{1,7},{2,4},{3,1},{4,6},{5,3},{6,0},{7,5},{8,10},{9,15},{10,... | collective-permute-start | bytes 3932168 | tf_op jit(solution)/shard_map/ppermute | solution.py:334
  6.6 6.3 %shard_map.76 = (f32[8,6,8,128]{3,2,1,0:T(8,128)}, f32[8,6,8,128]{3,2,1,0:T(8,128)}) custom-call(bf16[256,2560]{1,0:T(8,128)(2,1)} %x_any.3, bf16[256,2560]{1,0:T(8,128)(2,1)} %refs_4_.1, f32[32,2560]{1,0:T(8,128)} %bitcast.8, f32[320,2560]{1,0:T(8,128)} %refs_8_.1), custom_call_target="tpu_custom_call" | custom-call | flops 2000000000 | bytes 7340032 | tf_op jit(solution)/shard_map/pallas_call | solution.py:265
  13.2 1.5 %collective-permute-done = f32[8,6,8,128]{3,2,1,0:T(8,128)S(1)} collective-permute-done((f32[8,6,8,128]{3,2,1,0:T(8,128)}, f32[8,6,8,128]{3,2,1,0:T(8,128)S(1)}, u32[]{:S(2)}, u32[]{:S(2)}) %collective-permute-start) | collective-permute-done | bytes 196640 | tf_op jit(solution)/shard_map/ppermute | solution.py:330
  14.7 1.6 %add.41 = f32[8,6,8,128]{3,2,1,0:T(8,128)} add(f32[8,6,8,128]{3,2,1,0:T(8,128)} %get-tuple-element.64, f32[8,6,8,128]{3,2,1,0:T(8,128)S(1)} %collective-permute-done) | non-fusion elementwise | flops 49152 | bytes 589824 | tf_op jit(solution)/shard_map/add | solution.py:358
  16.3 6.5 %all-to-all-start = ((f32[8,6,8,128]{3,2,1,0:T(8,128)}), f32[8,6,8,128]{3,2,1,0:T(8,128)S(1)}, u32[]{:S(2)}, u32[]{:S(2)}) async-start(f32[8,6,8,128]{3,2,1,0:T(8,128)} %add.41), calls=%async_computation | async-start | bytes 393216 | tf_op jit(solution)/shard_map/all_to_all | solution.py:326
  22.9 1.1 constant_dynamic-slice_fusion
  24.0 3.4 %maximum_select_fusion.w_ref = bf16[640,2560]{1,0:T(8,128)(2,1)S(1)} fusion(bf16[320,2560]{1,0:T(8,128)(2,1)} %collective-permute-done.1, bf16[320,2560]{1,0:T(8,128)(2,1)} %param.7, pred[]{:T(512)S(6)} %eq.3), kind=kLoop, calls=%fused_computation | loop fusion | flops 14745600 | bytes 6553601 | tf_op jit(solution)/shard_map/jit(_where)/select_n | solution.py:361
  27.3 1.7 %shard_map.77.g0 = bf16[256,640]{1,0:T(8,128)(2,1)S(1)} custom-call(s32[6]{0:T(128)S(1)} %stack.27.place, bf16[256,2560]{1,0:T(8,128)(2,1)S(1)} %copy-done, bf16[640,2560]{1,0:T(8,128)(2,1)S(1)} %maximum_select_fusion.w_ref), custom_call_target="tpu_custom_call" | custom-call | flops 840000000 | bytes 5242880 | tf_op jit(solution)/shard_map/pallas_call | solution.py:159
  29.1 0.7 copy-done.1
  29.8 2.5 %all-to-all-done = f32[8,6,8,128]{3,2,1,0:T(8,128)S(1)} async-done(((f32[8,6,8,128]{3,2,1,0:T(8,128)}), f32[8,6,8,128]{3,2,1,0:T(8,128)S(1)}, u32[]{:S(2)}, u32[]{:S(2)}) %all-to-all-start) | async-done | bytes 196640 | tf_op jit(solution)/shard_map/all_to_all | solution.py:326
  32.3 0.8 broadcast_in_dim.8
  33.1 6.8 %all-to-all-start.1 = ((f32[16,6,8,128]{3,2,1,0:T(8,128)}), f32[16,6,8,128]{3,2,1,0:T(8,128)}, u32[]{:S(2)}, u32[]{:S(2)}) async-start(f32[16,6,8,128]{3,2,1,0:T(8,128)} %broadcast_in_dim.8), calls=%async_computation.1 | async-start | bytes 786432 | tf_op jit(solution)/shard_map/all_to_all | solution.py:326
  39.9 8.1 %all-to-all-done.1 = f32[16,6,8,128]{3,2,1,0:T(8,128)} async-done(((f32[16,6,8,128]{3,2,1,0:T(8,128)}), f32[16,6,8,128]{3,2,1,0:T(8,128)}, u32[]{:S(2)}, u32[]{:S(2)}) %all-to-all-start.1) | async-done | bytes 393248 | tf_op jit(solution)/shard_map/all_to_all | solution.py:326
  48.0 1.0 reduce_sum.37
  49.0 0.7 broadcast_in_dim.9
  49.7 0.7 collective-permute-start.6
  50.4 4.4 %all-to-all-start.2 = ((f32[8,6,8,128]{3,2,1,0:T(8,128)}), f32[8,6,8,128]{3,2,1,0:T(8,128)S(1)}, u32[]{:S(2)}, u32[]{:S(2)}) async-start(f32[8,6,8,128]{3,2,1,0:T(8,128)} %broadcast_in_dim.9), calls=%async_computation.2 | async-start | bytes 393216 | tf_op jit(solution)/shard_map/all_to_all | solution.py:326
  54.9 2.5 %shard_map.78 = bf16[256,640]{1,0:T(8,128)(2,1)S(1)} custom-call(s32[6]{0:T(128)S(1)} %stack.27.place, bf16[256,2560]{1,0:T(8,128)(2,1)} %collective-permute-done.2.c_ref.refs_5_, bf16[640,2560]{1,0:T(8,128)(2,1)S(1)} %maximum_select_fusion.w_ref), custom_call_target="tpu_custom_call" | custom-call | flops 840000000 | bytes 5242880 | tf_op jit(solution)/shard_map/pallas_call | solution.py:159
  57.4 0.7 copy-done.3
  58.1 2.5 %shard_map.79 = bf16[256,640]{1,0:T(8,128)(2,1)S(1)} custom-call(s32[6]{0:T(128)S(1)} %stack.27.place, bf16[256,2560]{1,0:T(8,128)(2,1)} %collective-permute-done.3.c_ref.refs_6_, bf16[640,2560]{1,0:T(8,128)(2,1)S(1)} %maximum_select_fusion.w_ref), custom_call_target="tpu_custom_call" | custom-call | flops 840000000 | bytes 5242880 | tf_op jit(solution)/shard_map/pallas_call | solution.py:159
  60.7 0.7 copy-done.2
  61.4 2.2 %all-to-all-done.2.mine_ref = f32[8,6,8,128]{3,2,1,0:T(8,128)S(1)} async-done(((f32[8,6,8,128]{3,2,1,0:T(8,128)}), f32[8,6,8,128]{3,2,1,0:T(8,128)S(1)}, u32[]{:S(2)}, u32[]{:S(2)}) %all-to-all-start.2) | async-done | bytes 196640 | tf_op jit(solution)/shard_map/all_to_all | solution.py:326
  63.6 3.4 %collective-permute-start.4 = (f32[8,6,8,128]{3,2,1,0:T(8,128)S(1)}, f32[8,6,8,128]{3,2,1,0:T(8,128)S(1)}, u32[]{:S(2)}, u32[]{:S(2)}) collective-permute-start(f32[8,6,8,128]{3,2,1,0:T(8,128)S(1)} %all-to-all-done.2.mine_ref), channel_id=1, source_target_pairs={{0,1},{1,0},{2,3},{3,2},{4,5},{5,4},{6,7},{7,6},{8,9},{9,8},{10,11... | collective-permute-start | bytes 589832 | tf_op jit(solution)/shard_map/ppermute | solution.py:330
  67.0 1.1 collective-permute-done.4.other_ref
  68.1 0.7 copy-done.11
  68.8 6.0 %shard_map.80 = (f32[16,3,8,128]{3,2,1,0:T(8,128)}, f32[16,3,8,128]{3,2,1,0:T(8,128)}, f32[32,32]{1,0:T(8,128)}, f32[32,384]{1,0:T(8,128)}) custom-call(s32[6]{0:T(128)} %copy-done.5, f32[8,6,8,128]{3,2,1,0:T(8,128)} %copy-done.10, f32[8,6,8,128]{3,2,1,0:T(8,128)} %copy-done.11, bf16[256,2560]{1,0:T(8,128)(2,1)} %x_any.3, bf16[256,2560]{1,0:T(8,128)(2,1)} %refs_4_.1, ...), custom_call_target="tpu_custom_call" | custom-call | flops 2000000000 | bytes 7340032 | tf_op jit(solution)/shard_map/pallas_call | solution.py:275
  75.3 2.6 %collective-permute-start.9 = (bf16[256,640]{1,0:T(8,128)(2,1)}, bf16[256,640]{1,0:T(8,128)(2,1)}, u32[]{:S(2)}, u32[]{:S(2)}) collective-permute-start(bf16[256,640]{1,0:T(8,128)(2,1)} %get-tuple-element.101), channel_id=1, source_target_pairs={{0,2},{1,7},{2,4},{3,1},{4,6},{5,3},{6,0},{7,5},{8,10},{9,15},{10,... | collective-permute-start | bytes 983048 | tf_op jit(solution)/shard_map/ppermute | solution.py:334
  77.9 1.2 collective-permute-start.11
  79.1 1.6 %add.46 = f32[16,3,8,128]{3,2,1,0:T(8,128)} add(f32[16,3,8,128]{3,2,1,0:T(8,128)} %get-tuple-element.80, f32[16,3,8,128]{3,2,1,0:T(8,128)S(1)} %collective-permute-done.5) | non-fusion elementwise | flops 49152 | bytes 589824 | tf_op jit(solution)/shard_map/add | solution.py:377
  80.7 4.2 %all-to-all-start.3 = ((f32[16,3,8,128]{3,2,1,0:T(8,128)}), f32[16,3,8,128]{3,2,1,0:T(8,128)S(1)}, u32[]{:S(2)}, u32[]{:S(2)}) async-start(f32[16,3,8,128]{3,2,1,0:T(8,128)} %add.46), calls=%async_computation.3 | async-start | bytes 393216 | tf_op jit(solution)/shard_map/all_to_all | solution.py:326
  85.0 4.3 %shard_map.81 = (f32[32,32]{1,0:T(8,128)}, f32[32,384]{1,0:T(8,128)}) custom-call(f32[32,32]{1,0:T(8,128)} %get-tuple-element.87.gram_ref, f32[32,384]{1,0:T(8,128)} %get-tuple-element.88.own_ref), custom_call_target="tpu_custom_call" | custom-call | flops 10000000 | bytes 1048576 | tf_op jit(solution)/shard_map/pallas_call | solution.py:302
  89.2 1.4 %collective-permute-start.7 = (bf16[256,640]{1,0:T(8,128)(2,1)}, bf16[256,640]{1,0:T(8,128)(2,1)}, u32[]{:S(2)}, u32[]{:S(2)}) collective-permute-start(bf16[256,640]{1,0:T(8,128)(2,1)} %copy-done.3), channel_id=1, source_target_pairs={{2,0},{7,1},{4,2},{1,3},{6,4},{3,5},{0,6},{5,7},{10,8},{15,9},{12,... | collective-permute-start | bytes 983048 | tf_op jit(solution)/shard_map/ppermute | solution.py:334
  90.6 1.3 collective-permute-start.8
  91.9 3.3 %shard_map.82 = bf16[256,640]{1,0:T(8,128)(2,1)} custom-call(s32[6]{0:T(128)S(1)} %copy-done.6, bf16[256,2560]{1,0:T(8,128)(2,1)} %collective-permute-done.6.c_ref.refs_7_, bf16[640,2560]{1,0:T(8,128)(2,1)S(1)} %maximum_select_fusion.w_ref), custom_call_target="tpu_custom_call" | custom-call | flops 840000000 | bytes 5242880 | tf_op jit(solution)/shard_map/pallas_call | solution.py:159
  95.2 1.1 all-to-all-done.3
  96.9 3.8 %all-to-all-start.4 = ((f32[8,3,8,128]{3,2,1,0:T(8,128)}), f32[8,3,8,128]{3,2,1,0:T(8,128)S(1)}, u32[]{:S(2)}, u32[]{:S(2)}) async-start(f32[8,3,8,128]{3,2,1,0:T(8,128)} %broadcast_in_dim.10), calls=%async_computation.4 | async-start | bytes 196608 | tf_op jit(solution)/shard_map/all_to_all | solution.py:326
  100.8 9.2 %shard_map.83 = (f32[320,2560]{1,0:T(8,128)}, f32[320,2560]{1,0:T(8,128)}) custom-call(s32[6]{0:T(128)} %copy-done.5, bf16[256,640]{1,0:T(8,128)(2,1)} %get-tuple-element.100.refs_0_, bf16[256,640]{1,0:T(8,128)(2,1)} %collective-permute-done.9.refs_1_, bf16[256,640]{1,0:T(8,128)(2,1)} %collective-permute-done.10.refs_2_, ...), custom_call_target="tpu_custom_call" | custom-call | flops 3400000000 | bytes 17825792 | tf_op jit(solution)/shard_map/pallas_call | solution.py:200
  110.0 0.7 broadcast_in_dim.11
  110.7 1.4 %collective-permute-start.12 = (f32[320,2560]{1,0:T(8,128)}, f32[320,2560]{1,0:T(8,128)}, u32[]{:S(2)}, u32[]{:S(2)}) collective-permute-start(f32[320,2560]{1,0:T(8,128)} %get-tuple-element.111), channel_id=1, source_target_pairs={{0,1},{1,0},{2,3},{3,2},{4,5},{5,4},{6,7},{7,6},{8,9},{9,8},{10,11... | collective-permute-start | bytes 9830408 | tf_op jit(solution)/shard_map/ppermute | solution.py:330
  112.1 1.5 %collective-permute-start.13 = (bf16[256,640]{1,0:T(8,128)(2,1)}, bf16[256,640]{1,0:T(8,128)(2,1)}, u32[]{:S(2)}, u32[]{:S(2)}) collective-permute-start(bf16[256,640]{1,0:T(8,128)(2,1)} %shard_map.82), channel_id=1, source_target_pairs={{0,4},{1,5},{2,6},{3,7},{4,0},{5,1},{6,2},{7,3},{8,12},{9,13},{10,... | collective-permute-start | bytes 983048 | tf_op jit(solution)/shard_map/ppermute | solution.py:334
  113.6 5.3 %all-to-all-start.5 = ((f32[16,3,8,128]{3,2,1,0:T(8,128)}), f32[16,3,8,128]{3,2,1,0:T(8,128)S(1)}, u32[]{:S(2)}, u32[]{:S(2)}) async-start(f32[16,3,8,128]{3,2,1,0:T(8,128)} %broadcast_in_dim.11), calls=%async_computation.5 | async-start | bytes 393216 | tf_op jit(solution)/shard_map/all_to_all | solution.py:326
  118.9 3.4 %add.47.grown_ref = f32[320,2560]{1,0:T(8,128)S(1)} add(f32[320,2560]{1,0:T(8,128)} %get-tuple-element.110, f32[320,2560]{1,0:T(8,128)} %collective-permute-done.12) | non-fusion elementwise | flops 819200 | bytes 9830400 | tf_op jit(solution)/shard_map/add | solution.py:391
  122.3 1.0 collective-permute-done.13.g3
  123.3 2.4 %shard_map.84 = bf16[256,2560]{1,0:T(8,128)(2,1)} custom-call(s32[6]{0:T(128)} %copy-done.5, bf16[256,640]{1,0:T(8,128)(2,1)} %copy-done.1, bf16[256,640]{1,0:T(8,128)(2,1)} %collective-permute-done.7.g1, bf16[256,640]{1,0:T(8,128)(2,1)} %collective-permute-done.8.g2, bf16[256,640]{1,0:T(8,128)(2,1)} %collective-permute-done.13.g3), custom_call_target="tpu_custom_call" | custom-call | bytes 3145728 | tf_op jit(solution)/shard_map/pallas_call | solution.py:219
  125.9 1.8 %collective-permute-start.14 = (f32[16,3,8,128]{3,2,1,0:T(8,128)S(1)}, f32[16,3,8,128]{3,2,1,0:T(8,128)S(1)}, u32[]{:S(2)}, u32[]{:S(2)}) collective-permute-start(f32[16,3,8,128]{3,2,1,0:T(8,128)S(1)} %all-to-all-done.5.mine_ref), channel_id=1, source_target_pairs={{0,1},{1,0},{2,3},{3,2},{4,5},{5,4},{6,7},{7,6},{8,9},{9,8},{10,11... | collective-permute-start | bytes 589832 | tf_op jit(solution)/shard_map/ppermute | solution.py:330
  127.7 1.1 collective-permute-done.14.other_ref
  128.8 3.8 %shard_map.85 = (f32[320,2560]{1,0:T(8,128)}, f32[32,2560]{1,0:T(8,128)}) custom-call(s32[6]{0:T(128)S(1)} %copy-done.7, f32[16,3,8,128]{3,2,1,0:T(8,128)S(1)} %all-to-all-done.5.mine_ref, f32[16,3,8,128]{3,2,1,0:T(8,128)S(1)} %collective-permute-done.14.other_ref, f32[32,32]{1,0:T(8,128)S(1)} %copy-done.8, f32[32,384]{1,0:T(8,128)S(1)} %copy-done.4, ...), custom_call_target="tpu_custom_call" | custom-call | flops 300000000 | bytes 8388608 | tf_op jit(solution)/shard_map/pallas_call | solution.py:312
  (42 shorter events, 1.6 us)
Async XLA Ops:
  0.6 23.3 %collective-permute-start.1 = (bf16[320,2560]{1,0:T(8,128)(2,1)}, bf16[320,2560]{1,0:T(8,128)(2,1)}, u32[]{:S(2)}, u32[]{:S(2)}) collective-permute-start(bf16[320,2560]{1,0:T(8,128)(2,1)} %param.7), channel_id=1, source_target_pairs={{0,1},{1,0},{2,3},{3,2},{4,5},{5,4},{6,7},{7,6},{8,9},{9,8},{10,11... | collective-permute-start | bytes 4915208 | tf_op jit(solution)/shard_map/ppermute | solution.py:330
  4.0 36.0 %collective-permute-start.3 = (bf16[256,2560]{1,0:T(8,128)(2,1)}, bf16[256,2560]{1,0:T(8,128)(2,1)}, u32[]{:S(2)}, u32[]{:S(2)}) collective-permute-start(bf16[256,2560]{1,0:T(8,128)(2,1)} %refs_4_.1), channel_id=1, source_target_pairs={{2,0},{7,1},{4,2},{1,3},{6,4},{3,5},{0,6},{5,7},{10,8},{15,9},{12,... | collective-permute-start | bytes 3932168 | tf_op jit(solution)/shard_map/ppermute | solution.py:334
  4.0 36.0 %collective-permute-start.2 = (bf16[256,2560]{1,0:T(8,128)(2,1)}, bf16[256,2560]{1,0:T(8,128)(2,1)}, u32[]{:S(2)}, u32[]{:S(2)}) collective-permute-start(bf16[256,2560]{1,0:T(8,128)(2,1)} %refs_4_.1), channel_id=1, source_target_pairs={{0,2},{1,7},{2,4},{3,1},{4,6},{5,3},{6,0},{7,5},{8,10},{9,15},{10,... | collective-permute-start | bytes 3932168 | tf_op jit(solution)/shard_map/ppermute | solution.py:334
  6.6 16.2 %copy-start.9 = (bf16[256,2560]{1,0:T(8,128)(2,1)S(1)}, bf16[256,2560]{1,0:T(8,128)(2,1)}, u32[]{:S(2)}) copy-start(bf16[256,2560]{1,0:T(8,128)(2,1)} %x_any.3) | copy-start | bytes 3932164
  13.0 1.7 %collective-permute-start = (f32[8,6,8,128]{3,2,1,0:T(8,128)}, f32[8,6,8,128]{3,2,1,0:T(8,128)S(1)}, u32[]{:S(2)}, u32[]{:S(2)}) collective-permute-start(f32[8,6,8,128]{3,2,1,0:T(8,128)} %get-tuple-element.65), channel_id=1, source_target_pairs={{0,1},{1,0},{2,3},{3,2},{4,5},{5,4},{6,7},{7,6},{8,9},{9,8},{10,11... | collective-permute-start | bytes 589832 | tf_op jit(solution)/shard_map/ppermute | solution.py:330
  13.2 44.2 %copy-start.5 = (s32[6]{0:T(128)}, s32[6]{0:T(128)S(1)}, u32[]{:S(2)}) copy-start(s32[6]{0:T(128)S(1)} %stack.27.place) | copy-start | bytes 76
  16.3 16.0 %all-to-all-start = ((f32[8,6,8,128]{3,2,1,0:T(8,128)}), f32[8,6,8,128]{3,2,1,0:T(8,128)S(1)}, u32[]{:S(2)}, u32[]{:S(2)}) async-start(f32[8,6,8,128]{3,2,1,0:T(8,128)} %add.41), calls=%async_computation | async-start | bytes 393216 | tf_op jit(solution)/shard_map/all_to_all | solution.py:326
  23.9 3.4 %copy-start = (bf16[256,2560]{1,0:T(8,128)(2,1)S(1)}, bf16[256,2560]{1,0:T(8,128)(2,1)}, u32[]{:S(2)}) copy-start(bf16[256,2560]{1,0:T(8,128)(2,1)} %refs_4_.1) | copy-start | bytes 3932164
  29.1 0.7 copy-start.1
  33.1 14.9 %all-to-all-start.1 = ((f32[16,6,8,128]{3,2,1,0:T(8,128)}), f32[16,6,8,128]{3,2,1,0:T(8,128)}, u32[]{:S(2)}, u32[]{:S(2)}) async-start(f32[16,6,8,128]{3,2,1,0:T(8,128)} %broadcast_in_dim.8), calls=%async_computation.1 | async-start | bytes 786432 | tf_op jit(solution)/shard_map/all_to_all | solution.py:326
  49.7 40.9 %collective-permute-start.6 = (bf16[256,2560]{1,0:T(8,128)(2,1)}, bf16[256,2560]{1,0:T(8,128)(2,1)}, u32[]{:S(2)}, u32[]{:S(2)}) collective-permute-start(bf16[256,2560]{1,0:T(8,128)(2,1)} %collective-permute-done.2.c_ref.refs_5_), channel_id=1, source_target_pairs={{0,2},{1,7},{2,4},{3,1},{4,6},{5,3},{6,0},{7,5},{8,10},{9,15},{10,... | collective-permute-start | bytes 3932168 | tf_op jit(solution)/shard_map/ppermute | solution.py:334
  50.4 13.2 %all-to-all-start.2 = ((f32[8,6,8,128]{3,2,1,0:T(8,128)}), f32[8,6,8,128]{3,2,1,0:T(8,128)S(1)}, u32[]{:S(2)}, u32[]{:S(2)}) async-start(f32[8,6,8,128]{3,2,1,0:T(8,128)} %broadcast_in_dim.9), calls=%async_computation.2 | async-start | bytes 393216 | tf_op jit(solution)/shard_map/all_to_all | solution.py:326
  57.4 0.7 copy-start.3
  60.7 0.7 copy-start.2
  61.4 30.5 %copy-start.6 = (s32[6]{0:T(128)S(1)}, s32[6]{0:T(128)}, u32[]{:S(2)}) copy-start(s32[6]{0:T(128)} %copy-done.5) | copy-start | bytes 76
  63.6 4.5 %copy-start.10 = (f32[8,6,8,128]{3,2,1,0:T(8,128)}, f32[8,6,8,128]{3,2,1,0:T(8,128)S(1)}, u32[]{:S(2)}) copy-start(f32[8,6,8,128]{3,2,1,0:T(8,128)S(1)} %all-to-all-done.2.mine_ref) | copy-start | bytes 589828
  63.6 4.5 %collective-permute-start.4 = (f32[8,6,8,128]{3,2,1,0:T(8,128)S(1)}, f32[8,6,8,128]{3,2,1,0:T(8,128)S(1)}, u32[]{:S(2)}, u32[]{:S(2)}) collective-permute-start(f32[8,6,8,128]{3,2,1,0:T(8,128)S(1)} %all-to-all-done.2.mine_ref), channel_id=1, source_target_pairs={{0,1},{1,0},{2,3},{3,2},{4,5},{5,4},{6,7},{7,6},{8,9},{9,8},{10,11... | collective-permute-start | bytes 589832 | tf_op jit(solution)/shard_map/ppermute | solution.py:330
  68.1 0.7 copy-start.11
  74.8 4.3 %collective-permute-start.5 = (f32[16,3,8,128]{3,2,1,0:T(8,128)}, f32[16,3,8,128]{3,2,1,0:T(8,128)S(1)}, u32[]{:S(2)}, u32[]{:S(2)}) collective-permute-start(f32[16,3,8,128]{3,2,1,0:T(8,128)} %get-tuple-element.81), channel_id=1, source_target_pairs={{0,1},{1,0},{2,3},{3,2},{4,5},{5,4},{6,7},{7,6},{8,9},{9,8},{10,11... | collective-permute-start | bytes 589832 | tf_op jit(solution)/shard_map/ppermute | solution.py:330
  75.3 25.4 %collective-permute-start.9 = (bf16[256,640]{1,0:T(8,128)(2,1)}, bf16[256,640]{1,0:T(8,128)(2,1)}, u32[]{:S(2)}, u32[]{:S(2)}) collective-permute-start(bf16[256,640]{1,0:T(8,128)(2,1)} %get-tuple-element.101), channel_id=1, source_target_pairs={{0,2},{1,7},{2,4},{3,1},{4,6},{5,3},{6,0},{7,5},{8,10},{9,15},{10,... | collective-permute-start | bytes 983048 | tf_op jit(solution)/shard_map/ppermute | solution.py:334
  77.9 22.8 %collective-permute-start.10 = (bf16[256,640]{1,0:T(8,128)(2,1)}, bf16[256,640]{1,0:T(8,128)(2,1)}, u32[]{:S(2)}, u32[]{:S(2)}) collective-permute-start(bf16[256,640]{1,0:T(8,128)(2,1)} %get-tuple-element.102), channel_id=1, source_target_pairs={{2,0},{7,1},{4,2},{1,3},{6,4},{3,5},{0,6},{5,7},{10,8},{15,9},{12,... | collective-permute-start | bytes 983048 | tf_op jit(solution)/shard_map/ppermute | solution.py:334
  77.9 22.8 %collective-permute-start.11 = (bf16[256,640]{1,0:T(8,128)(2,1)}, bf16[256,640]{1,0:T(8,128)(2,1)}, u32[]{:S(2)}, u32[]{:S(2)}) collective-permute-start(bf16[256,640]{1,0:T(8,128)(2,1)} %get-tuple-element.103), channel_id=1, source_target_pairs={{0,4},{1,5},{2,6},{3,7},{4,0},{5,1},{6,2},{7,3},{8,12},{9,13},{10,... | collective-permute-start | bytes 983048 | tf_op jit(solution)/shard_map/ppermute | solution.py:334
  80.7 15.5 %all-to-all-start.3 = ((f32[16,3,8,128]{3,2,1,0:T(8,128)}), f32[16,3,8,128]{3,2,1,0:T(8,128)S(1)}, u32[]{:S(2)}, u32[]{:S(2)}) async-start(f32[16,3,8,128]{3,2,1,0:T(8,128)} %add.46), calls=%async_computation.3 | async-start | bytes 393216 | tf_op jit(solution)/shard_map/all_to_all | solution.py:326
  89.2 20.7 %collective-permute-start.7 = (bf16[256,640]{1,0:T(8,128)(2,1)}, bf16[256,640]{1,0:T(8,128)(2,1)}, u32[]{:S(2)}, u32[]{:S(2)}) collective-permute-start(bf16[256,640]{1,0:T(8,128)(2,1)} %copy-done.3), channel_id=1, source_target_pairs={{2,0},{7,1},{4,2},{1,3},{6,4},{3,5},{0,6},{5,7},{10,8},{15,9},{12,... | collective-permute-start | bytes 983048 | tf_op jit(solution)/shard_map/ppermute | solution.py:334
  90.6 19.3 %collective-permute-start.8 = (bf16[256,640]{1,0:T(8,128)(2,1)}, bf16[256,640]{1,0:T(8,128)(2,1)}, u32[]{:S(2)}, u32[]{:S(2)}) collective-permute-start(bf16[256,640]{1,0:T(8,128)(2,1)} %copy-done.2), channel_id=1, source_target_pairs={{0,2},{1,7},{2,4},{3,1},{4,6},{5,3},{6,0},{7,5},{8,10},{9,15},{10,... | collective-permute-start | bytes 983048 | tf_op jit(solution)/shard_map/ppermute | solution.py:334
  96.9 13.0 %all-to-all-start.4 = ((f32[8,3,8,128]{3,2,1,0:T(8,128)}), f32[8,3,8,128]{3,2,1,0:T(8,128)S(1)}, u32[]{:S(2)}, u32[]{:S(2)}) async-start(f32[8,3,8,128]{3,2,1,0:T(8,128)} %broadcast_in_dim.10), calls=%async_computation.4 | async-start | bytes 196608 | tf_op jit(solution)/shard_map/all_to_all | solution.py:326
  110.7 8.2 %collective-permute-start.12 = (f32[320,2560]{1,0:T(8,128)}, f32[320,2560]{1,0:T(8,128)}, u32[]{:S(2)}, u32[]{:S(2)}) collective-permute-start(f32[320,2560]{1,0:T(8,128)} %get-tuple-element.111), channel_id=1, source_target_pairs={{0,1},{1,0},{2,3},{3,2},{4,5},{5,4},{6,7},{7,6},{8,9},{9,8},{10,11... | collective-permute-start | bytes 9830408 | tf_op jit(solution)/shard_map/ppermute | solution.py:330
  112.1 11.2 %collective-permute-start.13 = (bf16[256,640]{1,0:T(8,128)(2,1)}, bf16[256,640]{1,0:T(8,128)(2,1)}, u32[]{:S(2)}, u32[]{:S(2)}) collective-permute-start(bf16[256,640]{1,0:T(8,128)(2,1)} %shard_map.82), channel_id=1, source_target_pairs={{0,4},{1,5},{2,6},{3,7},{4,0},{5,1},{6,2},{7,3},{8,12},{9,13},{10,... | collective-permute-start | bytes 983048 | tf_op jit(solution)/shard_map/ppermute | solution.py:334
  113.6 12.3 %all-to-all-start.5 = ((f32[16,3,8,128]{3,2,1,0:T(8,128)}), f32[16,3,8,128]{3,2,1,0:T(8,128)S(1)}, u32[]{:S(2)}, u32[]{:S(2)}) async-start(f32[16,3,8,128]{3,2,1,0:T(8,128)} %broadcast_in_dim.11), calls=%async_computation.5 | async-start | bytes 393216 | tf_op jit(solution)/shard_map/all_to_all | solution.py:326
  118.9 9.9 %copy-start.4 = (f32[32,384]{1,0:T(8,128)S(1)}, f32[32,384]{1,0:T(8,128)}, u32[]{:S(2)}) copy-start(f32[32,384]{1,0:T(8,128)} %get-tuple-element.121.ortho_ref) | copy-start | bytes 147460
  118.9 9.9 %copy-start.7 = (s32[6]{0:T(128)S(1)}, s32[6]{0:T(128)}, u32[]{:S(2)}) copy-start(s32[6]{0:T(128)} %copy-done.5) | copy-start | bytes 76
  118.9 9.9 %copy-start.8 = (f32[32,32]{1,0:T(8,128)S(1)}, f32[32,32]{1,0:T(8,128)}, u32[]{:S(2)}) copy-start(f32[32,32]{1,0:T(8,128)} %get-tuple-element.120.inverse_ref) | copy-start | bytes 12292
  125.9 2.9 %collective-permute-start.14 = (f32[16,3,8,128]{3,2,1,0:T(8,128)S(1)}, f32[16,3,8,128]{3,2,1,0:T(8,128)S(1)}, u32[]{:S(2)}, u32[]{:S(2)}) collective-permute-start(f32[16,3,8,128]{3,2,1,0:T(8,128)S(1)} %all-to-all-done.5.mine_ref), channel_id=1, source_target_pairs={{0,1},{1,0},{2,3},{3,2},{4,5},{5,4},{6,7},{7,6},{8,9},{9,8},{10,11... | collective-permute-start | bytes 589832 | tf_op jit(solution)/shard_map/ppermute | solution.py:330
